TPU v7x, 256 devices: a whole 4x4x8 slice. The times are simulated.
256 devices in a mesh: gs: 128 (over z, x, y), px: 2 (over core).
Axes of the slice: x: 4, y: 4, z: 8, core: 2. Of those that a mesh axis runs over, the one named last changes fastest.
Arguments:
- features: float32 [262144, 128], P('gs'), may hold values from -6 to 6
- gauss_params: float32 [6, 262144], P(None, 'gs'), as said below
- send_index: int32 [131072], P('gs'), may hold values from 0 to 2047, as said below
- tile_ids: int32 [1024], P('gs'), may hold values from 0 to 1023, as said below
- tile_lists: int32 [1024, 512], P('gs'), may hold values from -1 to 1023, as said below
- teacher: float32 [1024, 256, 512], P('gs', 'px'), may hold values from -6 to 6
- decoder_weight: float32 [128, 512], replicated, may hold values from -0.5 to 0.5
- decoder_bias: float32 [512], replicated, may hold values from -3 to 3
Outputs:
- grad_features: float32 [262144, 128], P('gs')
- grad_params: float32 [6, 262144], P(None, 'gs')
- grad_decoder: float32 [128, 512], replicated
- grad_bias: float32 [512], replicated
- loss: float32 [], replicated
Inputs may be any that keep to these rules, and one draw needn't show every extreme that they name: `send_index`: each holder's 1024 entries are distinct local Gaussian numbers; entry o * 8 + s is what that holder puts in slot s for tile owner o, so every holder sends exactly 8 Gaussians to every owner. `tile_ids`: A permutation of all tile numbers. `tile_lists`: each row holds distinct live pool entries followed only by -1; within one owner's 8 rows no pool entry appears twice, and one row of each owner is live in all 512 entries. `gauss_params`: rows 2 to 4 form a positive definite conic (a > 0, c > 0, a c > b^2); opacity lies in (0, 0.95].
All inputs are finite; a program needn't handle non-finite values.
Results may differ from a plain program's by a relative error of at most 0.0003.
Values sent between devices are 32-bit elements; how exact they have to be, the bound alone decides.
No kernel may reach another device: no remote copies, remote signals or barrier semaphores. Data moves between devices by JAX's collectives and lax.ppermute only.
A program may use at most 128 MiB of HBM per device.

v0:
```python
import jax
import jax.numpy as jnp
from jax import lax
from jax.sharding import PartitionSpec as P

HIGH = lax.Precision.HIGHEST


def pixel_grid(tile_ids, stripe, tile_cols):
    pixel_index = jnp.arange(128, dtype=jnp.int32)
    pixel_x = ((tile_ids % tile_cols * 16)[:, None] + pixel_index[None, :] % 16).astype(
        jnp.float32
    ) + 0.5
    pixel_y = (
        (tile_ids // tile_cols * 16)[:, None] + stripe * 8 + pixel_index[None, :] // 16
    ).astype(jnp.float32) + 0.5
    return (pixel_x, pixel_y)


def composite(pixel_x, pixel_y, feat_rows, prm_rows, live_mask):
    upper_ones = (
        lax.broadcasted_iota(jnp.int32, (128, 128), 0)
        < lax.broadcasted_iota(jnp.int32, (128, 128), 1)
    ).astype(jnp.float32)
    nblocks = feat_rows.shape[0] // 128
    feat_blocks = feat_rows.reshape(nblocks, 128, feat_rows.shape[1])
    prm_blocks = prm_rows.reshape(nblocks, 128, 6)
    live_blocks = live_mask.reshape(nblocks, 128)

    def advance(state_pair, pack):
        log_trans, blended = state_pair
        feat_block, prm_block, live_block = pack
        delta_x = pixel_x[:, None] - prm_block[None, :, 0]
        delta_y = pixel_y[:, None] - prm_block[None, :, 1]
        exponent = (
            -0.5
            * (
                prm_block[None, :, 2] * delta_x * delta_x
                + prm_block[None, :, 4] * delta_y * delta_y
            )
            - prm_block[None, :, 3] * delta_x * delta_y
        )
        alphas = prm_block[None, :, 5] * live_block[None, :] * jnp.exp(exponent)
        log_keep = jnp.log1p(-alphas)
        within = jnp.dot(log_keep, upper_ones, precision=HIGH)
        weights = jnp.exp(log_trans[:, None] + within) * alphas
        blended = blended + jnp.dot(weights, feat_block, precision=HIGH)
        return ((log_trans + jnp.sum(log_keep, axis=1), blended), None)

    start_state = (
        jnp.zeros((128,), jnp.float32),
        jnp.zeros((128, feat_rows.shape[1]), jnp.float32),
    )
    (log_trans, blended), unused = lax.scan(
        advance, start_state, (feat_blocks, prm_blocks, live_blocks)
    )
    return blended


def local_objective(
    pool_feat, pool_prm, decoder_weight, decoder_bias, tile_lists, pixel_x, pixel_y, teacher
):
    live_mask = (tile_lists >= 0).astype(jnp.float32)
    clamped = jnp.maximum(tile_lists, 0)

    def one_tile(entry_pack):
        tile_index, tile_live, row_x, row_y = entry_pack
        return composite(row_x, row_y, pool_feat[tile_index], pool_prm[tile_index], tile_live)

    rendered = lax.map(one_tile, (clamped, live_mask, pixel_x, pixel_y))
    flat_render = rendered.reshape(-1, rendered.shape[2])
    decoded = jnp.dot(flat_render, decoder_weight, precision=HIGH) + decoder_bias
    resid = decoded - teacher.reshape(-1, teacher.shape[2])
    squares = jnp.sum(resid * resid)
    return (0.5 * squares, squares)


def per_device(
    features, gauss_params, send_index, tile_ids, tile_lists, teacher, decoder_weight, decoder_bias
):
    holders = lax.axis_size("gs")
    stripe = lax.axis_index("px")
    pool_size = send_index.shape[0]
    slot_count = pool_size // holders
    feat_width = features.shape[1]
    out_rows = features[send_index].reshape(holders, slot_count, feat_width)
    out_prm = gauss_params.T[send_index].reshape(holders, slot_count, 6)
    got_rows, got_prm = (
        lax.all_to_all(out_rows, "gs", split_axis=0, concat_axis=0, tiled=True),
        lax.all_to_all(out_prm, "gs", split_axis=0, concat_axis=0, tiled=True),
    )
    pool_feat = got_rows.reshape(pool_size, feat_width)
    pool_prm = got_prm.reshape(pool_size, 6)
    tile_cols = holders * tile_ids.shape[0] // 8
    pixel_x, pixel_y = pixel_grid(tile_ids, stripe, tile_cols)

    def objective(feat_in, prm_in, weight_in, bias_in):
        return local_objective(
            feat_in, prm_in, weight_in, bias_in, tile_lists, pixel_x, pixel_y, teacher
        )

    half_sq, pullback, squares = jax.vjp(
        objective, pool_feat, pool_prm, decoder_weight, decoder_bias, has_aux=True
    )
    grad_pool, grad_pprm, grad_weight, grad_bias = pullback(jnp.ones((), jnp.float32))
    grad_rows = grad_pool.reshape(holders, slot_count, feat_width)
    grad_prm3 = grad_pprm.reshape(holders, slot_count, 6)
    summed_rows, summed_prm = lax.psum((grad_rows, grad_prm3), "px")
    back_rows, back_prm = (
        lax.all_to_all(summed_rows, "gs", split_axis=0, concat_axis=0, tiled=True),
        lax.all_to_all(summed_prm, "gs", split_axis=0, concat_axis=0, tiled=True),
    )
    grad_features = (
        jnp.zeros(features.shape, jnp.float32)
        .at[send_index]
        .add(back_rows.reshape(pool_size, feat_width))
    )
    grad_params = (
        jnp.zeros((features.shape[0], 6), jnp.float32)
        .at[send_index]
        .add(back_prm.reshape(pool_size, 6))
        .T
    )
    totals = lax.psum((grad_weight, grad_bias, squares), ("gs", "px"))
    pixels = holders * tile_ids.shape[0] * 256
    return (
        grad_features,
        grad_params,
        totals[0] / pixels,
        totals[1] / pixels,
        totals[2] / (pixels * decoder_weight.shape[1]),
    )


def solution(mesh):
    return jax.shard_map(
        per_device,
        mesh=mesh,
        in_specs=(
            P("gs", None),
            P(None, "gs"),
            P("gs"),
            P("gs"),
            P("gs", None),
            P("gs", "px", None),
            P(),
            P(),
        ),
        out_specs=(P("gs", None), P(None, "gs"), P(), P(), P()),
        check_vma=False,
    )
```

profile of v0, /device:TPU:1, one launch (start us, length us, event | category | flops | bytes accessed | tf_op | source)
XLA Modules:
  0.0 986.6 jit_solution(6711503784718975346)
XLA Ops:
  14.6 16.3 %all-to-all-start.1 = ((f32[128,8,6]{2,1,0:T(8,128)}), f32[128,8,6]{2,1,0:T(8,128)S(1)}, u32[]{:S(2)}, u32[]{:S(2)}) async-start(f32[128,8,6]{2,1,0:T(8,128)} %bitcast.3), calls=%async_computation.1 | async-start | bytes 1048576 | tf_op jit(solution)/shard_map/all_to_all | solution.py:90
  35.0 14.2 %all-to-all-done.1 = f32[128,8,6]{2,1,0:T(8,128)S(1)} async-done(((f32[128,8,6]{2,1,0:T(8,128)}), f32[128,8,6]{2,1,0:T(8,128)S(1)}, u32[]{:S(2)}, u32[]{:S(2)}) %all-to-all-start.1) | async-done | bytes 24608 | tf_op jit(solution)/shard_map/all_to_all | solution.py:90
  57.0 16.6 %all-to-all-done = f32[128,8,128]{2,1,0:T(8,128)S(1)} async-done(((f32[128,8,128]{2,1,0:T(8,128)}), f32[128,8,128]{2,1,0:T(8,128)S(1)}, u32[]{:S(2)}, u32[]{:S(2)}) %all-to-all-start) | async-done | bytes 524320 | tf_op jit(solution)/shard_map/all_to_all | solution.py:89
  73.6 267.8 %while.173 = (s32[]{:T(128)}, f32[8,128,128]{2,1,0:T(8,128)}, s32[8,512,1]{1,2,0:T(1,128)}, f32[8,4,128,128]{3,2,1,0:T(8,128)}, f32[8,4,1,128]{3,1,2,0:T(4,128)}...) while((s32[]{:T(128)}, f32[8,128,128]{2,1,0:T(8,128)}, ...), condition=%wide.region_4.5_spmd.clone, body=%wide.region_0.4_spmd.clone.sunk | while | flops 51532160 | bytes 10269777 | solution.py:70
  76.6 20.3 %while.176 = (s32[]{:T(128)}, f32[128]{0:T(128)S(1)}, f32[128,128]{1,0:T(8,128)}, f32[4,128,128]{2,1,0:T(8,128)S(1)}, f32[4,1,128]{2,1,0:T(1,128)}, /*index=5*/f...) while((s32[]{:T(128)}, f32[128]{0:T(128)S(1)}, ...), condition=%wide.region_3.3_spmd.clone, body=%wide.region_1.2_spmd.clone.sunk | while | flops 51495296 | bytes 1092352 | solution.py:54
  110.0 20.3 %while.176 = (s32[]{:T(128)}, f32[128]{0:T(128)S(1)}, f32[128,128]{1,0:T(8,128)}, f32[4,128,128]{2,1,0:T(8,128)S(1)}, f32[4,1,128]{2,1,0:T(1,128)}, /*index=5*/f...) while((s32[]{:T(128)}, f32[128]{0:T(128)S(1)}, ...), condition=%wide.region_3.3_spmd.clone, body=%wide.region_1.2_spmd.clone.sunk | while | flops 51495296 | bytes 1092352 | solution.py:54
  143.5 20.3 %while.176 = (s32[]{:T(128)}, f32[128]{0:T(128)S(1)}, f32[128,128]{1,0:T(8,128)}, f32[4,128,128]{2,1,0:T(8,128)S(1)}, f32[4,1,128]{2,1,0:T(1,128)}, /*index=5*/f...) while((s32[]{:T(128)}, f32[128]{0:T(128)S(1)}, ...), condition=%wide.region_3.3_spmd.clone, body=%wide.region_1.2_spmd.clone.sunk | while | flops 51495296 | bytes 1092352 | solution.py:54
  176.9 20.3 %while.176 = (s32[]{:T(128)}, f32[128]{0:T(128)S(1)}, f32[128,128]{1,0:T(8,128)}, f32[4,128,128]{2,1,0:T(8,128)S(1)}, f32[4,1,128]{2,1,0:T(1,128)}, /*index=5*/f...) while((s32[]{:T(128)}, f32[128]{0:T(128)S(1)}, ...), condition=%wide.region_3.3_spmd.clone, body=%wide.region_1.2_spmd.clone.sunk | while | flops 51495296 | bytes 1092352 | solution.py:54
  210.5 20.3 %while.176 = (s32[]{:T(128)}, f32[128]{0:T(128)S(1)}, f32[128,128]{1,0:T(8,128)}, f32[4,128,128]{2,1,0:T(8,128)S(1)}, f32[4,1,128]{2,1,0:T(1,128)}, /*index=5*/f...) while((s32[]{:T(128)}, f32[128]{0:T(128)S(1)}, ...), condition=%wide.region_3.3_spmd.clone, body=%wide.region_1.2_spmd.clone.sunk | while | flops 51495296 | bytes 1092352 | solution.py:54
  244.0 20.3 %while.176 = (s32[]{:T(128)}, f32[128]{0:T(128)S(1)}, f32[128,128]{1,0:T(8,128)}, f32[4,128,128]{2,1,0:T(8,128)S(1)}, f32[4,1,128]{2,1,0:T(1,128)}, /*index=5*/f...) while((s32[]{:T(128)}, f32[128]{0:T(128)S(1)}, ...), condition=%wide.region_3.3_spmd.clone, body=%wide.region_1.2_spmd.clone.sunk | while | flops 51495296 | bytes 1092352 | solution.py:54
  277.5 20.3 %while.176 = (s32[]{:T(128)}, f32[128]{0:T(128)S(1)}, f32[128,128]{1,0:T(8,128)}, f32[4,128,128]{2,1,0:T(8,128)S(1)}, f32[4,1,128]{2,1,0:T(1,128)}, /*index=5*/f...) while((s32[]{:T(128)}, f32[128]{0:T(128)S(1)}, ...), condition=%wide.region_3.3_spmd.clone, body=%wide.region_1.2_spmd.clone.sunk | while | flops 51495296 | bytes 1092352 | solution.py:54
  311.0 20.3 %while.176 = (s32[]{:T(128)}, f32[128]{0:T(128)S(1)}, f32[128,128]{1,0:T(8,128)}, f32[4,128,128]{2,1,0:T(8,128)S(1)}, f32[4,1,128]{2,1,0:T(1,128)}, /*index=5*/f...) while((s32[]{:T(128)}, f32[128]{0:T(128)S(1)}, ...), condition=%wide.region_3.3_spmd.clone, body=%wide.region_1.2_spmd.clone.sunk | while | flops 51495296 | bytes 1092352 | solution.py:54
  349.0 319.4 %while.175 = (s32[]{:T(128)}, f32[1024,128]{1,0:T(8,128)S(1)}, f32[1024,6]{1,0:T(8,128)S(1)}, s32[8,512,1]{1,2,0:T(1,128)}, f32[8,4,128,128]{3,2,1,0:T(8,128)}, ...) while((s32[]{:T(128)}, f32[1024,128]{1,0:T(8,128)S(1)}, ...), condition=%wide.region_17.18_spmd.clone, body=%wide.region_5.17_spmd.clone.sunk | while | flops 76208640 | bytes 9697576 | solution.py:70
  362.0 17.7 %while.177 = (s32[]{:T(128)}, f32[128]{0:T(128)S(1)}, f32[4,128,128]{2,1,0:T(8,128)}, f32[4,128,6]{1,2,0:T(8,128)S(1)}, f32[4,128,128]{2,1,0:T(8,128)S(1)}, /*in...) while((s32[]{:T(128)}, f32[128]{0:T(128)S(1)}, ...), condition=%wide.region_14.14_spmd.clone, body=%wide.region_6.13_spmd.clone.sunk | while | flops 76107264 | bytes 1533703 | solution.py:54
  402.1 17.7 %while.177 = (s32[]{:T(128)}, f32[128]{0:T(128)S(1)}, f32[4,128,128]{2,1,0:T(8,128)}, f32[4,128,6]{1,2,0:T(8,128)S(1)}, f32[4,128,128]{2,1,0:T(8,128)S(1)}, /*in...) while((s32[]{:T(128)}, f32[128]{0:T(128)S(1)}, ...), condition=%wide.region_14.14_spmd.clone, body=%wide.region_6.13_spmd.clone.sunk | while | flops 76107264 | bytes 1533703 | solution.py:54
  440.6 17.7 %while.177 = (s32[]{:T(128)}, f32[128]{0:T(128)S(1)}, f32[4,128,128]{2,1,0:T(8,128)}, f32[4,128,6]{1,2,0:T(8,128)S(1)}, f32[4,128,128]{2,1,0:T(8,128)S(1)}, /*in...) while((s32[]{:T(128)}, f32[128]{0:T(128)S(1)}, ...), condition=%wide.region_14.14_spmd.clone, body=%wide.region_6.13_spmd.clone.sunk | while | flops 76107264 | bytes 1533703 | solution.py:54
  480.7 17.7 %while.177 = (s32[]{:T(128)}, f32[128]{0:T(128)S(1)}, f32[4,128,128]{2,1,0:T(8,128)}, f32[4,128,6]{1,2,0:T(8,128)S(1)}, f32[4,128,128]{2,1,0:T(8,128)S(1)}, /*in...) while((s32[]{:T(128)}, f32[128]{0:T(128)S(1)}, ...), condition=%wide.region_14.14_spmd.clone, body=%wide.region_6.13_spmd.clone.sunk | while | flops 76107264 | bytes 1533703 | solution.py:54
  520.9 17.7 %while.177 = (s32[]{:T(128)}, f32[128]{0:T(128)S(1)}, f32[4,128,128]{2,1,0:T(8,128)}, f32[4,128,6]{1,2,0:T(8,128)S(1)}, f32[4,128,128]{2,1,0:T(8,128)S(1)}, /*in...) while((s32[]{:T(128)}, f32[128]{0:T(128)S(1)}, ...), condition=%wide.region_14.14_spmd.clone, body=%wide.region_6.13_spmd.clone.sunk | while | flops 76107264 | bytes 1533703 | solution.py:54
  560.9 17.7 %while.177 = (s32[]{:T(128)}, f32[128]{0:T(128)S(1)}, f32[4,128,128]{2,1,0:T(8,128)}, f32[4,128,6]{1,2,0:T(8,128)S(1)}, f32[4,128,128]{2,1,0:T(8,128)S(1)}, /*in...) while((s32[]{:T(128)}, f32[128]{0:T(128)S(1)}, ...), condition=%wide.region_14.14_spmd.clone, body=%wide.region_6.13_spmd.clone.sunk | while | flops 76107264 | bytes 1533703 | solution.py:54
  601.0 17.7 %while.177 = (s32[]{:T(128)}, f32[128]{0:T(128)S(1)}, f32[4,128,128]{2,1,0:T(8,128)}, f32[4,128,6]{1,2,0:T(8,128)S(1)}, f32[4,128,128]{2,1,0:T(8,128)S(1)}, /*in...) while((s32[]{:T(128)}, f32[128]{0:T(128)S(1)}, ...), condition=%wide.region_14.14_spmd.clone, body=%wide.region_6.13_spmd.clone.sunk | while | flops 76107264 | bytes 1533703 | solution.py:54
  641.0 17.7 %while.177 = (s32[]{:T(128)}, f32[128]{0:T(128)S(1)}, f32[4,128,128]{2,1,0:T(8,128)}, f32[4,128,6]{1,2,0:T(8,128)S(1)}, f32[4,128,128]{2,1,0:T(8,128)S(1)}, /*in...) while((s32[]{:T(128)}, f32[128]{0:T(128)S(1)}, ...), condition=%wide.region_14.14_spmd.clone, body=%wide.region_6.13_spmd.clone.sunk | while | flops 76107264 | bytes 1533703 | solution.py:54
  679.5 25.0 %all_to_all.20 = f32[128,8,6]{1,2,0:T(8,128)S(1)} all-to-all(f32[128,8,6]{1,2,0:T(8,128)S(1)} %copy.30), channel_id=1, replica_groups=mesh['gs'=128,'px'=2] {'gs'}, dimensions={0} | all-to-all | bytes 49152 | tf_op jit(solution)/shard_map/all_to_all | solution.py:111
  714.6 77.7 %all-reduce.6 = (f32[512]{0:T(512)S(1)}, f32[]{:T(128)}) all-reduce(f32[512]{0:T(512)S(1)} %get-tuple-element.1748, f32[]{:T(128)} %get-tuple-element.1747), channel_id=1, replica_groups=mesh['gs'=128,'px'=2] {'gs','px'}, use_global_device_ids=true, to_apply=%region_24.25 | all-reduce | flops 513 | bytes 4104 | tf_op jit(solution)/shard_map/psum | solution.py:124
  802.3 166.9 %all-reduce.12.cloned.1.call-done = f32[128,512]{1,0:T(8,128)} async-done(((f32[128,512]{1,0:T(8,128)}), f32[128,512]{1,0:T(8,128)}) %all-reduce.12.cloned.1.call-update) | async-done | bytes 262160 | tf_op jit(solution)/shard_map/psum | solution.py:124
  (1368 shorter events, 646.9 us)
Async XLA Ops:
  8.0 23.0 %copy-start = (f32[2048,128]{1,0:T(8,128)S(1)}, f32[2048,128]{1,0:T(8,128)}, u32[]{:S(2)}) copy-start(f32[2048,128]{1,0:T(8,128)} %param.16) | copy-start | bytes 3145732
  14.6 34.6 %all-to-all-start.1 = ((f32[128,8,6]{2,1,0:T(8,128)}), f32[128,8,6]{2,1,0:T(8,128)S(1)}, u32[]{:S(2)}, u32[]{:S(2)}) async-start(f32[128,8,6]{2,1,0:T(8,128)} %bitcast.3), calls=%async_computation.1 | async-start | bytes 1048576 | tf_op jit(solution)/shard_map/all_to_all | solution.py:90
  31.0 25.9 %copy-start.20 = (s32[8]{0:T(128)S(1)}, s32[8]{0:T(128)}, u32[]{:S(2)}) copy-start(s32[8]{0:T(128)} %param.19) | copy-start | bytes 100
  31.0 26.0 %copy-start.9 = (s32[8,512]{1,0:T(8,128)S(1)}, s32[8,512]{1,0:T(8,128)}, u32[]{:S(2)}) copy-start(s32[8,512]{1,0:T(8,128)} %param.20) | copy-start | bytes 49156
  49.3 24.3 %all-to-all-start = ((f32[128,8,128]{2,1,0:T(8,128)}), f32[128,8,128]{2,1,0:T(8,128)S(1)}, u32[]{:S(2)}, u32[]{:S(2)}) async-start(f32[128,8,128]{2,1,0:T(8,128)} %bitcast), calls=%async_computation | async-start | bytes 1048576 | tf_op jit(solution)/shard_map/all_to_all | solution.py:89
  56.4 648.0 %all-reduce.10.cloned.1.call-start = ((), (), s32[]{:S(2)}) async-start(), calls=%async_computation.4 | async-start | bytes 1048576 | tf_op jit(solution)/shard_map/psum | solution.py:108
  134.2 6.3 copy-start.15
  134.2 6.3 copy-start.17
  134.2 6.3 copy-start.19
  199.2 6.3 copy-start.13
  201.1 6.3 copy-start.15
  201.2 6.3 copy-start.17
  201.2 6.3 copy-start.19
  234.7 6.3 copy-start.17
  234.7 6.3 copy-start.19
  266.3 6.3 copy-start.13
  299.7 6.3 copy-start.13
  301.6 6.3 copy-start.15
  301.6 6.3 copy-start.17
  301.6 6.3 copy-start.19
  333.3 6.3 copy-start.13
  670.3 40.5 %copy-start.6 = (f32[8,128,128]{2,1,0:T(8,128)S(1)}, f32[8,128,128]{2,1,0:T(8,128)}, u32[]{:S(2)}) copy-start(f32[8,128,128]{2,1,0:T(8,128)} %get-tuple-element.1324) | copy-start | bytes 1572868
  704.5 266.4 %all-to-all-start.2 = ((f32[128,8,128]{2,1,0:T(8,128)}), f32[128,8,128]{2,1,0:T(8,128)S(1)}, u32[]{:S(2)}, u32[]{:S(2)}) async-start(f32[128,8,128]{2,1,0:T(8,128)} %all-reduce.10.cloned.1.call-done), calls=%async_computation.2 | async-start | bytes 1048576 | tf_op jit(solution)/shard_map/all_to_all | solution.py:110
  710.7 258.4 %all-reduce.12.cloned.1.call-start = ((), (), s32[]{:S(2)}) async-start(), calls=%async_computation.5 | async-start | bytes 524288 | tf_op jit(solution)/shard_map/psum | solution.py:124
  (100 other events, 452.1 us)
Sparse Core Ops, SparseCore 0:
  669.3 26.5 all-reduce.9
Sparse Core Ops, SparseCore 1:
  718.1 251.0 all-reduce.11
where the time goes:
time: 997 us; the launch traced here: 987 us
  matrix products  227 us (23%)
  local copies, waits for them, and re-layouts  224 us (22%)
  waiting for transfers between devices  198 us (20%)
  other arithmetic  173 us (17%)
  blocking collectives  112 us (11%)
  starting transfers between devices  30 us (3%)
  between operations  17.6 us (2%)
    psum x1, waiting for transfers between devices, per_device(): totals = lax.psum((grad_weight, grad_bias, squares), ('gs', 'px'))  167 us
    dot_general x96, matrix products, advance(): blended = blended + jnp.dot(weights, feat_block, precision=HIGH)  122 us
    dot_general x64, matrix products, advance(): within = jnp.dot(log_keep, upper_ones, precision=HIGH)  93.4 us
    squeeze x56, local copies, waits for them, and re-layouts, local_objective(): rendered = lax.map(one_tile, (clamped, live_mask, pixel_x, pixel_y))  82.3 us
    psum x1, blocking collectives, per_device(): totals = lax.psum((grad_weight, grad_bias, squares), ('gs', 'px'))  77.7 us
    dynamic_update_slice x80, local copies, waits for them, and re-layouts, local_objective(): rendered = lax.map(one_tile, (clamped, live_mask, pixel_x, pixel_y))  75.8 us
    reduce_sum x32, other arithmetic, advance(): prm_block[None, :, 3] * delta_x * delta_y  33.4 us
    scatter-add x8, other arithmetic, one_tile(): pool_feat[tile_index]  33.2 us
  transfers between devices with their start and end apart: 5, of which 3 were waited for; matrix products, arithmetic and copies ran while one was open for 2% of the time, Pallas kernels for 0%

commit v1 on v0

v1 whole, which is shorter than its diff:
```python
import functools

import jax
import jax.numpy as jnp
from jax import lax
from jax.experimental import pallas as pl
from jax.experimental.pallas import tpu as pltpu
from jax.sharding import PartitionSpec as P

F32 = jnp.float32
BF16 = jnp.bfloat16
L = 128
SWAP = [(0, 1), (1, 0)]
FWD = 5
RET = 7
GAT = 3
VMEM = pl.BlockSpec(memory_space=pltpu.VMEM)
SMEM = pl.BlockSpec(memory_space=pltpu.SMEM)
PARAMS = pltpu.CompilerParams(vmem_limit_bytes=48 * 1024 * 1024)


def nn(lhs, rhs):
    return lax.dot_general(lhs, rhs, (((1,), (0,)), ((), ())), preferred_element_type=F32)


def nt(lhs, rhs):
    return lax.dot_general(lhs, rhs, (((1,), (1,)), ((), ())), preferred_element_type=F32)


def split2(value):
    high = value.astype(BF16)
    return high, (value - high.astype(F32)).astype(BF16)


def split3(value):
    high = value.astype(BF16)
    rest = value - high.astype(F32)
    mid = rest.astype(BF16)
    return high, mid, (rest - mid.astype(F32)).astype(BF16)


def ones_where(mask):
    return jnp.where(mask, 1.0, 0.0).astype(F32)


def column_of(rows):
    pad = jnp.zeros((L - rows.shape[0], L), F32)
    return jnp.concatenate([rows, pad], axis=0).T


def pack_kernel(par_ref, idx_ref, feat_ref, prm_ref, out_ref):
    gauss = feat_ref.shape[0]
    first = par_ref[0] == 0
    rows = jnp.where(first, idx_ref[0:4, :], idx_ref[4:8, :])
    cols = column_of(rows.astype(F32))
    high, mid = split2(feat_ref[...])
    table = jnp.concatenate([high, mid], axis=1)
    lane = lax.broadcasted_iota(jnp.int32, (L, gauss), 1).astype(F32)
    groups = gauss // L
    pieces = [prm_ref[:, g * L : (g + 1) * L] for g in range(groups)]
    pad = jnp.zeros((2, L), F32)
    stacked = jnp.concatenate([x for piece in pieces for x in (piece, pad)], axis=0)
    stack3 = jnp.concatenate(split3(stacked), axis=0)
    low_iota = lax.broadcasted_iota(jnp.int32, (L, L), 0)
    packed = []
    for c in range(4):
        onehot = ones_where(cols[:, c : c + 1] == lane).astype(BF16)
        got = nn(onehot, table)
        out_ref[pl.ds(c, L, stride=FWD), :] = got[:, :L] + got[:, L:]
        row = rows[c : c + 1, :]
        low = ones_where((row & (L - 1)) == low_iota).astype(BF16)
        part = nn(stack3, low)
        span = groups * 8
        part = part[:span] + part[span : 2 * span] + part[2 * span :]
        total = jnp.zeros((8, L), F32)
        for g in range(groups):
            total = total + jnp.where((row >> 7) == g, part[g * 8 : g * 8 + 8], 0.0)
        packed.append(total)
    out_ref[pl.ds(4, L, stride=FWD), :] = column_of(jnp.concatenate(packed, axis=0))


def key_kernel(par_ref, lists_ref, row_ref, col_ref):
    shift = par_ref[0] * 4
    tiles, length = lists_ref.shape
    slot_iota = lax.broadcasted_iota(jnp.int32, (8, length), 0)
    holder_iota = lax.broadcasted_iota(jnp.int32, (L, length), 0)
    place = lax.broadcasted_iota(jnp.int32, (8, length), 1)
    place_high = (place >> 4).astype(F32)
    place_low = (place & 15).astype(F32)
    total = jnp.zeros((32, L), F32)
    for t in range(tiles):
        entry = lists_ref[t : t + 1, :]
        holder = ones_where((entry >> 3) == holder_iota).astype(BF16)
        slot = ones_where(((entry + shift) & 7) == slot_iota)
        left = jnp.concatenate(
            [slot * (t + 1.0), slot * place_high, slot * place_low, jnp.zeros((8, length), F32)],
            axis=0,
        ).astype(BF16)
        total = total + nt(left, holder)
    tile = total[0:8]
    key = jnp.where(tile > 0.5, (tile - 1.0) * length + total[8:16] * 16.0 + total[16:24], -1.0)
    row_ref[...] = key
    col_ref[...] = column_of(key)


def main_kernel(
    length,
    par_ref,
    own_ref,
    peer_ref,
    keyrow_ref,
    keycol_ref,
    teacher_hbm,
    weight_ref,
    bias_ref,
    keep_ref,
    give_ref,
    teacher_ref,
    teacher_sem,
    mask_ref,
    prm_ref,
    feat_ref,
    feat2_ref,
    ex_ref,
    alpha_ref,
    trans_ref,
    lk_ref,
    wm_hi,
    wm_lo,
    rt_ref,
    resid_hi,
    resid_lo,
    drt_ref,
    dw_ref,
):
    stripe = par_ref[0]
    fetch = pltpu.make_async_copy(teacher_hbm, teacher_ref, teacher_sem)
    fetch.start()
    tiles = 8
    keyrow = keyrow_ref[...]
    live_all = keyrow >= 0.0
    tile_all = jnp.floor(keyrow * (1.0 / length))
    base_all = jnp.where(live_all, tile_all * length, 1.0e9)
    ox_all = jnp.zeros((8, L), F32)
    oy_all = jnp.zeros((8, L), F32)
    for t in range(tiles):
        ident = par_ref[1 + t]
        here = tile_all == float(t)
        ox_all = jnp.where(here, ((ident & 127) * 16).astype(F32) + 0.5, ox_all)
        oy_all = jnp.where(here, ((ident >> 7) * 16 + stripe * 8).astype(F32) + 0.5, oy_all)
    live_all = ones_where(live_all)

    for side, ref in ((0, own_ref), (1, peer_ref)):
        for c in range(4):
            at = (side * 4 + c) * L
            high, low = split2(ref[pl.ds(c, L, stride=FWD), :])
            feat_ref[at : at + L, 0:L] = high
            feat_ref[at : at + L, L : 2 * L] = low
            feat2_ref[at : at + L, 0:L] = high
            feat2_ref[at : at + L, L : 2 * L] = high
        prm_ref[side * 32 : side * 32 + 32, :] = ref[pl.ds(4, L, stride=FWD), :].T[0:32]

    for a in range(8):
        front = jnp.broadcast_to(keycol_ref[:, a : a + 1], (L, L))
        for b in range(8):
            hit = (front < keyrow[b : b + 1, :]) & (front >= base_all[b : b + 1, :])
            mask_ref[a * L : a * L + L, b * L : b * L + L] = ones_where(hit).astype(BF16)

    kx = lax.broadcasted_iota(jnp.int32, (16, L), 0).astype(F32)
    ky = lax.broadcasted_iota(jnp.int32, (8, L), 0).astype(F32)

    def geometry(b):
        prm = prm_ref[b * 8 : b * 8 + 8, :]
        dx = (kx + ox_all[b : b + 1, :]) - prm[0:1]
        dy = (ky + oy_all[b : b + 1, :]) - prm[1:2]
        return prm, dx, dy

    for b in range(8):
        prm, dx, dy = geometry(b)
        live = live_all[b : b + 1, :]
        ax = prm[2:3] * dx * dx
        cy = prm[4:5] * dy * dy
        bx = prm[3:4] * dx
        cols = slice(b * L, b * L + L)
        for j in range(8):
            power = -0.5 * (ax + cy[j : j + 1]) - bx * dy[j : j + 1]
            ex = live * jnp.exp(power)
            alpha = prm[5:6] * ex
            high, low = split2(jnp.log1p(-alpha))
            spot = slice(j * 16, j * 16 + 16)
            ex_ref[spot, cols] = ex
            alpha_ref[spot, cols] = alpha
            lk_ref[spot, cols] = high
            lk_ref[L + j * 16 : L + j * 16 + 16, cols] = low

    for b in range(8):
        cols = slice(b * L, b * L + L)
        both = nn(lk_ref[...], mask_ref[:, cols])
        trans = jnp.exp(both[:L] + both[L:])
        trans_ref[:, cols] = trans
        high, low = split2(trans * alpha_ref[:, cols])
        for t in range(tiles):
            here = ones_where(tile_all[b : b + 1, :] == float(t))
            here = jnp.broadcast_to(here, (L, L)).astype(BF16)
            wm_hi[t * L : t * L + L, cols] = high * here
            wm_lo[t * L : t * L + L, cols] = low * here

    w_hi, w_lo = split2(weight_ref[...])
    w_pair = jnp.concatenate([w_hi, w_hi], axis=0)
    w_both = jnp.concatenate([w_hi, w_lo], axis=0)
    width = weight_ref.shape[1]
    squares = jnp.zeros((1, width), F32)
    bias_sum = jnp.zeros((1, width), F32)
    dw_ref[...] = jnp.zeros(dw_ref.shape, F32)
    fetch.wait()
    step = 2 * L
    for r in range(tiles // 2):
        rows = slice(r * step, r * step + step)
        both = nn(wm_hi[rows, :], feat_ref[...])
        rendered = both[:, :L] + both[:, L:] + nn(wm_lo[rows, :], feat_ref[:, 0:L])
        high, low = split2(rendered)
        rt_hi, rt_lo = split2(rendered.T)
        rt_ref[0:L, rows] = rt_hi
        rt_ref[L : 2 * L, rows] = rt_lo
        decoded = nn(jnp.concatenate([high, low], axis=1), w_pair) + nn(high, w_lo)
        resid = decoded + bias_ref[...] - teacher_ref[rows, :]
        squares = squares + jnp.sum(resid * resid, axis=0, keepdims=True)
        bias_sum = bias_sum + jnp.sum(resid, axis=0, keepdims=True)
        high, low = split2(resid)
        resid_hi[rows, :] = high
        resid_lo[rows, :] = low
        both = nt(high, w_both)
        grad = both[:, :L] + both[:, L:] + nt(low, w_hi)
        high, low = split2(grad)
        pair = jnp.concatenate([high, low], axis=1)
        dt_hi, dt_lo = split2(grad.T)
        drt_ref[0:L, rows] = dt_hi
        drt_ref[L : 2 * L, rows] = dt_lo
        for b in range(0, 8, 2):
            entries = slice(b * L, b * L + step)
            part = nt(pair, feat2_ref[entries, :]) + nt(high, feat_ref[entries, L : 2 * L])
            for q in range(2):
                cols = slice((b + q) * L, (b + q) * L + L)
                tile = tile_all[b + q : b + q + 1, :]
                got = part[:, q * L : q * L + L]
                kept = jnp.where(tile == float(2 * r), got[:L], dw_ref[:, cols])
                dw_ref[:, cols] = jnp.where(tile == float(2 * r + 1), got[L:], kept)

    both = nn(rt_ref[...], resid_hi[...])
    grad_w = both[:L] + both[L:] + nn(rt_ref[0:L, :], resid_lo[...])

    for b in range(8):
        cols = slice(b * L, b * L + L)
        high, low = split2(dw_ref[:, cols] * (trans_ref[:, cols] * alpha_ref[:, cols]))
        lk_ref[0:L, cols] = high
        lk_ref[L : 2 * L, cols] = low

    blocks = []
    for b in range(8):
        cols = slice(b * L, b * L + L)
        both = nt(lk_ref[...], mask_ref[cols, :])
        alpha = alpha_ref[:, cols]
        dalpha = dw_ref[:, cols] * trans_ref[:, cols] - (both[:L] + both[L:]) / (1.0 - alpha)
        prm, dx, dy = geometry(b)
        dpower = dalpha * alpha
        dopac = jnp.sum(dalpha * ex_ref[:, cols], axis=0, keepdims=True)
        flat = jnp.zeros((16, L), F32)
        by_y = jnp.zeros((16, L), F32)
        by_yy = jnp.zeros((16, L), F32)
        for j in range(8):
            part = dpower[j * 16 : j * 16 + 16]
            scaled = part * dy[j : j + 1]
            flat = flat + part
            by_y = by_y + scaled
            by_yy = by_yy + scaled * dy[j : j + 1]

        def total(value):
            return jnp.sum(value, axis=0, keepdims=True)

        sx = total(flat * dx)
        sxx = total(flat * dx * dx)
        sy = total(by_y)
        sxy = total(by_y * dx)
        syy = total(by_yy)
        blocks += [
            prm[2:3] * sx + prm[3:4] * sy,
            prm[4:5] * sy + prm[3:4] * sx,
            -0.5 * sxx,
            -sxy,
            -0.5 * syy,
            dopac,
            jnp.zeros((2, L), F32),
        ]

    sq_row = jnp.broadcast_to(jnp.sum(squares, axis=1, keepdims=True), (1, L))
    first = stripe == 0
    half = width // 2
    for side, ref in ((0, keep_ref), (1, give_ref)):
        for c in range(4):
            b = side * 4 + c
            cols = slice(b * L, b * L + L)
            both = nn(drt_ref[...], wm_hi[:, cols])
            grad = both[:L] + both[L:] + nn(drt_ref[0:L, :], wm_lo[:, cols])
            ref[pl.ds(c, L, stride=RET), :] = grad.T
        left = first if side == 0 else jnp.logical_not(first)
        piece = jnp.where(left, bias_sum[:, :half], bias_sum[:, half:])
        extra = blocks[side * 28 : side * 28 + 28] + [piece[:, :L], piece[:, L:], sq_row]
        ref[pl.ds(4, L, stride=RET), :] = column_of(jnp.concatenate(extra, axis=0))
        piece = jnp.where(left, grad_w[:, :half], grad_w[:, half:])
        ref[pl.ds(5, L, stride=RET), :] = piece[:, :L]
        ref[pl.ds(6, L, stride=RET), :] = piece[:, L:]


def share_kernel(got_ref, out_ref):
    for at, row in enumerate((5, 6, 4)):
        total = jnp.sum(got_ref[pl.ds(row, L, stride=RET), :], axis=0, keepdims=True)
        out_ref[pl.ds(at, L, stride=GAT), :] = jnp.broadcast_to(total, (L, L))


def scatter_kernel(par_ref, idx_ref, own_ref, peer_ref, feat_ref, prm_ref):
    gauss = feat_ref.shape[0]
    groups = gauss // L
    first = par_ref[0] == 0
    idx = idx_ref[...]
    top, bottom = idx[0:4], idx[4:8]
    idx = jnp.concatenate(
        [jnp.where(first, top, bottom), jnp.where(first, bottom, top)], axis=0
    )
    grads = []
    hots = []
    sub = lax.broadcasted_iota(jnp.int32, (gauss, L), 0)
    low_iota = lax.broadcasted_iota(jnp.int32, (L, L), 0)
    params = jnp.zeros((2 * groups * 8, L), F32)
    for side, ref in ((0, own_ref), (1, peer_ref)):
        prm = ref[pl.ds(4, L, stride=RET), :].T
        for c in range(4):
            b = side * 4 + c
            row = idx[b : b + 1]
            high, low = split2(ref[pl.ds(c, L, stride=RET), :])
            grads.append(jnp.concatenate([high, low], axis=1))
            hots.append(ones_where(row == sub).astype(BF16))
            block = prm[c * 8 : c * 8 + 8]
            spread = jnp.concatenate(
                [jnp.where((row >> 7) == g, block, 0.0) for g in range(groups)], axis=0
            )
            both = jnp.concatenate(split2(spread), axis=0)
            hot = ones_where((row & (L - 1)) == low_iota).astype(BF16)
            params = params + nt(both, hot)
    params = params[: groups * 8] + params[groups * 8 :]
    for g in range(groups):
        prm_ref[:, g * L : g * L + L] = params[g * 8 : g * 8 + 6]
    onehot = jnp.concatenate(hots, axis=1)
    both = nn(onehot, jnp.concatenate(grads, axis=0))
    feat_ref[...] = both[:, :L] + both[:, L:]


def finish_kernel(pixels, par_ref, own_ref, peer_ref, weight_ref, bias_ref, loss_ref):
    first = par_ref[0] == 0
    width = weight_ref.shape[1]
    scale = 1.0 / pixels

    def halves(ref):
        wide = jnp.concatenate(
            [ref[pl.ds(0, L, stride=GAT), :], ref[pl.ds(1, L, stride=GAT), :]], axis=1
        )
        small = ref[pl.ds(2, L, stride=GAT), :].T
        return wide * scale, jnp.concatenate([small[32:33], small[33:34]], axis=1) * scale, small

    own_w, own_b, small = halves(own_ref)
    peer_w, peer_b, unused = halves(peer_ref)
    weight_ref[:, : width // 2] = jnp.where(first, own_w, peer_w)
    weight_ref[:, width // 2 :] = jnp.where(first, peer_w, own_w)
    bias_ref[:, : width // 2] = jnp.where(first, own_b, peer_b)
    bias_ref[:, width // 2 :] = jnp.where(first, peer_b, own_b)
    loss_ref[...] = small[34:35, :] * (scale / width)


def call(kernel, shapes, specs, scratch=()):
    single = not isinstance(shapes, (list, tuple))
    count = 1 if single else len(shapes)
    return pl.pallas_call(
        kernel,
        out_shape=shapes,
        in_specs=specs,
        out_specs=VMEM if single else [VMEM] * count,
        scratch_shapes=list(scratch),
        compiler_params=PARAMS,
    )


def f32(*shape):
    return jax.ShapeDtypeStruct(shape, F32)


def pack(par, idx, features, gauss_params):
    return call(pack_kernel, f32(FWD * L, L), [SMEM, VMEM, VMEM, VMEM])(
        par, idx, features, gauss_params
    )


def keys(par, tile_lists):
    return call(key_kernel, [f32(8, L), f32(L, L)], [SMEM, VMEM])(par, tile_lists)


def main(par, own, peer, keyrow, keycol, teacher, weight, bias, length):
    pixels, width = teacher.shape
    pool = 8 * L
    scratch = [
        pltpu.VMEM((pixels, width), F32),
        pltpu.SemaphoreType.DMA,
        pltpu.VMEM((pool, pool), BF16),
        pltpu.VMEM((64, L), F32),
        pltpu.VMEM((pool, 2 * L), BF16),
        pltpu.VMEM((pool, 2 * L), BF16),
        pltpu.VMEM((L, pool), F32),
        pltpu.VMEM((L, pool), F32),
        pltpu.VMEM((L, pool), F32),
        pltpu.VMEM((2 * L, pool), BF16),
        pltpu.VMEM((pixels, pool), BF16),
        pltpu.VMEM((pixels, pool), BF16),
        pltpu.VMEM((2 * L, pixels), BF16),
        pltpu.VMEM((pixels, width), BF16),
        pltpu.VMEM((pixels, width), BF16),
        pltpu.VMEM((2 * L, pixels), BF16),
        pltpu.VMEM((L, pool), F32),
    ]
    return call(
        functools.partial(main_kernel, float(length)),
        [f32(RET * L, L), f32(RET * L, L)],
        [SMEM, VMEM, VMEM, VMEM, VMEM, pl.BlockSpec(memory_space=pl.ANY), VMEM, VMEM],
        scratch,
    )(par, own, peer, keyrow, keycol, teacher, weight, bias)


def share(got):
    return call(share_kernel, f32(GAT * L, L), [VMEM])(got)


def scatter(par, idx, own, peer, gauss):
    return call(scatter_kernel, [f32(gauss, L), f32(6, gauss)], [SMEM, VMEM, VMEM, VMEM])(
        par, idx, own, peer
    )


def finish(par, own, peer, width, pixels):
    return call(
        functools.partial(finish_kernel, float(pixels)),
        [f32(L, width), f32(1, width), f32(1, L)],
        [SMEM, VMEM, VMEM],
    )(par, own, peer)


def swap(value):
    return lax.ppermute(value, "px", SWAP)


def exchange(value, rows):
    sent = value.reshape(L, 1, rows * L)
    return lax.all_to_all(sent, "gs", split_axis=0, concat_axis=0, tiled=True).reshape(rows * L, L)


def per_device(
    features, gauss_params, send_index, tile_ids, tile_lists, teacher, decoder_weight, decoder_bias
):
    holders = lax.axis_size("gs")
    stripe = lax.axis_index("px").astype(jnp.int32)
    par = jnp.concatenate([stripe[None], tile_ids])
    idx = send_index.reshape(holders, -1).T
    width = teacher.shape[2]
    got = exchange(pack(par, idx, features, gauss_params), FWD)
    keyrow, keycol = keys(par, tile_lists)
    keep, give = main(
        par,
        got,
        swap(got),
        keyrow,
        keycol,
        teacher.reshape(-1, width),
        decoder_weight,
        decoder_bias.reshape(1, -1),
        tile_lists.shape[1],
    )
    back = exchange(keep + swap(give), RET)
    shares = exchange(share(back), GAT)
    grad_features, grad_params = scatter(par, idx, back, swap(back), features.shape[0])
    pixels = holders * tile_ids.shape[0] * 256
    grad_weight, grad_bias, loss = finish(par, shares, swap(shares), width, pixels)
    return grad_features, grad_params, grad_weight, grad_bias.reshape(-1), loss[0, 0]


def solution(mesh):
    return jax.shard_map(
        per_device,
        mesh=mesh,
        in_specs=(
            P("gs", None),
            P(None, "gs"),
            P("gs"),
            P("gs"),
            P("gs", None),
            P("gs", "px", None),
            P(),
            P(),
        ),
        out_specs=(P("gs", None), P(None, "gs"), P(), P(), P()),
        check_vma=False,
    )
```

time: 997 us -> 107 us (0.11); the launches traced: 987 us -> 107 us
  matrix products: 227 us -> 0 us
  local copies, waits for them, and re-layouts: 224 us -> 3.99 us
  waiting for transfers between devices: 198 us -> 11.3 us
  other arithmetic: 173 us -> 0.82 us
  blocking collectives: 112 us -> 54.4 us
  Pallas kernels: 0 us -> 20.2 us
  between operations: 17.6 us -> 0.69 us
  starting transfers between devices: 30 us -> 15.2 us
    dot_general x163 -> x0, matrix products: 227 us -> none  [the longest x96 122 us: advance(): blended = blended + jnp.dot(weights, feat_block, precision=HIGH)]
    psum x2 -> x0, waiting for transfers between devices: 167 us -> none  [the longest x1 167 us: per_device(): totals = lax.psum((grad_weight, grad_bias, squares), ('gs', 'px'))]
    psum x2 -> x0, blocking collectives: 86.7 us -> none  [the longest x1 77.7 us: per_device(): totals = lax.psum((grad_weight, grad_bias, squares), ('gs', 'px'))]
    squeeze x88 -> x0, local copies, waits for them, and re-layouts: 82.4 us -> none  [the longest x56 82.3 us: local_objective(): rendered = lax.map(one_tile, (clamped, live_mask, pixel_x, pixel_y))]
    scatter-add x18 -> x0, other arithmetic: 79.7 us -> none  [the longest x8 33.2 us: one_tile(): pool_feat[tile_index]]
    dynamic_update_slice x80 -> x0, local copies, waits for them, and re-layouts: 75.8 us -> none  [local_objective(): rendered = lax.map(one_tile, (clamped, live_mask, pixel_x, pixel_y))]
    reduce_sum x64 -> x0, other arithmetic: 61.4 us -> none  [the longest x32 33.4 us: advance(): prm_block[None, :, 3] * delta_x * delta_y]
    all_to_all x1 -> x2, blocking collectives: 25 us -> 54.4 us  [exchange(): lax.all_to_all(sent, 'gs', split_axis=0, concat_axis=0, tiled=True)]
  transfers between devices with their start and end apart: 5 -> 5, of which waited for: 3 -> 3; matrix products, arithmetic and copies ran while one was open for 2% -> 0% of each run, Pallas kernels for 0% -> 4%
where the time goes in v1:
time: 107 us
  blocking collectives  54.4 us (51%)
  Pallas kernels  20.2 us (19%)
  starting transfers between devices  15.2 us (14%)
  waiting for transfers between devices  11.3 us (11%)
  local copies, waits for them, and re-layouts  3.99 us (4%)
    all_to_all x2, blocking collectives, exchange(): lax.all_to_all(sent, 'gs', split_axis=0, concat_axis=0, tiled=True)  54.4 us
    pallas_call x1, Pallas kernels, main(): call(functools.partial(main_kernel, float(length)), [f32(RET * L, L), f32...  12.5 us
    all_to_all x1, waiting for transfers between devices, exchange(): lax.all_to_all(sent, 'gs', split_axis=0, concat_axis=0, tiled=True)  9.65 us
    ppermute x4, starting transfers between devices, swap(): return lax.ppermute(value, 'px', SWAP)  8.83 us
    all_to_all x1, starting transfers between devices, exchange(): lax.all_to_all(sent, 'gs', split_axis=0, concat_axis=0, tiled=True)  6.4 us
    unnamed x12, local copies, waits for them, and re-layouts  3.03 us
    pallas_call x1, Pallas kernels, scatter(): call(scatter_kernel, [f32(gauss, L), f32(6, gauss)], [SMEM, VMEM, VMEM, V...  2.94 us
  transfers between devices with their start and end apart: 5, of which 3 were waited for; matrix products, arithmetic and copies ran while one was open for 0% of the time, Pallas kernels for 4%

profile of v1, /device:TPU:1, one launch (start us, length us, event | category | flops | bytes accessed | tf_op | source)
XLA Modules:
  0.0 106.5 jit_solution(1000691563439124838)
XLA Ops:
  0.6 0.9 reshape.40
  1.6 0.8 pad_add_fusion.par_ref
  2.4 1.2 %copy-done.1 = f32[2048,128]{1,0:T(8,128)S(1)} copy-done((f32[2048,128]{1,0:T(8,128)S(1)}, f32[2048,128]{1,0:T(8,128)}, u32[]{:S(2)}) %copy-start.1) | copy-done | bytes 1048600
  3.6 0.8 copy-done.3
  4.4 1.6 %shard_map.119 = f32[640,128]{1,0:T(8,128)S(1)} custom-call(s32[9]{0:T(128)S(1)} %pad_add_fusion.par_ref, s32[8,128]{1,0:T(8,128)S(1)} %bitcast.22, f32[2048,128]{1,0:T(8,128)S(1)} %copy-done.1, f32[6,2048]{1,0:T(8,128)S(1)} %copy-done.3), custom_call_target="tpu_custom_call" | custom-call | tf_op jit(solution)/shard_map/pallas_call | solution.py:396
  6.0 30.8 %all_to_all.15 = f32[128,1,640]{2,1,0:T(1,128)S(1)} all-to-all(f32[128,1,640]{2,1,0:T(1,128)S(1)} %bitcast.19), channel_id=1, replica_groups=mesh['gs'=128,'px'=2] {'gs'}, dimensions={0} | all-to-all | bytes 655360 | tf_op jit(solution)/shard_map/all_to_all | solution.py:459
  36.9 2.8 %collective-permute-start = (f32[640,128]{1,0:T(8,128)S(1)}, f32[640,128]{1,0:T(8,128)S(1)}, u32[]{:S(2)}, u32[]{:S(2)}) collective-permute-start(f32[640,128]{1,0:T(8,128)S(1)} %bitcast.17), channel_id=1, source_target_pairs={{0,1},{1,0},{2,3},{3,2},{4,5},{5,4},{6,7},{7,6},{8,9},{9,8},{10,11... | collective-permute-start | bytes 983048 | tf_op jit(solution)/shard_map/ppermute | solution.py:454
  39.6 1.1 %shard_map.120 = (f32[8,128]{1,0:T(8,128)S(1)}, f32[128,128]{1,0:T(8,128)S(1)}) custom-call(s32[9]{0:T(128)S(1)} %pad_add_fusion.par_ref, s32[8,512]{1,0:T(8,128)S(1)} %copy-done.4), custom_call_target="tpu_custom_call" | custom-call | tf_op jit(solution)/shard_map/pallas_call | solution.py:402
  40.7 0.2 collective-permute-done.peer_ref
  40.9 0.9 copy-done.2
  41.9 12.5 %shard_map.121 = (f32[896,128]{1,0:T(8,128)S(1)}, f32[896,128]{1,0:T(8,128)S(1)}) custom-call(s32[9]{0:T(128)S(1)} %pad_add_fusion.par_ref, f32[640,128]{1,0:T(8,128)S(1)} %bitcast.18, f32[640,128]{1,0:T(8,128)S(1)} %collective-permute-done.peer_ref, f32[8,128]{1,0:T(8,128)S(1)} %get-tuple-element.14.keyrow_ref, ...), custom_call_target="tpu_custom_call" | custom-call | tf_op jit(solution)/shard_map/pallas_call | solution.py:427
  54.4 0.5 collective-permute-start.1
  54.9 1.4 %collective-permute-done.1 = f32[896,128]{1,0:T(8,128)S(1)} collective-permute-done((f32[896,128]{1,0:T(8,128)S(1)}, f32[896,128]{1,0:T(8,128)S(1)}, u32[]{:S(2)}, u32[]{:S(2)}) %collective-permute-start.1) | collective-permute-done | bytes 458784 | tf_op jit(solution)/shard_map/ppermute | solution.py:454
  56.3 0.1 add.3
  56.4 23.6 %all_to_all.16 = f32[128,1,896]{2,1,0:T(1,128)S(1)} all-to-all(f32[128,1,896]{2,1,0:T(1,128)S(1)} %bitcast.25), channel_id=1, replica_groups=mesh['gs'=128,'px'=2] {'gs'}, dimensions={0} | all-to-all | bytes 917504 | tf_op jit(solution)/shard_map/all_to_all | solution.py:459
  79.9 0.7 shard_map.123
  80.6 6.4 %all-to-all-start.2 = ((f32[128,1,384]{2,1,0:T(1,128)}), f32[128,1,384]{2,1,0:T(1,128)S(1)}, u32[]{:S(2)}, u32[]{:S(2)}) async-start(f32[128,1,384]{2,1,0:T(1,128)} %bitcast.8), calls=%async_computation.2 | async-start | bytes 393216 | tf_op jit(solution)/shard_map/all_to_all | solution.py:459
  87.1 2.3 %collective-permute-start.2 = (f32[896,128]{1,0:T(8,128)S(1)}, f32[896,128]{1,0:T(8,128)S(1)}, u32[]{:S(2)}, u32[]{:S(2)}) collective-permute-start(f32[896,128]{1,0:T(8,128)S(1)} %bitcast.14), channel_id=1, source_target_pairs={{0,1},{1,0},{2,3},{3,2},{4,5},{5,4},{6,7},{7,6},{8,9},{9,8},{10,11... | collective-permute-start | bytes 1376264 | tf_op jit(solution)/shard_map/ppermute | solution.py:454
  89.3 9.6 %all-to-all-done.2 = f32[128,1,384]{2,1,0:T(1,128)S(1)} async-done(((f32[128,1,384]{2,1,0:T(1,128)}), f32[128,1,384]{2,1,0:T(1,128)S(1)}, u32[]{:S(2)}, u32[]{:S(2)}) %all-to-all-start.2) | async-done | bytes 196640 | tf_op jit(solution)/shard_map/all_to_all | solution.py:459
  99.0 3.3 %collective-permute-start.3 = (f32[384,128]{1,0:T(8,128)S(1)}, f32[384,128]{1,0:T(8,128)S(1)}, u32[]{:S(2)}, u32[]{:S(2)}) collective-permute-start(f32[384,128]{1,0:T(8,128)S(1)} %bitcast.20), channel_id=1, source_target_pairs={{0,1},{1,0},{2,3},{3,2},{4,5},{5,4},{6,7},{7,6},{8,9},{9,8},{10,11... | collective-permute-start | bytes 589832 | tf_op jit(solution)/shard_map/ppermute | solution.py:454
  102.3 0.0 collective-permute-done.2.peer_ref
  102.3 2.9 %shard_map.122 = (f32[2048,128]{1,0:T(8,128)}, f32[6,2048]{1,0:T(8,128)}) custom-call(s32[9]{0:T(128)S(1)} %pad_add_fusion.par_ref, s32[8,128]{1,0:T(8,128)S(1)} %bitcast.23, f32[896,128]{1,0:T(8,128)S(1)} %bitcast.15, f32[896,128]{1,0:T(8,128)S(1)} %collective-permute-done.2.peer_ref), custom_call_target="tpu_custom_call" | custom-call | tf_op jit(solution)/shard_map/pallas_call | solution.py:440
  105.2 0.0 collective-permute-done.3.peer_ref
  105.2 1.3 %shard_map.124 = (f32[128,512]{1,0:T(8,128)}, f32[1,512]{1,0:T(1,128)}, f32[1,128]{1,0:T(1,128)}) custom-call(s32[9]{0:T(128)S(1)} %pad_add_fusion.par_ref, f32[384,128]{1,0:T(8,128)S(1)} %bitcast.21, f32[384,128]{1,0:T(8,128)S(1)} %collective-permute-done.3.peer_ref), custom_call_target="tpu_custom_call" | custom-call | tf_op jit(solution)/shard_map/pallas_call | solution.py:446
  (10 shorter events, 0.1 us)
Async XLA Ops:
  0.6 40.3 %copy-start = (f32[8,128,512]{2,1,0:T(8,128)S(1)}, f32[8,128,512]{2,1,0:T(8,128)}, u32[]{:S(2)}) copy-start(f32[8,128,512]{2,1,0:T(8,128)} %param.13) | copy-start | bytes 6291460
  2.4 1.2 %copy-start.1 = (f32[2048,128]{1,0:T(8,128)S(1)}, f32[2048,128]{1,0:T(8,128)}, u32[]{:S(2)}) copy-start(f32[2048,128]{1,0:T(8,128)} %feat_ref.1) | copy-start | bytes 3145732
  3.6 0.8 copy-start.3
  4.4 35.2 %copy-start.4 = (s32[8,512]{1,0:T(8,128)S(1)}, s32[8,512]{1,0:T(8,128)}, u32[]{:S(2)}) copy-start(s32[8,512]{1,0:T(8,128)} %lists_ref.1) | copy-start | bytes 49156
  4.4 36.5 %copy-start.5 = (f32[512]{0:T(512)S(1)}, f32[512]{0:T(512)}, u32[]{:S(2)}) copy-start(f32[512]{0:T(512)} %param.15) | copy-start | bytes 6148
  36.9 4.0 %collective-permute-start = (f32[640,128]{1,0:T(8,128)S(1)}, f32[640,128]{1,0:T(8,128)S(1)}, u32[]{:S(2)}, u32[]{:S(2)}) collective-permute-start(f32[640,128]{1,0:T(8,128)S(1)} %bitcast.17), channel_id=1, source_target_pairs={{0,1},{1,0},{2,3},{3,2},{4,5},{5,4},{6,7},{7,6},{8,9},{9,8},{10,11... | collective-permute-start | bytes 983048 | tf_op jit(solution)/shard_map/ppermute | solution.py:454
  40.9 1.0 copy-start.2
  54.4 1.9 %collective-permute-start.1 = (f32[896,128]{1,0:T(8,128)S(1)}, f32[896,128]{1,0:T(8,128)S(1)}, u32[]{:S(2)}, u32[]{:S(2)}) collective-permute-start(f32[896,128]{1,0:T(8,128)S(1)} %get-tuple-element.17), channel_id=1, source_target_pairs={{0,1},{1,0},{2,3},{3,2},{4,5},{5,4},{6,7},{7,6},{8,9},{9,8},{10,11... | collective-permute-start | bytes 1376264 | tf_op jit(solution)/shard_map/ppermute | solution.py:454
  80.6 18.3 %all-to-all-start.2 = ((f32[128,1,384]{2,1,0:T(1,128)}), f32[128,1,384]{2,1,0:T(1,128)S(1)}, u32[]{:S(2)}, u32[]{:S(2)}) async-start(f32[128,1,384]{2,1,0:T(1,128)} %bitcast.8), calls=%async_computation.2 | async-start | bytes 393216 | tf_op jit(solution)/shard_map/all_to_all | solution.py:459
  87.1 15.2 %collective-permute-start.2 = (f32[896,128]{1,0:T(8,128)S(1)}, f32[896,128]{1,0:T(8,128)S(1)}, u32[]{:S(2)}, u32[]{:S(2)}) collective-permute-start(f32[896,128]{1,0:T(8,128)S(1)} %bitcast.14), channel_id=1, source_target_pairs={{0,1},{1,0},{2,3},{3,2},{4,5},{5,4},{6,7},{7,6},{8,9},{9,8},{10,11... | collective-permute-start | bytes 1376264 | tf_op jit(solution)/shard_map/ppermute | solution.py:454
  99.0 6.3 %collective-permute-start.3 = (f32[384,128]{1,0:T(8,128)S(1)}, f32[384,128]{1,0:T(8,128)S(1)}, u32[]{:S(2)}, u32[]{:S(2)}) collective-permute-start(f32[384,128]{1,0:T(8,128)S(1)} %bitcast.20), channel_id=1, source_target_pairs={{0,1},{1,0},{2,3},{3,2},{4,5},{5,4},{6,7},{7,6},{8,9},{9,8},{10,11... | collective-permute-start | bytes 589832 | tf_op jit(solution)/shard_map/ppermute | solution.py:454

commit v2 on v1

--- a/solution.py
+++ b/solution.py
@@ -48,10 +48,27 @@
     return jnp.concatenate([rows, pad], axis=0).T
 
 
-def pack_kernel(par_ref, idx_ref, feat_ref, prm_ref, out_ref):
+def slot_rows(raw):
+    slot = lax.broadcasted_iota(jnp.int32, (8, L), 1) & 7
+    mine = slot == lax.broadcasted_iota(jnp.int32, (8, L), 0)
+    spread = []
+    for r in range(8):
+        row = raw[r : r + 1, :]
+        high = jnp.where(mine, row >> 4, 0).astype(F32)
+        low = jnp.where(mine, row & 15, 0).astype(F32)
+        spread.append(jnp.concatenate([high, low], axis=0).astype(BF16))
+    source = lax.broadcasted_iota(jnp.int32, (8 * L, L), 0) >> 3
+    owner = lax.broadcasted_iota(jnp.int32, (8 * L, L), 1)
+    got = nn(jnp.concatenate(spread, axis=1), ones_where(source == owner).astype(BF16))
+    return (got[:8] * 16.0 + got[8:]).astype(jnp.int32)
+
+
+def pack_kernel(par_ref, send_ref, feat_ref, prm_ref, out_ref, idx_ref):
     gauss = feat_ref.shape[0]
     first = par_ref[0] == 0
-    rows = jnp.where(first, idx_ref[0:4, :], idx_ref[4:8, :])
+    idx = slot_rows(send_ref[...])
+    idx_ref[...] = idx
+    rows = jnp.where(first, idx[0:4, :], idx[4:8, :])
     cols = column_of(rows.astype(F32))
     high, mid = split2(feat_ref[...])
     table = jnp.concatenate([high, mid], axis=1)
@@ -79,7 +96,8 @@
     out_ref[pl.ds(4, L, stride=FWD), :] = column_of(jnp.concatenate(packed, axis=0))
 
 
-def key_kernel(par_ref, lists_ref, row_ref, col_ref):
+def key_kernel(par_ref, lists_ref, weight_ref, row_ref, mask_ref, high_ref, low_ref):
+    high_ref[...], low_ref[...] = split2(weight_ref[...])
     shift = par_ref[0] * 4
     tiles, length = lists_ref.shape
     slot_iota = lax.broadcasted_iota(jnp.int32, (8, length), 0)
@@ -100,24 +118,31 @@
     tile = total[0:8]
     key = jnp.where(tile > 0.5, (tile - 1.0) * length + total[8:16] * 16.0 + total[16:24], -1.0)
     row_ref[...] = key
-    col_ref[...] = column_of(key)
+    cols = column_of(key)
+    base = jnp.where(key >= 0.0, (tile - 1.0) * length, 1.0e9)
+    for a in range(8):
+        front = jnp.broadcast_to(cols[:, a : a + 1], (L, L))
+        for b in range(8):
+            hit = (front < key[b : b + 1, :]) & (front >= base[b : b + 1, :])
+            mask_ref[a * L : a * L + L, b * L : b * L + L] = ones_where(hit).astype(BF16)
 
 
 def main_kernel(
     length,
     par_ref,
+    ids_ref,
     own_ref,
     peer_ref,
     keyrow_ref,
-    keycol_ref,
+    mask_ref,
     teacher_hbm,
-    weight_ref,
+    whigh_ref,
+    wlow_ref,
     bias_ref,
     keep_ref,
     give_ref,
     teacher_ref,
     teacher_sem,
-    mask_ref,
     prm_ref,
     feat_ref,
     feat2_ref,
@@ -140,11 +165,10 @@
     keyrow = keyrow_ref[...]
     live_all = keyrow >= 0.0
     tile_all = jnp.floor(keyrow * (1.0 / length))
-    base_all = jnp.where(live_all, tile_all * length, 1.0e9)
     ox_all = jnp.zeros((8, L), F32)
     oy_all = jnp.zeros((8, L), F32)
     for t in range(tiles):
-        ident = par_ref[1 + t]
+        ident = ids_ref[t]
         here = tile_all == float(t)
         ox_all = jnp.where(here, ((ident & 127) * 16).astype(F32) + 0.5, ox_all)
         oy_all = jnp.where(here, ((ident >> 7) * 16 + stripe * 8).astype(F32) + 0.5, oy_all)
@@ -159,12 +183,6 @@
             feat2_ref[at : at + L, 0:L] = high
             feat2_ref[at : at + L, L : 2 * L] = high
         prm_ref[side * 32 : side * 32 + 32, :] = ref[pl.ds(4, L, stride=FWD), :].T[0:32]
-
-    for a in range(8):
-        front = jnp.broadcast_to(keycol_ref[:, a : a + 1], (L, L))
-        for b in range(8):
-            hit = (front < keyrow[b : b + 1, :]) & (front >= base_all[b : b + 1, :])
-            mask_ref[a * L : a * L + L, b * L : b * L + L] = ones_where(hit).astype(BF16)
 
     kx = lax.broadcasted_iota(jnp.int32, (16, L), 0).astype(F32)
     ky = lax.broadcasted_iota(jnp.int32, (8, L), 0).astype(F32)
@@ -205,10 +223,10 @@
             wm_hi[t * L : t * L + L, cols] = high * here
             wm_lo[t * L : t * L + L, cols] = low * here
 
-    w_hi, w_lo = split2(weight_ref[...])
+    w_hi, w_lo = whigh_ref[...], wlow_ref[...]
     w_pair = jnp.concatenate([w_hi, w_hi], axis=0)
     w_both = jnp.concatenate([w_hi, w_lo], axis=0)
-    width = weight_ref.shape[1]
+    width = whigh_ref.shape[1]
     squares = jnp.zeros((1, width), F32)
     bias_sum = jnp.zeros((1, width), F32)
     dw_ref[...] = jnp.zeros(dw_ref.shape, F32)
@@ -375,9 +393,10 @@
     loss_ref[...] = small[34:35, :] * (scale / width)
 
 
-def call(kernel, shapes, specs, scratch=()):
+def call(kernel, shapes, specs, scratch=(), flops=0):
     single = not isinstance(shapes, (list, tuple))
     count = 1 if single else len(shapes)
+    cost = pl.CostEstimate(flops=flops, bytes_accessed=flops // 300, transcendentals=0)
     return pl.pallas_call(
         kernel,
         out_shape=shapes,
@@ -385,6 +404,7 @@
         out_specs=VMEM if single else [VMEM] * count,
         scratch_shapes=list(scratch),
         compiler_params=PARAMS,
+        cost_estimate=cost,
     )
 
 
@@ -392,23 +412,28 @@
     return jax.ShapeDtypeStruct(shape, F32)
 
 
-def pack(par, idx, features, gauss_params):
-    return call(pack_kernel, f32(FWD * L, L), [SMEM, VMEM, VMEM, VMEM])(
-        par, idx, features, gauss_params
-    )
-
-
-def keys(par, tile_lists):
-    return call(key_kernel, [f32(8, L), f32(L, L)], [SMEM, VMEM])(par, tile_lists)
-
-
-def main(par, own, peer, keyrow, keycol, teacher, weight, bias, length):
+def bf16(*shape):
+    return jax.ShapeDtypeStruct(shape, BF16)
+
+
+def pack(par, send, features, gauss_params):
+    shapes = [f32(FWD * L, L), jax.ShapeDtypeStruct((8, L), jnp.int32)]
+    return call(pack_kernel, shapes, [SMEM, VMEM, VMEM, VMEM], flops=2 * 10**9)(
+        par, send, features, gauss_params
+    )
+
+
+def keys(par, tile_lists, weight):
+    shapes = [f32(8, L), bf16(8 * L, 8 * L), bf16(*weight.shape), bf16(*weight.shape)]
+    return call(key_kernel, shapes, [SMEM, VMEM, VMEM], flops=3 * 10**9)(par, tile_lists, weight)
+
+
+def main(par, ids, own, peer, keyrow, mask, teacher, whigh, wlow, bias, length):
     pixels, width = teacher.shape
     pool = 8 * L
     scratch = [
         pltpu.VMEM((pixels, width), F32),
         pltpu.SemaphoreType.DMA,
-        pltpu.VMEM((pool, pool), BF16),
         pltpu.VMEM((64, L), F32),
         pltpu.VMEM((pool, 2 * L), BF16),
         pltpu.VMEM((pool, 2 * L), BF16),
@@ -424,20 +449,23 @@
         pltpu.VMEM((2 * L, pixels), BF16),
         pltpu.VMEM((L, pool), F32),
     ]
+    anywhere = pl.BlockSpec(memory_space=pl.ANY)
     return call(
         functools.partial(main_kernel, float(length)),
         [f32(RET * L, L), f32(RET * L, L)],
-        [SMEM, VMEM, VMEM, VMEM, VMEM, pl.BlockSpec(memory_space=pl.ANY), VMEM, VMEM],
+        [SMEM, SMEM, VMEM, VMEM, VMEM, VMEM, anywhere, VMEM, VMEM, VMEM],
         scratch,
-    )(par, own, peer, keyrow, keycol, teacher, weight, bias)
+        flops=10**10,
+    )(par, ids, own, peer, keyrow, mask, teacher, whigh, wlow, bias)
 
 
 def share(got):
-    return call(share_kernel, f32(GAT * L, L), [VMEM])(got)
+    return call(share_kernel, f32(GAT * L, L), [VMEM], flops=10**9)(got)
 
 
 def scatter(par, idx, own, peer, gauss):
-    return call(scatter_kernel, [f32(gauss, L), f32(6, gauss)], [SMEM, VMEM, VMEM, VMEM])(
+    shapes = [f32(gauss, L), f32(6, gauss)]
+    return call(scatter_kernel, shapes, [SMEM, VMEM, VMEM, VMEM], flops=4 * 10**9)(
         par, idx, own, peer
     )
 
@@ -447,6 +475,7 @@
         functools.partial(finish_kernel, float(pixels)),
         [f32(L, width), f32(1, width), f32(1, L)],
         [SMEM, VMEM, VMEM],
+        flops=10**9,
     )(par, own, peer)
 
 
@@ -463,26 +492,33 @@
     features, gauss_params, send_index, tile_ids, tile_lists, teacher, decoder_weight, decoder_bias
 ):
     holders = lax.axis_size("gs")
-    stripe = lax.axis_index("px").astype(jnp.int32)
-    par = jnp.concatenate([stripe[None], tile_ids])
-    idx = send_index.reshape(holders, -1).T
+    par = lax.axis_index("px").astype(jnp.int32).reshape(1)
     width = teacher.shape[2]
-    got = exchange(pack(par, idx, features, gauss_params), FWD)
-    keyrow, keycol = keys(par, tile_lists)
+    sent, idx = pack(par, send_index.reshape(8, -1), features, gauss_params)
+    sent, tile_lists, decoder_weight, teacher = lax.optimization_barrier(
+        (sent, tile_lists, decoder_weight, teacher)
+    )
+    got = exchange(sent, FWD)
+    prepared = keys(par, tile_lists, decoder_weight)
+    got, prepared = lax.optimization_barrier((got, prepared))
+    keyrow, mask, whigh, wlow = prepared
     keep, give = main(
         par,
+        tile_ids,
         got,
         swap(got),
         keyrow,
-        keycol,
+        mask,
         teacher.reshape(-1, width),
-        decoder_weight,
+        whigh,
+        wlow,
         decoder_bias.reshape(1, -1),
         tile_lists.shape[1],
     )
     back = exchange(keep + swap(give), RET)
     shares = exchange(share(back), GAT)
-    grad_features, grad_params = scatter(par, idx, back, swap(back), features.shape[0])
+    grads = scatter(par, idx, back, swap(back), features.shape[0])
+    shares, (grad_features, grad_params) = lax.optimization_barrier((shares, grads))
     pixels = holders * tile_ids.shape[0] * 256
     grad_weight, grad_bias, loss = finish(par, shares, swap(shares), width, pixels)
     return grad_features, grad_params, grad_weight, grad_bias.reshape(-1), loss[0, 0]

time: 107 us -> 105 us (0.981)
  blocking collectives: 54.4 us -> 23.3 us
  waiting for transfers between devices: 11.3 us -> 26.2 us
  starting transfers between devices: 15.2 us -> 30 us
  local copies, waits for them, and re-layouts: 3.99 us -> 5.68 us
  Pallas kernels: 20.2 us -> 18.9 us
    all_to_all x2 -> x1, blocking collectives: 54.4 us -> 23.3 us  [exchange(): lax.all_to_all(sent, 'gs', split_axis=0, concat_axis=0, tiled=True)]
    all_to_all x1 -> x2, starting transfers between devices: 6.4 us -> 22.5 us  [exchange(): lax.all_to_all(sent, 'gs', split_axis=0, concat_axis=0, tiled=True)]
    all_to_all x1 -> x2, waiting for transfers between devices: 9.65 us -> 22.4 us  [exchange(): lax.all_to_all(sent, 'gs', split_axis=0, concat_axis=0, tiled=True)]
    unnamed x12 -> x20, local copies, waits for them, and re-layouts: 3.03 us -> 5.68 us
    ppermute x4, waiting for transfers between devices: 1.6 us -> 3.77 us  [swap(): return lax.ppermute(value, 'px', SWAP)]
    ppermute x4, starting transfers between devices: 8.83 us -> 7.47 us  [swap(): return lax.ppermute(value, 'px', SWAP)]
  transfers between devices with their start and end apart: 5 -> 6, of which waited for: 3 -> 5; matrix products, arithmetic and copies ran while one was open for 0% -> 0% of each run, Pallas kernels for 4% -> 4%
where the time goes in v2:
time: 105 us
  starting transfers between devices  30 us (29%)
  waiting for transfers between devices  26.2 us (25%)
  blocking collectives  23.3 us (22%)
  Pallas kernels  18.9 us (18%)
  local copies, waits for them, and re-layouts  5.68 us (5%)
    all_to_all x1, blocking collectives, exchange(): lax.all_to_all(sent, 'gs', split_axis=0, concat_axis=0, tiled=True)  23.3 us
    all_to_all x2, starting transfers between devices, exchange(): lax.all_to_all(sent, 'gs', split_axis=0, concat_axis=0, tiled=True)  22.5 us
    all_to_all x2, waiting for transfers between devices, exchange(): lax.all_to_all(sent, 'gs', split_axis=0, concat_axis=0, tiled=True)  22.4 us
    pallas_call x1, Pallas kernels, main(): call(functools.partial(main_kernel, float(length)), [f32(RET * L, L), f32...  11.7 us
    ppermute x4, starting transfers between devices, swap(): return lax.ppermute(value, 'px', SWAP)  7.47 us
    unnamed x20, local copies, waits for them, and re-layouts  5.68 us
    ppermute x4, waiting for transfers between devices, swap(): return lax.ppermute(value, 'px', SWAP)  3.77 us
    pallas_call x1, Pallas kernels, scatter(): call(scatter_kernel, shapes, [SMEM, VMEM, VMEM, VMEM], flops=4 * 10 ** 9)  2.41 us
  transfers between devices with their start and end apart: 6, of which 5 were waited for; matrix products, arithmetic and copies ran while one was open for 0% of the time, Pallas kernels for 4%

profile of v2, /device:TPU:1, one launch (start us, length us, event | category | flops | bytes accessed | tf_op | source)
XLA Modules:
  0.0 104.9 jit_solution(11229308980610318553)
XLA Ops:
  0.6 1.2 %copy-done.1 = f32[2048,128]{1,0:T(8,128)S(1)} copy-done((f32[2048,128]{1,0:T(8,128)S(1)}, f32[2048,128]{1,0:T(8,128)}, u32[]{:S(2)}) %copy-start.1) | copy-done | bytes 1048600
  1.9 0.8 copy-done.3
  2.7 0.7 copy-done.5
  3.4 1.9 %shard_map.119 = (f32[640,128]{1,0:T(8,128)}, s32[8,128]{1,0:T(8,128)S(1)}) custom-call(s32[1]{0:T(128)} %bitcast.par_ref, s32[8,128]{1,0:T(8,128)S(1)} %bitcast.21, f32[2048,128]{1,0:T(8,128)S(1)} %copy-done.1, f32[6,2048]{1,0:T(8,128)S(1)} %copy-done.3), custom_call_target="tpu_custom_call" | custom-call | flops 2000000000 | bytes 6666666 | tf_op jit(solution)/shard_map/pallas_call | solution.py:421
  5.3 16.3 %all-to-all-start = ((f32[128,1,640]{2,1,0:T(1,128)}), f32[128,1,640]{2,1,0:T(1,128)S(1)}, u32[]{:S(2)}, u32[]{:S(2)}) async-start(f32[128,1,640]{2,1,0:T(1,128)} %bitcast.2), calls=%async_computation | async-start | bytes 655360 | tf_op jit(solution)/shard_map/all_to_all | solution.py:488
  21.7 0.0 copy-start
  21.7 1.3 %shard_map.120 = (f32[8,128]{1,0:T(8,128)S(1)}, bf16[1024,1024]{1,0:T(8,128)(2,1)S(1)}, bf16[128,512]{1,0:T(8,128)(2,1)S(1)}, bf16[128,512]{1,0:T(8,128)(2,1)S(1)}) custom-call(s32[1]{0:T(128)} %bitcast.par_ref, s32[8,512]{1,0:T(8,128)S(1)} %copy-done.4, f32[128,512]{1,0:T(8,128)S(1)} %copy-done.2), custom_call_target="tpu_custom_call" | custom-call | flops 3000000000 | bytes 10000000 | tf_op jit(solution)/shard_map/pallas_call | solution.py:428
  23.1 1.3 %copy-done.8 = bf16[1024,1024]{1,0:T(8,128)(2,1)} copy-done((bf16[1024,1024]{1,0:T(8,128)(2,1)}, bf16[1024,1024]{1,0:T(8,128)(2,1)S(1)}, u32[]{:S(2)}) %copy-start.8) | copy-done | bytes 2097176
  24.4 12.0 %all-to-all-done = f32[128,1,640]{2,1,0:T(1,128)S(1)} async-done(((f32[128,1,640]{2,1,0:T(1,128)}), f32[128,1,640]{2,1,0:T(1,128)S(1)}, u32[]{:S(2)}, u32[]{:S(2)}) %all-to-all-start) | async-done | bytes 327712 | tf_op jit(solution)/shard_map/all_to_all | solution.py:488
  36.4 2.8 %collective-permute-start = (f32[640,128]{1,0:T(8,128)S(1)}, f32[640,128]{1,0:T(8,128)S(1)}, u32[]{:S(2)}, u32[]{:S(2)}) collective-permute-start(f32[640,128]{1,0:T(8,128)S(1)} %bitcast.16), channel_id=1, source_target_pairs={{0,1},{1,0},{2,3},{3,2},{4,5},{5,4},{6,7},{7,6},{8,9},{9,8},{10,11... | collective-permute-start | bytes 983048 | tf_op jit(solution)/shard_map/ppermute | solution.py:483
  39.2 1.3 %collective-permute-done.peer_ref = f32[640,128]{1,0:T(8,128)S(1)} collective-permute-done((f32[640,128]{1,0:T(8,128)S(1)}, f32[640,128]{1,0:T(8,128)S(1)}, u32[]{:S(2)}, u32[]{:S(2)}) %collective-permute-start) | collective-permute-done | bytes 327712 | tf_op jit(solution)/shard_map/ppermute | solution.py:483
  40.4 1.6 %copy-done.9 = bf16[1024,1024]{1,0:T(8,128)(2,1)S(1)} copy-done((bf16[1024,1024]{1,0:T(8,128)(2,1)S(1)}, bf16[1024,1024]{1,0:T(8,128)(2,1)}, u32[]{:S(2)}) %copy-start.9) | copy-done | bytes 2097176
  42.0 11.7 %shard_map.121 = (f32[896,128]{1,0:T(8,128)S(1)}, f32[896,128]{1,0:T(8,128)S(1)}) custom-call(s32[1]{0:T(128)} %bitcast.par_ref, s32[8]{0:T(128)S(1)} %copy-done.7, f32[640,128]{1,0:T(8,128)S(1)} %bitcast.17, f32[640,128]{1,0:T(8,128)S(1)} %collective-permute-done.peer_ref, f32[8,128]{1,0:T(8,128)S(1)} %get-tuple-element.39.keyrow_ref, ...), custom_call_target="tpu_custom_call" | custom-call | flops 10000000000 | bytes 33333332 | tf_op jit(solution)/shard_map/pallas_call | solution.py:453
  53.8 0.5 collective-permute-start.1
  54.2 1.4 %collective-permute-done.1 = f32[896,128]{1,0:T(8,128)S(1)} collective-permute-done((f32[896,128]{1,0:T(8,128)S(1)}, f32[896,128]{1,0:T(8,128)S(1)}, u32[]{:S(2)}, u32[]{:S(2)}) %collective-permute-start.1) | collective-permute-done | bytes 458784 | tf_op jit(solution)/shard_map/ppermute | solution.py:483
  55.7 23.3 %all_to_all.15 = f32[128,1,896]{2,1,0:T(1,128)S(1)} all-to-all(f32[128,1,896]{2,1,0:T(1,128)S(1)} %bitcast.23), channel_id=1, replica_groups=mesh['gs'=128,'px'=2] {'gs'}, dimensions={0} | all-to-all | bytes 917504 | tf_op jit(solution)/shard_map/all_to_all | solution.py:488
  79.1 2.4 %collective-permute-start.2 = (f32[896,128]{1,0:T(8,128)S(1)}, f32[896,128]{1,0:T(8,128)S(1)}, u32[]{:S(2)}, u32[]{:S(2)}) collective-permute-start(f32[896,128]{1,0:T(8,128)S(1)} %bitcast.13), channel_id=1, source_target_pairs={{0,1},{1,0},{2,3},{3,2},{4,5},{5,4},{6,7},{7,6},{8,9},{9,8},{10,11... | collective-permute-start | bytes 1376264 | tf_op jit(solution)/shard_map/ppermute | solution.py:483
  81.5 0.7 shard_map.122
  82.2 6.2 %all-to-all-start.2 = ((f32[128,1,384]{2,1,0:T(1,128)}), f32[128,1,384]{2,1,0:T(1,128)S(1)}, u32[]{:S(2)}, u32[]{:S(2)}) async-start(f32[128,1,384]{2,1,0:T(1,128)} %bitcast.8), calls=%async_computation.2 | async-start | bytes 393216 | tf_op jit(solution)/shard_map/all_to_all | solution.py:488
  88.4 2.4 %shard_map.123 = (f32[2048,128]{1,0:T(8,128)}, f32[6,2048]{1,0:T(8,128)}) custom-call(s32[1]{0:T(128)} %bitcast.par_ref, s32[8,128]{1,0:T(8,128)S(1)} %get-tuple-element.46.idx_ref, f32[896,128]{1,0:T(8,128)S(1)} %bitcast.15, f32[896,128]{1,0:T(8,128)S(1)} %collective-permute-done.2.peer_ref), custom_call_target="tpu_custom_call" | custom-call | flops 4000000000 | bytes 13333333 | tf_op jit(solution)/shard_map/pallas_call | solution.py:468
  90.8 10.4 %all-to-all-done.2 = f32[128,1,384]{2,1,0:T(1,128)S(1)} async-done(((f32[128,1,384]{2,1,0:T(1,128)}), f32[128,1,384]{2,1,0:T(1,128)S(1)}, u32[]{:S(2)}, u32[]{:S(2)}) %all-to-all-start.2) | async-done | bytes 196640 | tf_op jit(solution)/shard_map/all_to_all | solution.py:488
  101.3 1.8 %collective-permute-start.3 = (f32[384,128]{1,0:T(8,128)S(1)}, f32[384,128]{1,0:T(8,128)S(1)}, u32[]{:S(2)}, u32[]{:S(2)}) collective-permute-start(f32[384,128]{1,0:T(8,128)S(1)} %bitcast.18), channel_id=1, source_target_pairs={{0,1},{1,0},{2,3},{3,2},{4,5},{5,4},{6,7},{7,6},{8,9},{9,8},{10,11... | collective-permute-start | bytes 589832 | tf_op jit(solution)/shard_map/ppermute | solution.py:483
  103.1 1.1 %collective-permute-done.3.peer_ref = f32[384,128]{1,0:T(8,128)S(1)} collective-permute-done((f32[384,128]{1,0:T(8,128)S(1)}, f32[384,128]{1,0:T(8,128)S(1)}, u32[]{:S(2)}, u32[]{:S(2)}) %collective-permute-start.3) | collective-permute-done | bytes 196640 | tf_op jit(solution)/shard_map/ppermute | solution.py:483
  104.1 0.8 shard_map.124
  (16 shorter events, 0.1 us)
Async XLA Ops:
  0.6 1.2 %copy-start.1 = (f32[2048,128]{1,0:T(8,128)S(1)}, f32[2048,128]{1,0:T(8,128)}, u32[]{:S(2)}) copy-start(f32[2048,128]{1,0:T(8,128)} %feat_ref.1) | copy-start | bytes 3145732
  1.9 0.8 copy-start.3
  2.7 0.7 copy-start.5
  3.4 18.3 %copy-start.2 = (f32[128,512]{1,0:T(8,128)S(1)}, f32[128,512]{1,0:T(8,128)}, u32[]{:S(2)}) copy-start(f32[128,512]{1,0:T(8,128)} %weight_ref) | copy-start | bytes 786436
  3.4 18.3 %copy-start.4 = (s32[8,512]{1,0:T(8,128)S(1)}, s32[8,512]{1,0:T(8,128)}, u32[]{:S(2)}) copy-start(s32[8,512]{1,0:T(8,128)} %lists_ref) | copy-start | bytes 49156
  5.3 31.1 %all-to-all-start = ((f32[128,1,640]{2,1,0:T(1,128)}), f32[128,1,640]{2,1,0:T(1,128)S(1)}, u32[]{:S(2)}, u32[]{:S(2)}) async-start(f32[128,1,640]{2,1,0:T(1,128)} %bitcast.2), calls=%async_computation | async-start | bytes 655360 | tf_op jit(solution)/shard_map/all_to_all | solution.py:488
  21.7 18.7 %copy-start = (f32[8,128,512]{2,1,0:T(8,128)S(1)}, f32[8,128,512]{2,1,0:T(8,128)}, u32[]{:S(2)}) copy-start(f32[8,128,512]{2,1,0:T(8,128)} %param.13) | copy-start | bytes 6291460
  21.7 18.7 %copy-start.6 = (f32[512]{0:T(512)S(1)}, f32[512]{0:T(512)}, u32[]{:S(2)}) copy-start(f32[512]{0:T(512)} %param.15) | copy-start | bytes 6148
  21.7 18.7 %copy-start.7 = (s32[8]{0:T(128)S(1)}, s32[8]{0:T(128)}, u32[]{:S(2)}) copy-start(s32[8]{0:T(128)} %ids_ref.1) | copy-start | bytes 100
  23.1 1.3 %copy-start.8 = (bf16[1024,1024]{1,0:T(8,128)(2,1)}, bf16[1024,1024]{1,0:T(8,128)(2,1)S(1)}, u32[]{:S(2)}) copy-start(bf16[1024,1024]{1,0:T(8,128)(2,1)S(1)} %get-tuple-element.40.mask_ref) | copy-start | bytes 6291460
  36.4 4.0 %collective-permute-start = (f32[640,128]{1,0:T(8,128)S(1)}, f32[640,128]{1,0:T(8,128)S(1)}, u32[]{:S(2)}, u32[]{:S(2)}) collective-permute-start(f32[640,128]{1,0:T(8,128)S(1)} %bitcast.16), channel_id=1, source_target_pairs={{0,1},{1,0},{2,3},{3,2},{4,5},{5,4},{6,7},{7,6},{8,9},{9,8},{10,11... | collective-permute-start | bytes 983048 | tf_op jit(solution)/shard_map/ppermute | solution.py:483
  40.4 1.6 %copy-start.9 = (bf16[1024,1024]{1,0:T(8,128)(2,1)S(1)}, bf16[1024,1024]{1,0:T(8,128)(2,1)}, u32[]{:S(2)}) copy-start(bf16[1024,1024]{1,0:T(8,128)(2,1)} %copy-done.8) | copy-start | bytes 6291460
  53.8 1.9 %collective-permute-start.1 = (f32[896,128]{1,0:T(8,128)S(1)}, f32[896,128]{1,0:T(8,128)S(1)}, u32[]{:S(2)}, u32[]{:S(2)}) collective-permute-start(f32[896,128]{1,0:T(8,128)S(1)} %get-tuple-element.45), channel_id=1, source_target_pairs={{0,1},{1,0},{2,3},{3,2},{4,5},{5,4},{6,7},{7,6},{8,9},{9,8},{10,11... | collective-permute-start | bytes 1376264 | tf_op jit(solution)/shard_map/ppermute | solution.py:483
  79.1 9.3 %collective-permute-start.2 = (f32[896,128]{1,0:T(8,128)S(1)}, f32[896,128]{1,0:T(8,128)S(1)}, u32[]{:S(2)}, u32[]{:S(2)}) collective-permute-start(f32[896,128]{1,0:T(8,128)S(1)} %bitcast.13), channel_id=1, source_target_pairs={{0,1},{1,0},{2,3},{3,2},{4,5},{5,4},{6,7},{7,6},{8,9},{9,8},{10,11... | collective-permute-start | bytes 1376264 | tf_op jit(solution)/shard_map/ppermute | solution.py:483
  82.2 19.0 %all-to-all-start.2 = ((f32[128,1,384]{2,1,0:T(1,128)}), f32[128,1,384]{2,1,0:T(1,128)S(1)}, u32[]{:S(2)}, u32[]{:S(2)}) async-start(f32[128,1,384]{2,1,0:T(1,128)} %bitcast.8), calls=%async_computation.2 | async-start | bytes 393216 | tf_op jit(solution)/shard_map/all_to_all | solution.py:488
  101.3 2.9 %collective-permute-start.3 = (f32[384,128]{1,0:T(8,128)S(1)}, f32[384,128]{1,0:T(8,128)S(1)}, u32[]{:S(2)}, u32[]{:S(2)}) collective-permute-start(f32[384,128]{1,0:T(8,128)S(1)} %bitcast.18), channel_id=1, source_target_pairs={{0,1},{1,0},{2,3},{3,2},{4,5},{5,4},{6,7},{7,6},{8,9},{9,8},{10,11... | collective-permute-start | bytes 589832 | tf_op jit(solution)/shard_map/ppermute | solution.py:483

commit v3 on v2

v3 whole, which is shorter than its diff:
```python
import functools

import jax
import jax.numpy as jnp
from jax import lax
from jax.experimental import pallas as pl
from jax.experimental.pallas import tpu as pltpu
from jax.sharding import PartitionSpec as P

F32 = jnp.float32
BF16 = jnp.bfloat16
L = 128
SWAP = [(0, 1), (1, 0)]
FWD = 5
RET = 7
GAT = 3
VMEM = pl.BlockSpec(memory_space=pltpu.VMEM)
SMEM = pl.BlockSpec(memory_space=pltpu.SMEM)
HBM = pl.BlockSpec(memory_space=pltpu.HBM)
PARAMS = pltpu.CompilerParams(vmem_limit_bytes=40 * 1024 * 1024)


def nn(lhs, rhs):
    return lax.dot_general(lhs, rhs, (((1,), (0,)), ((), ())), preferred_element_type=F32)


def nt(lhs, rhs):
    return lax.dot_general(lhs, rhs, (((1,), (1,)), ((), ())), preferred_element_type=F32)


def split2(value):
    high = value.astype(BF16)
    return high, (value - high.astype(F32)).astype(BF16)


def split3(value):
    high = value.astype(BF16)
    rest = value - high.astype(F32)
    mid = rest.astype(BF16)
    return high, mid, (rest - mid.astype(F32)).astype(BF16)


def ones_where(mask):
    return jnp.where(mask, 1.0, 0.0).astype(F32)


def column_of(rows):
    pad = jnp.zeros((L - rows.shape[0], L), F32)
    return jnp.concatenate([rows, pad], axis=0).T


def slot_rows(raw):
    slot = lax.broadcasted_iota(jnp.int32, (8, L), 1) & 7
    mine = slot == lax.broadcasted_iota(jnp.int32, (8, L), 0)
    spread = []
    for r in range(8):
        row = raw[r : r + 1, :]
        high = jnp.where(mine, row >> 4, 0).astype(F32)
        low = jnp.where(mine, row & 15, 0).astype(F32)
        spread.append(jnp.concatenate([high, low], axis=0).astype(BF16))
    source = lax.broadcasted_iota(jnp.int32, (8 * L, L), 0) >> 3
    owner = lax.broadcasted_iota(jnp.int32, (8 * L, L), 1)
    got = nn(jnp.concatenate(spread, axis=1), ones_where(source == owner).astype(BF16))
    return (got[:8] * 16.0 + got[8:]).astype(jnp.int32)


def pack_kernel(par_ref, send_hbm, feat_hbm, prm_hbm, out_ref, idx_ref, send_ref, feat_ref, prm_ref, sems):
    copies = [
        pltpu.make_async_copy(src, dst, sems.at[n])
        for n, (src, dst) in enumerate(
            ((send_hbm, send_ref), (feat_hbm, feat_ref), (prm_hbm, prm_ref))
        )
    ]
    for copy in copies:
        copy.start()
    gauss = feat_ref.shape[0]
    copies[0].wait()
    first = par_ref[0] == 0
    idx = slot_rows(send_ref[...])
    idx_ref[...] = idx
    rows = jnp.where(first, idx[0:4, :], idx[4:8, :])
    cols = column_of(rows.astype(F32))
    lane = lax.broadcasted_iota(jnp.int32, (L, gauss), 1).astype(F32)
    hots = [ones_where(cols[:, c : c + 1] == lane).astype(BF16) for c in range(4)]
    copies[2].wait()
    copies[1].wait()
    got = nn(
        jnp.concatenate(hots, axis=0), jnp.concatenate(split2(feat_ref[...]), axis=1)
    )
    groups = gauss // L
    pieces = [prm_ref[:, g * L : (g + 1) * L] for g in range(groups)]
    pad = jnp.zeros((2, L), F32)
    stacked = jnp.concatenate([x for piece in pieces for x in (piece, pad)], axis=0)
    stack3 = jnp.concatenate(split3(stacked), axis=0)
    low_iota = lax.broadcasted_iota(jnp.int32, (L, L), 0)
    packed = []
    for c in range(4):
        part = got[c * L : c * L + L]
        out_ref[pl.ds(c, L, stride=FWD), :] = part[:, :L] + part[:, L:]
        row = rows[c : c + 1, :]
        low = ones_where((row & (L - 1)) == low_iota).astype(BF16)
        part = nn(stack3, low)
        span = groups * 8
        part = part[:span] + part[span : 2 * span] + part[2 * span :]
        total = jnp.zeros((8, L), F32)
        for g in range(groups):
            total = total + jnp.where((row >> 7) == g, part[g * 8 : g * 8 + 8], 0.0)
        packed.append(total)
    out_ref[pl.ds(4, L, stride=FWD), :] = column_of(jnp.concatenate(packed, axis=0))


def key_kernel(par_ref, lists_ref, weight_ref, row_ref, high_ref, low_ref):
    high_ref[...], low_ref[...] = split2(weight_ref[...])
    shift = par_ref[0] * 4
    tiles, length = lists_ref.shape
    slot_iota = lax.broadcasted_iota(jnp.int32, (8, length), 0)
    holder_iota = lax.broadcasted_iota(jnp.int32, (L, length), 0)
    place = lax.broadcasted_iota(jnp.int32, (8, length), 1)
    place_high = (place >> 4).astype(F32)
    place_low = (place & 15).astype(F32)
    total = jnp.zeros((32, L), F32)
    for t in range(tiles):
        entry = lists_ref[t : t + 1, :]
        holder = ones_where((entry >> 3) == holder_iota).astype(BF16)
        slot = ones_where(((entry + shift) & 7) == slot_iota)
        left = jnp.concatenate(
            [slot * (t + 1.0), slot * place_high, slot * place_low, jnp.zeros((8, length), F32)],
            axis=0,
        ).astype(BF16)
        total = total + nt(left, holder)
    tile = total[0:8]
    key = jnp.where(tile > 0.5, (tile - 1.0) * length + total[8:16] * 16.0 + total[16:24], -1.0)
    row_ref[...] = key


class Pool:
    def __init__(self, length, par_ref, ids_ref, keyrow_ref, prm_ref, own_ref, peer_ref):
        self.length, self.prm_ref = length, prm_ref
        stripe = par_ref[0]
        self.key = keyrow_ref[...]
        live = self.key >= 0.0
        self.tile = jnp.floor(self.key * (1.0 / length))
        self.ox = jnp.zeros((8, L), F32)
        self.oy = jnp.zeros((8, L), F32)
        for t in range(8):
            ident = ids_ref[t]
            here = self.tile == float(t)
            self.ox = jnp.where(here, ((ident & 127) * 16).astype(F32) + 0.5, self.ox)
            self.oy = jnp.where(
                here, ((ident >> 7) * 16 + stripe * 8).astype(F32) + 0.5, self.oy
            )
        self.base = jnp.where(live, self.tile * length, 1.0e9)
        self.live = ones_where(live)
        self.kx = lax.broadcasted_iota(jnp.int32, (16, L), 0).astype(F32)
        self.ky = lax.broadcasted_iota(jnp.int32, (8, L), 0).astype(F32)
        for side, ref in ((0, own_ref), (1, peer_ref)):
            prm_ref[side * 32 : side * 32 + 32, :] = ref[pl.ds(4, L, stride=FWD), :].T[0:32]

    def geometry(self, b):
        prm = self.prm_ref[b * 8 : b * 8 + 8, :]
        dx = (self.kx + self.ox[b : b + 1, :]) - prm[0:1]
        dy = (self.ky + self.oy[b : b + 1, :]) - prm[1:2]
        return prm, dx, dy

    def alphas(self, b):
        prm, dx, dy = self.geometry(b)
        ax = prm[2:3] * dx * dx
        cy = prm[4:5] * dy * dy
        bx = prm[3:4] * dx
        for j in range(8):
            power = -0.5 * (ax + cy[j : j + 1]) - bx * dy[j : j + 1]
            ex = self.live[b : b + 1, :] * jnp.exp(power)
            yield slice(j * 16, j * 16 + 16), ex, prm[5:6] * ex

    def fill_mask(self, mask_ref):
        cols = column_of(self.key)
        for a in range(8):
            front = jnp.broadcast_to(cols[:, a : a + 1], (L, L))
            for b in range(8):
                hit = (front < self.key[b : b + 1, :]) & (front >= self.base[b : b + 1, :])
                mask_ref[a * L : a * L + L, b * L : b * L + L] = ones_where(hit).astype(BF16)

    def spread(self, b, weights, high_ref, low_ref):
        cols = slice(b * L, b * L + L)
        high, low = split2(weights)
        for t in range(8):
            here = ones_where(self.tile[b : b + 1, :] == float(t))
            here = jnp.broadcast_to(here, (L, L)).astype(BF16)
            high_ref[t * L : t * L + L, cols] = high * here
            low_ref[t * L : t * L + L, cols] = low * here


def fill_features(own_ref, peer_ref, feat_ref):
    for side, ref in ((0, own_ref), (1, peer_ref)):
        for c in range(4):
            at = (side * 4 + c) * L
            high, low = split2(ref[pl.ds(c, L, stride=FWD), :])
            feat_ref[at : at + L, 0:L] = high
            feat_ref[at : at + L, L : 2 * L] = low


def front_kernel(
    length,
    par_ref,
    ids_ref,
    own_ref,
    peer_ref,
    keyrow_ref,
    teacher_ref,
    whigh_ref,
    wlow_ref,
    bias_ref,
    keep_ref,
    give_ref,
    trans_ref,
    grad_ref,
    mask_ref,
    prm_ref,
    feat_ref,
    alpha_ref,
    lk_ref,
    wm_hi,
    wm_lo,
    rt_ref,
    resid_hi,
    resid_lo,
):
    pool = Pool(length, par_ref, ids_ref, keyrow_ref, prm_ref, own_ref, peer_ref)
    fill_features(own_ref, peer_ref, feat_ref)
    pool.fill_mask(mask_ref)
    for b in range(8):
        cols = slice(b * L, b * L + L)
        for spot, ex, alpha in pool.alphas(b):
            high, low = split2(jnp.log1p(-alpha))
            alpha_ref[spot, cols] = alpha
            lk_ref[spot, cols] = high
            lk_ref[L + spot.start : L + spot.stop, cols] = low

    for b in range(0, 8, 2):
        both = nn(lk_ref[...], mask_ref[:, b * L : b * L + 2 * L])
        trans = jnp.exp(both[:L] + both[L:])
        trans_ref[:, b * L : b * L + 2 * L] = trans
        for q in range(2):
            cols = slice((b + q) * L, (b + q) * L + L)
            weights = trans[:, q * L : q * L + L] * alpha_ref[:, cols]
            pool.spread(b + q, weights, wm_hi, wm_lo)

    w_hi, w_lo = whigh_ref[...], wlow_ref[...]
    w_pair = jnp.concatenate([w_hi, w_hi], axis=0)
    w_both = jnp.concatenate([w_hi, w_lo], axis=0)
    width = whigh_ref.shape[1]
    squares = jnp.zeros((1, width), F32)
    bias_sum = jnp.zeros((1, width), F32)
    step = 2 * L
    for r in range(4):
        rows = slice(r * step, r * step + step)
        both = nn(wm_hi[rows, :], feat_ref[...])
        rendered = both[:, :L] + both[:, L:] + nn(wm_lo[rows, :], feat_ref[:, 0:L])
        high, low = split2(rendered)
        rt_hi, rt_lo = split2(rendered.T)
        rt_ref[0:L, rows] = rt_hi
        rt_ref[L : 2 * L, rows] = rt_lo
        decoded = nn(jnp.concatenate([high, low], axis=1), w_pair) + nn(high, w_lo)
        resid = decoded + bias_ref[...] - teacher_ref[rows, :]
        squares = squares + jnp.sum(resid * resid, axis=0, keepdims=True)
        bias_sum = bias_sum + jnp.sum(resid, axis=0, keepdims=True)
        high, low = split2(resid)
        resid_hi[rows, :] = high
        resid_lo[rows, :] = low
        both = nt(high, w_both)
        grad_ref[rows, :] = both[:, :L] + both[:, L:] + nt(low, w_hi)

    both = nn(rt_ref[...], resid_hi[...])
    grad_w = both[:L] + both[L:] + nn(rt_ref[0:L, :], resid_lo[...])
    sq_row = jnp.broadcast_to(jnp.sum(squares, axis=1, keepdims=True), (1, L))
    first = par_ref[0] == 0
    half = width // 2
    for ref, left in ((keep_ref, first), (give_ref, jnp.logical_not(first))):
        piece = jnp.where(left, grad_w[:, :half], grad_w[:, half:])
        ref[pl.ds(0, L, stride=GAT), :] = piece[:, :L]
        ref[pl.ds(1, L, stride=GAT), :] = piece[:, L:]
        piece = jnp.where(left, bias_sum[:, :half], bias_sum[:, half:])
        rows = jnp.concatenate([piece[:, :L], piece[:, L:], sq_row], axis=0)
        ref[pl.ds(2, L, stride=GAT), :] = column_of(rows)


def back_kernel(
    length,
    par_ref,
    ids_ref,
    own_ref,
    peer_ref,
    keyrow_ref,
    trans_ref,
    grad_ref,
    keep_ref,
    give_ref,
    mask_ref,
    prm_ref,
    feat_ref,
    feat2_ref,
    ex_ref,
    alpha_ref,
    lk_ref,
    wm_hi,
    wm_lo,
    drt_ref,
    dw_ref,
):
    pool = Pool(length, par_ref, ids_ref, keyrow_ref, prm_ref, own_ref, peer_ref)
    fill_features(own_ref, peer_ref, feat_ref)
    feat2_ref[:, 0:L] = feat_ref[:, 0:L]
    feat2_ref[:, L : 2 * L] = feat_ref[:, 0:L]
    pool.fill_mask(mask_ref)
    for b in range(8):
        cols = slice(b * L, b * L + L)
        for spot, ex, alpha in pool.alphas(b):
            ex_ref[spot, cols] = ex
            alpha_ref[spot, cols] = alpha
        pool.spread(b, trans_ref[:, cols] * alpha_ref[:, cols], wm_hi, wm_lo)

    dw_ref[...] = jnp.zeros(dw_ref.shape, F32)
    step = 2 * L
    for r in range(4):
        rows = slice(r * step, r * step + step)
        grad = grad_ref[rows, :]
        high, low = split2(grad)
        pair = jnp.concatenate([high, low], axis=1)
        dt_hi, dt_lo = split2(grad.T)
        drt_ref[0:L, rows] = dt_hi
        drt_ref[L : 2 * L, rows] = dt_lo
        for b in range(0, 8, 2):
            entries = slice(b * L, b * L + step)
            part = nt(pair, feat2_ref[entries, :]) + nt(high, feat_ref[entries, L : 2 * L])
            for q in range(2):
                cols = slice((b + q) * L, (b + q) * L + L)
                tile = pool.tile[b + q : b + q + 1, :]
                got = part[:, q * L : q * L + L]
                kept = jnp.where(tile == float(2 * r), got[:L], dw_ref[:, cols])
                dw_ref[:, cols] = jnp.where(tile == float(2 * r + 1), got[L:], kept)

    for b in range(8):
        cols = slice(b * L, b * L + L)
        high, low = split2(dw_ref[:, cols] * (trans_ref[:, cols] * alpha_ref[:, cols]))
        lk_ref[0:L, cols] = high
        lk_ref[L : 2 * L, cols] = low

    def total(value):
        return jnp.sum(value, axis=0, keepdims=True)

    blocks = []
    for b in range(0, 8, 2):
        wide = slice(b * L, b * L + step)
        both = nt(lk_ref[...], mask_ref[wide, :])
        alpha = alpha_ref[:, wide]
        dalpha = dw_ref[:, wide] * trans_ref[:, wide] - (both[:L] + both[L:]) / (1.0 - alpha)
        dpower = dalpha * alpha
        dopac = total(dalpha * ex_ref[:, wide])
        for q in range(2):
            prm, dx, dy = pool.geometry(b + q)
            flat = jnp.zeros((16, L), F32)
            by_y = jnp.zeros((16, L), F32)
            by_yy = jnp.zeros((16, L), F32)
            for j in range(8):
                part = dpower[j * 16 : j * 16 + 16, q * L : q * L + L]
                scaled = part * dy[j : j + 1]
                flat = flat + part
                by_y = by_y + scaled
                by_yy = by_yy + scaled * dy[j : j + 1]
            sx = total(flat * dx)
            sxx = total(flat * dx * dx)
            sy = total(by_y)
            sxy = total(by_y * dx)
            syy = total(by_yy)
            blocks += [
                prm[2:3] * sx + prm[3:4] * sy,
                prm[4:5] * sy + prm[3:4] * sx,
                -0.5 * sxx,
                -sxy,
                -0.5 * syy,
                dopac[:, q * L : q * L + L],
                jnp.zeros((2, L), F32),
            ]

    for side, ref in ((0, keep_ref), (1, give_ref)):
        for c in range(0, 4, 2):
            wide = slice((side * 4 + c) * L, (side * 4 + c) * L + step)
            both = nn(drt_ref[...], wm_hi[:, wide])
            grad = both[:L] + both[L:] + nn(drt_ref[0:L, :], wm_lo[:, wide])
            ref[pl.ds(c, L, stride=FWD), :] = grad[:, :L].T
            ref[pl.ds(c + 1, L, stride=FWD), :] = grad[:, L:].T
        rows = jnp.concatenate(blocks[side * 28 : side * 28 + 28], axis=0)
        ref[pl.ds(4, L, stride=FWD), :] = column_of(rows)


def compose_kernel(share_ref, keep_ref, give_ref, out_ref):
    for c in range(5):
        spot = pl.ds(c, L, stride=FWD)
        rows = keep_ref[spot, :] + give_ref[spot, :]
        if c == 4:
            small = jnp.sum(share_ref[pl.ds(2, L, stride=GAT), :], axis=0, keepdims=True)
            rows = rows + pltpu.roll(jnp.broadcast_to(small, (L, L)), 32, 1)
        out_ref[pl.ds(c, L, stride=RET), :] = rows
    for c in range(2):
        total = jnp.sum(share_ref[pl.ds(c, L, stride=GAT), :], axis=0, keepdims=True)
        out_ref[pl.ds(5 + c, L, stride=RET), :] = jnp.broadcast_to(total, (L, L))


def final_kernel(
    pixels, par_ref, idx_ref, own_ref, peer_ref, feat_ref, prm_ref, weight_ref, bias_ref, loss_ref
):
    gauss = feat_ref.shape[0]
    groups = gauss // L
    first = par_ref[0] == 0
    idx = idx_ref[...]
    top, bottom = idx[0:4], idx[4:8]
    idx = jnp.concatenate(
        [jnp.where(first, top, bottom), jnp.where(first, bottom, top)], axis=0
    )
    grads = []
    hots = []
    sub = lax.broadcasted_iota(jnp.int32, (gauss, L), 0)
    low_iota = lax.broadcasted_iota(jnp.int32, (L, L), 0)
    params = jnp.zeros((2 * groups * 8, L), F32)
    for side, ref in ((0, own_ref), (1, peer_ref)):
        prm = ref[pl.ds(4, L, stride=RET), :].T
        for c in range(4):
            b = side * 4 + c
            row = idx[b : b + 1]
            high, low = split2(ref[pl.ds(c, L, stride=RET), :])
            grads.append(jnp.concatenate([high, low], axis=1))
            hots.append(ones_where(row == sub).astype(BF16))
            block = prm[c * 8 : c * 8 + 8]
            spread = jnp.concatenate(
                [jnp.where((row >> 7) == g, block, 0.0) for g in range(groups)], axis=0
            )
            both = jnp.concatenate(split2(spread), axis=0)
            hot = ones_where((row & (L - 1)) == low_iota).astype(BF16)
            params = params + nt(both, hot)
    params = params[: groups * 8] + params[groups * 8 :]
    for g in range(groups):
        prm_ref[:, g * L : g * L + L] = params[g * 8 : g * 8 + 6]
    onehot = jnp.concatenate(hots, axis=1)
    both = nn(onehot, jnp.concatenate(grads, axis=0))
    feat_ref[...] = both[:, :L] + both[:, L:]

    width = weight_ref.shape[1]
    half = width // 2
    scale = 1.0 / pixels
    for ref, left in ((own_ref, first), (peer_ref, jnp.logical_not(first))):
        small = ref[pl.ds(4, L, stride=RET), :].T
        wide = [ref[pl.ds(5 + c, L, stride=RET), :] * scale for c in range(2)]
        row = jnp.concatenate([small[32:33], small[33:34]], axis=1) * scale
        wide = jnp.concatenate(wide, axis=1)

        def store(at):
            weight_ref[:, at : at + half] = wide
            bias_ref[:, at : at + half] = row

        pl.when(left)(functools.partial(store, 0))
        pl.when(jnp.logical_not(left))(functools.partial(store, half))
    loss_ref[...] = small[34:35, :] * (scale / width)


def call(kernel, shapes, specs, scratch=(), flops=0):
    single = not isinstance(shapes, (list, tuple))
    count = 1 if single else len(shapes)
    cost = pl.CostEstimate(flops=flops, bytes_accessed=flops // 300, transcendentals=0)
    return pl.pallas_call(
        kernel,
        out_shape=shapes,
        in_specs=specs,
        out_specs=VMEM if single else [VMEM] * count,
        scratch_shapes=list(scratch),
        compiler_params=PARAMS,
        cost_estimate=cost,
    )


def f32(*shape):
    return jax.ShapeDtypeStruct(shape, F32)


def bf16(*shape):
    return jax.ShapeDtypeStruct(shape, BF16)


def pack(par, send, features, gauss_params):
    shapes = [f32(FWD * L, L), jax.ShapeDtypeStruct((8, L), jnp.int32)]
    inputs = (send, features, gauss_params)
    scratch = [pltpu.VMEM(x.shape, x.dtype) for x in inputs]
    scratch.append(pltpu.SemaphoreType.DMA((3,)))
    return call(pack_kernel, shapes, [SMEM, HBM, HBM, HBM], scratch, flops=2 * 10**9)(par, *inputs)


def keys(par, tile_lists, weight):
    shapes = [f32(8, L), bf16(*weight.shape), bf16(*weight.shape)]
    return call(key_kernel, shapes, [SMEM, VMEM, VMEM], flops=2 * 10**9)(par, tile_lists, weight)


def front(par, ids, own, peer, keyrow, teacher, whigh, wlow, bias, length):
    pixels, width = teacher.shape
    pool = 8 * L
    scratch = [
        pltpu.VMEM((pool, pool), BF16),
        pltpu.VMEM((64, L), F32),
        pltpu.VMEM((pool, 2 * L), BF16),
        pltpu.VMEM((L, pool), F32),
        pltpu.VMEM((2 * L, pool), BF16),
        pltpu.VMEM((pixels, pool), BF16),
        pltpu.VMEM((pixels, pool), BF16),
        pltpu.VMEM((2 * L, pixels), BF16),
        pltpu.VMEM((pixels, width), BF16),
        pltpu.VMEM((pixels, width), BF16),
    ]
    return call(
        functools.partial(front_kernel, float(length)),
        [f32(GAT * L, L), f32(GAT * L, L), f32(L, pool), f32(pixels, L)],
        [SMEM, SMEM] + [VMEM] * 7,
        scratch,
        flops=10**10,
    )(par, ids, own, peer, keyrow, teacher, whigh, wlow, bias)


def back(par, ids, own, peer, keyrow, trans, grad, length):
    pool = 8 * L
    pixels = grad.shape[0]
    scratch = [
        pltpu.VMEM((pool, pool), BF16),
        pltpu.VMEM((64, L), F32),
        pltpu.VMEM((pool, 2 * L), BF16),
        pltpu.VMEM((pool, 2 * L), BF16),
        pltpu.VMEM((L, pool), F32),
        pltpu.VMEM((L, pool), F32),
        pltpu.VMEM((2 * L, pool), BF16),
        pltpu.VMEM((pixels, pool), BF16),
        pltpu.VMEM((pixels, pool), BF16),
        pltpu.VMEM((2 * L, pixels), BF16),
        pltpu.VMEM((L, pool), F32),
    ]
    return call(
        functools.partial(back_kernel, float(length)),
        [f32(FWD * L, L), f32(FWD * L, L)],
        [SMEM, SMEM] + [VMEM] * 5,
        scratch,
        flops=8 * 10**9,
    )(par, ids, own, peer, keyrow, trans, grad)


def compose(share, keep, give):
    return call(compose_kernel, f32(RET * L, L), [VMEM] * 3, flops=10**9)(share, keep, give)


def final(par, idx, own, peer, gauss, width, pixels):
    return call(
        functools.partial(final_kernel, float(pixels)),
        [f32(gauss, L), f32(6, gauss), f32(L, width), f32(1, width), f32(1, L)],
        [SMEM, VMEM, VMEM, VMEM],
        flops=4 * 10**9,
    )(par, idx, own, peer)


def swap(value):
    return lax.ppermute(value, "px", SWAP)


def exchange(value, rows):
    sent = value.reshape(L, 1, rows * L)
    return lax.all_to_all(sent, "gs", split_axis=0, concat_axis=0, tiled=True).reshape(rows * L, L)


def per_device(
    features, gauss_params, send_index, tile_ids, tile_lists, teacher, decoder_weight, decoder_bias
):
    holders = lax.axis_size("gs")
    par = lax.axis_index("px").astype(jnp.int32).reshape(1)
    width = teacher.shape[2]
    sent, idx = pack(par, send_index.reshape(8, -1), features, gauss_params)
    sent, tile_lists, decoder_weight, teacher = lax.optimization_barrier(
        (sent, tile_lists, decoder_weight, teacher)
    )
    got = exchange(sent, FWD)
    prepared = keys(par, tile_lists, decoder_weight)
    got, (keyrow, whigh, wlow) = lax.optimization_barrier((got, prepared))
    peer = swap(got)
    length = tile_lists.shape[1]
    flat_teacher = teacher.reshape(-1, width)
    bias = decoder_bias.reshape(1, -1)
    keep, give, trans, grad = front(
        par, tile_ids, got, peer, keyrow, flat_teacher, whigh, wlow, bias, length
    )
    part, trans, grad = lax.optimization_barrier((keep + swap(give), trans, grad))
    share = exchange(part, GAT)
    keep, give = back(par, tile_ids, got, peer, keyrow, trans, grad, length)
    ret = exchange(compose(share, keep, swap(give)), RET)
    pixels = holders * tile_ids.shape[0] * 256
    grad_features, grad_params, grad_weight, grad_bias, loss = final(
        par, idx, ret, swap(ret), features.shape[0], width, pixels
    )
    return grad_features, grad_params, grad_weight, grad_bias.reshape(-1), loss[0, 0]


def solution(mesh):
    return jax.shard_map(
        per_device,
        mesh=mesh,
        in_specs=(
            P("gs", None),
            P(None, "gs"),
            P("gs"),
            P("gs"),
            P("gs", None),
            P("gs", "px", None),
            P(),
            P(),
        ),
        out_specs=(P("gs", None), P(None, "gs"), P(), P(), P()),
        check_vma=False,
    )
```

time: 105 us -> 101 us (0.962)
  Pallas kernels: 18.9 us -> 16.3 us
  blocking collectives: 23.3 us -> 25.7 us
  waiting for transfers between devices: 26.2 us -> 24.1 us
  local copies, waits for them, and re-layouts: 5.68 us -> 3.81 us
    all_to_all x2, waiting for transfers between devices: 22.4 us -> 19 us  [exchange(): lax.all_to_all(sent, 'gs', split_axis=0, concat_axis=0, tiled=True)]
    pallas_call x6, Pallas kernels: 18.9 us -> 16.3 us  [the longest x1 6.14 us: front(): call(functools.partial(front_kernel, float(length)), [f32(GAT * L, L), f3...]
    all_to_all x1, blocking collectives: 23.3 us -> 25.7 us  [exchange(): lax.all_to_all(sent, 'gs', split_axis=0, concat_axis=0, tiled=True)]
    unnamed x20, local copies, waits for them, and re-layouts: 5.68 us -> 3.81 us
    ppermute x4, waiting for transfers between devices: 3.77 us -> 5.03 us  [swap(): return lax.ppermute(value, 'px', SWAP)]
  transfers between devices with their start and end apart: 6 -> 6, of which waited for: 5 -> 6; matrix products, arithmetic and copies ran while one was open for 0% -> 0% of each run, Pallas kernels for 4% -> 5%
where the time goes in v3:
time: 101 us
  starting transfers between devices  29.2 us (29%)
  blocking collectives  25.7 us (25%)
  waiting for transfers between devices  24.1 us (24%)
  Pallas kernels  16.3 us (16%)
  local copies, waits for them, and re-layouts  3.81 us (4%)
    all_to_all x1, blocking collectives, exchange(): lax.all_to_all(sent, 'gs', split_axis=0, concat_axis=0, tiled=True)  25.7 us
    all_to_all x2, starting transfers between devices, exchange(): lax.all_to_all(sent, 'gs', split_axis=0, concat_axis=0, tiled=True)  22.7 us
    all_to_all x2, waiting for transfers between devices, exchange(): lax.all_to_all(sent, 'gs', split_axis=0, concat_axis=0, tiled=True)  19 us
    ppermute x4, starting transfers between devices, swap(): return lax.ppermute(value, 'px', SWAP)  6.45 us
    pallas_call x1, Pallas kernels, front(): call(functools.partial(front_kernel, float(length)), [f32(GAT * L, L), f3...  6.14 us
    ppermute x4, waiting for transfers between devices, swap(): return lax.ppermute(value, 'px', SWAP)  5.03 us
    pallas_call x1, Pallas kernels, back(): call(functools.partial(back_kernel, float(length)), [f32(FWD * L, L), f32...  4.71 us
    unnamed x20, local copies, waits for them, and re-layouts  3.81 us
  transfers between devices with their start and end apart: 6, of which 6 were waited for; matrix products, arithmetic and copies ran while one was open for 0% of the time, Pallas kernels for 5%

profile of v3, /device:TPU:1, one launch (start us, length us, event | category | flops | bytes accessed | tf_op | source)
XLA Modules:
  0.0 100.5 jit_solution(15781681904304138260)
XLA Ops:
  0.6 1.2 %copy-done.1 = f32[2048,128]{1,0:T(8,128)S(1)} copy-done((f32[2048,128]{1,0:T(8,128)S(1)}, f32[2048,128]{1,0:T(8,128)}, u32[]{:S(2)}) %copy-start.1) | copy-done | bytes 1048600
  1.9 0.8 copy-done.3
  2.7 0.7 copy-done.5
  3.4 2.3 %shard_map.119 = (f32[640,128]{1,0:T(8,128)}, s32[8,128]{1,0:T(8,128)S(1)}) custom-call(s32[1]{0:T(128)} %bitcast.par_ref, s32[8,128]{1,0:T(8,128)S(1)} %bitcast.21, f32[2048,128]{1,0:T(8,128)S(1)} %copy-done.1, f32[6,2048]{1,0:T(8,128)S(1)} %copy-done.3), custom_call_target="tpu_custom_call" | custom-call | flops 2000000000 | bytes 6666666 | tf_op jit(solution)/shard_map/pallas_call | solution.py:493
  5.7 16.3 %all-to-all-start = ((f32[128,1,640]{2,1,0:T(1,128)}), f32[128,1,640]{2,1,0:T(1,128)S(1)}, u32[]{:S(2)}, u32[]{:S(2)}) async-start(f32[128,1,640]{2,1,0:T(1,128)} %bitcast.2), calls=%async_computation | async-start | bytes 655360 | tf_op jit(solution)/shard_map/all_to_all | solution.py:569
  22.1 0.5 shard_map.120
  22.6 14.1 %all-to-all-done = f32[128,1,640]{2,1,0:T(1,128)S(1)} async-done(((f32[128,1,640]{2,1,0:T(1,128)}), f32[128,1,640]{2,1,0:T(1,128)S(1)}, u32[]{:S(2)}, u32[]{:S(2)}) %all-to-all-start) | async-done | bytes 327712 | tf_op jit(solution)/shard_map/all_to_all | solution.py:569
  36.7 2.8 %collective-permute-start = (f32[640,128]{1,0:T(8,128)S(1)}, f32[640,128]{1,0:T(8,128)S(1)}, u32[]{:S(2)}, u32[]{:S(2)}) collective-permute-start(f32[640,128]{1,0:T(8,128)S(1)} %bitcast.16), channel_id=1, source_target_pairs={{0,1},{1,0},{2,3},{3,2},{4,5},{5,4},{6,7},{7,6},{8,9},{9,8},{10,11... | collective-permute-start | bytes 983048 | tf_op jit(solution)/shard_map/ppermute | solution.py:564
  39.5 1.3 %collective-permute-done.peer_ref = f32[640,128]{1,0:T(8,128)S(1)} collective-permute-done((f32[640,128]{1,0:T(8,128)S(1)}, f32[640,128]{1,0:T(8,128)S(1)}, u32[]{:S(2)}, u32[]{:S(2)}) %collective-permute-start) | collective-permute-done | bytes 327712 | tf_op jit(solution)/shard_map/ppermute | solution.py:564
  40.8 6.1 %shard_map.121 = (f32[384,128]{1,0:T(8,128)S(1)}, f32[384,128]{1,0:T(8,128)S(1)}, f32[128,1024]{1,0:T(8,128)S(1)}, f32[1024,128]{1,0:T(8,128)S(1)}) custom-call(s32[1]{0:T(128)} %bitcast.par_ref, s32[8]{0:T(128)S(1)} %copy-done.7, f32[640,128]{1,0:T(8,128)S(1)} %bitcast.17, f32[640,128]{1,0:T(8,128)S(1)} %collective-permute-done.peer_ref, ...), custom_call_target="tpu_custom_call" | custom-call | flops 10000000000 | bytes 33333332 | tf_op jit(solution)/shard_map/pallas_call | solution.py:516
  46.9 0.5 collective-permute-start.1
  47.4 1.1 %collective-permute-done.1 = f32[384,128]{1,0:T(8,128)S(1)} collective-permute-done((f32[384,128]{1,0:T(8,128)S(1)}, f32[384,128]{1,0:T(8,128)S(1)}, u32[]{:S(2)}, u32[]{:S(2)}) %collective-permute-start.1) | collective-permute-done | bytes 196640 | tf_op jit(solution)/shard_map/ppermute | solution.py:564
  48.5 0.7 add.3
  49.2 6.4 %all-to-all-start.1 = ((f32[128,1,384]{2,1,0:T(1,128)}), f32[128,1,384]{2,1,0:T(1,128)S(1)}, u32[]{:S(2)}, u32[]{:S(2)}) async-start(f32[128,1,384]{2,1,0:T(1,128)} %bitcast.6), calls=%async_computation.1 | async-start | bytes 393216 | tf_op jit(solution)/shard_map/all_to_all | solution.py:569
  55.6 1.0 %copy-done.9 = f32[1024,128]{1,0:T(8,128)S(1)} copy-done((f32[1024,128]{1,0:T(8,128)S(1)}, f32[1024,128]{1,0:T(8,128)}, u32[]{:S(2)}) %copy-start.9) | copy-done | bytes 524312
  56.6 4.7 %shard_map.122 = (f32[640,128]{1,0:T(8,128)S(1)}, f32[640,128]{1,0:T(8,128)S(1)}) custom-call(s32[1]{0:T(128)} %bitcast.par_ref, s32[8]{0:T(128)S(1)} %copy-done.7, f32[640,128]{1,0:T(8,128)S(1)} %bitcast.18, f32[640,128]{1,0:T(8,128)S(1)} %collective-permute-done.peer_ref, f32[8,128]{1,0:T(8,128)S(1)} %get-tuple-element.41.keyrow_ref, ...), custom_call_target="tpu_custom_call" | custom-call | flops 8000000000 | bytes 26666666 | tf_op jit(solution)/shard_map/pallas_call | solution.py:541
  61.3 0.5 collective-permute-start.2
  61.8 1.3 %collective-permute-done.2.give_ref = f32[640,128]{1,0:T(8,128)S(1)} collective-permute-done((f32[640,128]{1,0:T(8,128)S(1)}, f32[640,128]{1,0:T(8,128)S(1)}, u32[]{:S(2)}, u32[]{:S(2)}) %collective-permute-start.2) | collective-permute-done | bytes 327712 | tf_op jit(solution)/shard_map/ppermute | solution.py:564
  63.0 4.9 %all-to-all-done.1 = f32[128,1,384]{2,1,0:T(1,128)S(1)} async-done(((f32[128,1,384]{2,1,0:T(1,128)}), f32[128,1,384]{2,1,0:T(1,128)S(1)}, u32[]{:S(2)}, u32[]{:S(2)}) %all-to-all-start.1) | async-done | bytes 196640 | tf_op jit(solution)/shard_map/all_to_all | solution.py:569
  67.9 0.1 shard_map.123
  68.0 25.7 %all_to_all.15 = f32[128,1,896]{2,1,0:T(1,128)S(1)} all-to-all(f32[128,1,896]{2,1,0:T(1,128)S(1)} %bitcast.15), channel_id=1, replica_groups=mesh['gs'=128,'px'=2] {'gs'}, dimensions={0} | all-to-all | bytes 917504 | tf_op jit(solution)/shard_map/all_to_all | solution.py:569
  93.7 2.7 %collective-permute-start.3 = (f32[896,128]{1,0:T(8,128)S(1)}, f32[896,128]{1,0:T(8,128)S(1)}, u32[]{:S(2)}, u32[]{:S(2)}) collective-permute-start(f32[896,128]{1,0:T(8,128)S(1)} %bitcast.13), channel_id=1, source_target_pairs={{0,1},{1,0},{2,3},{3,2},{4,5},{5,4},{6,7},{7,6},{8,9},{9,8},{10,11... | collective-permute-start | bytes 1376264 | tf_op jit(solution)/shard_map/ppermute | solution.py:564
  96.5 1.4 %collective-permute-done.3.peer_ref = f32[896,128]{1,0:T(8,128)S(1)} collective-permute-done((f32[896,128]{1,0:T(8,128)S(1)}, f32[896,128]{1,0:T(8,128)S(1)}, u32[]{:S(2)}, u32[]{:S(2)}) %collective-permute-start.3) | collective-permute-done | bytes 458784 | tf_op jit(solution)/shard_map/ppermute | solution.py:564
  97.9 2.6 %shard_map.124 = (f32[2048,128]{1,0:T(8,128)}, f32[6,2048]{1,0:T(8,128)}, f32[128,512]{1,0:T(8,128)}, f32[1,512]{1,0:T(1,128)}, f32[1,128]{1,0:T(1,128)}) custom-call(s32[1]{0:T(128)} %bitcast.par_ref, s32[8,128]{1,0:T(8,128)S(1)} %get-tuple-element.32.idx_ref, f32[896,128]{1,0:T(8,128)S(1)} %bitcast.14, f32[896,128]{1,0:T(8,128)S(1)} %collective-permute-done.3.peer_ref), custom_call_target="tpu_custom_call" | custom-call | flops 4000000000 | bytes 13333333 | tf_op jit(solution)/shard_map/pallas_call | solution.py:555
  (16 shorter events, 0.0 us)
Async XLA Ops:
  0.6 1.2 %copy-start.1 = (f32[2048,128]{1,0:T(8,128)S(1)}, f32[2048,128]{1,0:T(8,128)}, u32[]{:S(2)}) copy-start(f32[2048,128]{1,0:T(8,128)} %feat_hbm.1) | copy-start | bytes 3145732
  1.9 0.8 copy-start.3
  2.7 0.7 copy-start.5
  3.4 18.6 %copy-start.2 = (f32[128,512]{1,0:T(8,128)S(1)}, f32[128,512]{1,0:T(8,128)}, u32[]{:S(2)}) copy-start(f32[128,512]{1,0:T(8,128)} %weight_ref) | copy-start | bytes 786436
  3.4 18.6 %copy-start.4 = (s32[8,512]{1,0:T(8,128)S(1)}, s32[8,512]{1,0:T(8,128)}, u32[]{:S(2)}) copy-start(s32[8,512]{1,0:T(8,128)} %lists_ref) | copy-start | bytes 49156
  5.7 31.1 %all-to-all-start = ((f32[128,1,640]{2,1,0:T(1,128)}), f32[128,1,640]{2,1,0:T(1,128)S(1)}, u32[]{:S(2)}, u32[]{:S(2)}) async-start(f32[128,1,640]{2,1,0:T(1,128)} %bitcast.2), calls=%async_computation | async-start | bytes 655360 | tf_op jit(solution)/shard_map/all_to_all | solution.py:569
  22.0 18.7 %copy-start = (f32[8,128,512]{2,1,0:T(8,128)S(1)}, f32[8,128,512]{2,1,0:T(8,128)}, u32[]{:S(2)}) copy-start(f32[8,128,512]{2,1,0:T(8,128)} %param.13) | copy-start | bytes 6291460
  22.0 18.7 %copy-start.6 = (f32[512]{0:T(512)S(1)}, f32[512]{0:T(512)}, u32[]{:S(2)}) copy-start(f32[512]{0:T(512)} %param.15) | copy-start | bytes 6148
  22.1 18.7 %copy-start.7 = (s32[8]{0:T(128)S(1)}, s32[8]{0:T(128)}, u32[]{:S(2)}) copy-start(s32[8]{0:T(128)} %ids_ref.3) | copy-start | bytes 100
  36.7 4.0 %collective-permute-start = (f32[640,128]{1,0:T(8,128)S(1)}, f32[640,128]{1,0:T(8,128)S(1)}, u32[]{:S(2)}, u32[]{:S(2)}) collective-permute-start(f32[640,128]{1,0:T(8,128)S(1)} %bitcast.16), channel_id=1, source_target_pairs={{0,1},{1,0},{2,3},{3,2},{4,5},{5,4},{6,7},{7,6},{8,9},{9,8},{10,11... | collective-permute-start | bytes 983048 | tf_op jit(solution)/shard_map/ppermute | solution.py:564
  46.9 2.3 %copy-start.8 = (f32[1024,128]{1,0:T(8,128)}, f32[1024,128]{1,0:T(8,128)S(1)}, u32[]{:S(2)}) copy-start(f32[1024,128]{1,0:T(8,128)S(1)} %get-tuple-element.51.grad_ref) | copy-start | bytes 1572868
  46.9 1.5 %collective-permute-start.1 = (f32[384,128]{1,0:T(8,128)S(1)}, f32[384,128]{1,0:T(8,128)S(1)}, u32[]{:S(2)}, u32[]{:S(2)}) collective-permute-start(f32[384,128]{1,0:T(8,128)S(1)} %get-tuple-element.46), channel_id=1, source_target_pairs={{0,1},{1,0},{2,3},{3,2},{4,5},{5,4},{6,7},{7,6},{8,9},{9,8},{10,11... | collective-permute-start | bytes 589832 | tf_op jit(solution)/shard_map/ppermute | solution.py:564
  49.2 18.7 %all-to-all-start.1 = ((f32[128,1,384]{2,1,0:T(1,128)}), f32[128,1,384]{2,1,0:T(1,128)S(1)}, u32[]{:S(2)}, u32[]{:S(2)}) async-start(f32[128,1,384]{2,1,0:T(1,128)} %bitcast.6), calls=%async_computation.1 | async-start | bytes 393216 | tf_op jit(solution)/shard_map/all_to_all | solution.py:569
  55.5 1.0 %copy-start.9 = (f32[1024,128]{1,0:T(8,128)S(1)}, f32[1024,128]{1,0:T(8,128)}, u32[]{:S(2)}) copy-start(f32[1024,128]{1,0:T(8,128)} %copy-done.8) | copy-start | bytes 1572868
  61.3 1.7 %collective-permute-start.2 = (f32[640,128]{1,0:T(8,128)S(1)}, f32[640,128]{1,0:T(8,128)S(1)}, u32[]{:S(2)}, u32[]{:S(2)}) collective-permute-start(f32[640,128]{1,0:T(8,128)S(1)} %get-tuple-element.53), channel_id=1, source_target_pairs={{0,1},{1,0},{2,3},{3,2},{4,5},{5,4},{6,7},{7,6},{8,9},{9,8},{10,11... | collective-permute-start | bytes 983048 | tf_op jit(solution)/shard_map/ppermute | solution.py:564
  93.7 4.2 %collective-permute-start.3 = (f32[896,128]{1,0:T(8,128)S(1)}, f32[896,128]{1,0:T(8,128)S(1)}, u32[]{:S(2)}, u32[]{:S(2)}) collective-permute-start(f32[896,128]{1,0:T(8,128)S(1)} %bitcast.13), channel_id=1, source_target_pairs={{0,1},{1,0},{2,3},{3,2},{4,5},{5,4},{6,7},{7,6},{8,9},{9,8},{10,11... | collective-permute-start | bytes 1376264 | tf_op jit(solution)/shard_map/ppermute | solution.py:564

commit v4 on v3

--- a/solution.py
+++ b/solution.py
@@ -17,7 +17,6 @@
 VMEM = pl.BlockSpec(memory_space=pltpu.VMEM)
 SMEM = pl.BlockSpec(memory_space=pltpu.SMEM)
 HBM = pl.BlockSpec(memory_space=pltpu.HBM)
-PARAMS = pltpu.CompilerParams(vmem_limit_bytes=40 * 1024 * 1024)
 
 
 def nn(lhs, rhs):
@@ -462,7 +461,7 @@
     loss_ref[...] = small[34:35, :] * (scale / width)
 
 
-def call(kernel, shapes, specs, scratch=(), flops=0):
+def call(kernel, shapes, specs, scratch=(), flops=0, limit=40):
     single = not isinstance(shapes, (list, tuple))
     count = 1 if single else len(shapes)
     cost = pl.CostEstimate(flops=flops, bytes_accessed=flops // 300, transcendentals=0)
@@ -472,7 +471,7 @@
         in_specs=specs,
         out_specs=VMEM if single else [VMEM] * count,
         scratch_shapes=list(scratch),
-        compiler_params=PARAMS,
+        compiler_params=pltpu.CompilerParams(vmem_limit_bytes=limit * 1024 * 1024),
         cost_estimate=cost,
     )
 
@@ -490,7 +489,7 @@
     inputs = (send, features, gauss_params)
     scratch = [pltpu.VMEM(x.shape, x.dtype) for x in inputs]
     scratch.append(pltpu.SemaphoreType.DMA((3,)))
-    return call(pack_kernel, shapes, [SMEM, HBM, HBM, HBM], scratch, flops=2 * 10**9)(par, *inputs)
+    return call(pack_kernel, shapes, [SMEM, HBM, HBM, HBM], scratch, flops=2 * 10**9, limit=62)(par, *inputs)
 
 
 def keys(par, tile_lists, weight):

time: 101 us -> 98.8 us (0.978)
  local copies, waits for them, and re-layouts: 3.81 us -> 1.07 us
    unnamed x20 -> x16, local copies, waits for them, and re-layouts: 3.81 us -> 1.07 us
where the time goes in v4:
time: 98.8 us; the launch traced here: 98.4 us
  starting transfers between devices  29.2 us (30%)
  blocking collectives  25.7 us (26%)
  waiting for transfers between devices  24.1 us (24%)
  Pallas kernels  17 us (17%)
  local copies, waits for them, and re-layouts  1.07 us (1%)
    all_to_all x1, blocking collectives, exchange(): lax.all_to_all(sent, 'gs', split_axis=0, concat_axis=0, tiled=True)  25.7 us
    all_to_all x2, starting transfers between devices, exchange(): lax.all_to_all(sent, 'gs', split_axis=0, concat_axis=0, tiled=True)  22.7 us
    all_to_all x2, waiting for transfers between devices, exchange(): lax.all_to_all(sent, 'gs', split_axis=0, concat_axis=0, tiled=True)  19 us
    ppermute x4, starting transfers between devices, swap(): return lax.ppermute(value, 'px', SWAP)  6.45 us
    pallas_call x1, Pallas kernels, front(): call(functools.partial(front_kernel, float(length)), [f32(GAT * L, L), f3...  6.13 us
    ppermute x4, waiting for transfers between devices, swap(): return lax.ppermute(value, 'px', SWAP)  5.03 us
    pallas_call x1, Pallas kernels, back(): call(functools.partial(back_kernel, float(length)), [f32(FWD * L, L), f32...  4.71 us
    pallas_call x1, Pallas kernels, pack(): call(pack_kernel, shapes, [SMEM, HBM, HBM, HBM], scratch, flops=2 * 10 **...  2.95 us
  transfers between devices with their start and end apart: 6, of which 6 were waited for; matrix products, arithmetic and copies ran while one was open for 0% of the time, Pallas kernels for 5%

profile of v4, /device:TPU:1, one launch (start us, length us, event | category | flops | bytes accessed | tf_op | source)
XLA Modules:
  0.0 98.4 jit_solution(3399555195474298009)
XLA Ops:
  0.7 2.9 %shard_map.119 = (f32[640,128]{1,0:T(8,128)}, s32[8,128]{1,0:T(8,128)}) custom-call(s32[1]{0:T(128)} %bitcast.par_ref, s32[8,128]{1,0:T(8,128)} %bitcast.23, f32[2048,128]{1,0:T(8,128)} %feat_hbm.1, f32[6,2048]{1,0:T(8,128)} %prm_hbm.1), custom_call_target="tpu_custom_call" | custom-call | flops 2000000000 | bytes 6666666 | tf_op jit(solution)/shard_map/pallas_call | solution.py:492
  3.6 16.3 %all-to-all-start = ((f32[128,1,640]{2,1,0:T(1,128)}), f32[128,1,640]{2,1,0:T(1,128)S(1)}, u32[]{:S(2)}, u32[]{:S(2)}) async-start(f32[128,1,640]{2,1,0:T(1,128)} %bitcast.22), calls=%async_computation | async-start | bytes 655360 | tf_op jit(solution)/shard_map/all_to_all | solution.py:568
  20.0 0.0 copy-start
  20.0 0.0 copy-start.3
  20.0 0.0 copy-start.4
  20.0 0.5 shard_map.120
  20.5 14.1 %all-to-all-done = f32[128,1,640]{2,1,0:T(1,128)S(1)} async-done(((f32[128,1,640]{2,1,0:T(1,128)}), f32[128,1,640]{2,1,0:T(1,128)S(1)}, u32[]{:S(2)}, u32[]{:S(2)}) %all-to-all-start) | async-done | bytes 327712 | tf_op jit(solution)/shard_map/all_to_all | solution.py:568
  34.7 2.8 %collective-permute-start = (f32[640,128]{1,0:T(8,128)S(1)}, f32[640,128]{1,0:T(8,128)S(1)}, u32[]{:S(2)}, u32[]{:S(2)}) collective-permute-start(f32[640,128]{1,0:T(8,128)S(1)} %bitcast.16), channel_id=1, source_target_pairs={{0,1},{1,0},{2,3},{3,2},{4,5},{5,4},{6,7},{7,6},{8,9},{9,8},{10,11... | collective-permute-start | bytes 983048 | tf_op jit(solution)/shard_map/ppermute | solution.py:563
  37.5 1.3 %collective-permute-done.peer_ref = f32[640,128]{1,0:T(8,128)S(1)} collective-permute-done((f32[640,128]{1,0:T(8,128)S(1)}, f32[640,128]{1,0:T(8,128)S(1)}, u32[]{:S(2)}, u32[]{:S(2)}) %collective-permute-start) | collective-permute-done | bytes 327712 | tf_op jit(solution)/shard_map/ppermute | solution.py:563
  38.7 6.1 %shard_map.121 = (f32[384,128]{1,0:T(8,128)S(1)}, f32[384,128]{1,0:T(8,128)S(1)}, f32[128,1024]{1,0:T(8,128)S(1)}, f32[1024,128]{1,0:T(8,128)S(1)}) custom-call(s32[1]{0:T(128)} %bitcast.par_ref, s32[8]{0:T(128)S(1)} %copy-done.4, f32[640,128]{1,0:T(8,128)S(1)} %bitcast.17, f32[640,128]{1,0:T(8,128)S(1)} %collective-permute-done.peer_ref, ...), custom_call_target="tpu_custom_call" | custom-call | flops 10000000000 | bytes 33333332 | tf_op jit(solution)/shard_map/pallas_call | solution.py:515
  44.9 0.5 collective-permute-start.1
  45.3 1.1 %collective-permute-done.1 = f32[384,128]{1,0:T(8,128)S(1)} collective-permute-done((f32[384,128]{1,0:T(8,128)S(1)}, f32[384,128]{1,0:T(8,128)S(1)}, u32[]{:S(2)}, u32[]{:S(2)}) %collective-permute-start.1) | collective-permute-done | bytes 196640 | tf_op jit(solution)/shard_map/ppermute | solution.py:563
  46.4 0.7 add.3
  47.1 6.4 %all-to-all-start.1 = ((f32[128,1,384]{2,1,0:T(1,128)}), f32[128,1,384]{2,1,0:T(1,128)S(1)}, u32[]{:S(2)}, u32[]{:S(2)}) async-start(f32[128,1,384]{2,1,0:T(1,128)} %bitcast.6), calls=%async_computation.1 | async-start | bytes 393216 | tf_op jit(solution)/shard_map/all_to_all | solution.py:568
  53.5 1.0 %copy-done.6 = f32[1024,128]{1,0:T(8,128)S(1)} copy-done((f32[1024,128]{1,0:T(8,128)S(1)}, f32[1024,128]{1,0:T(8,128)}, u32[]{:S(2)}) %copy-start.6) | copy-done | bytes 524312
  54.5 4.7 %shard_map.122 = (f32[640,128]{1,0:T(8,128)S(1)}, f32[640,128]{1,0:T(8,128)S(1)}) custom-call(s32[1]{0:T(128)} %bitcast.par_ref, s32[8]{0:T(128)S(1)} %copy-done.4, f32[640,128]{1,0:T(8,128)S(1)} %bitcast.18, f32[640,128]{1,0:T(8,128)S(1)} %collective-permute-done.peer_ref, f32[8,128]{1,0:T(8,128)S(1)} %get-tuple-element.41.keyrow_ref, ...), custom_call_target="tpu_custom_call" | custom-call | flops 8000000000 | bytes 26666666 | tf_op jit(solution)/shard_map/pallas_call | solution.py:540
  59.2 0.5 collective-permute-start.2
  59.7 1.3 %collective-permute-done.2.give_ref = f32[640,128]{1,0:T(8,128)S(1)} collective-permute-done((f32[640,128]{1,0:T(8,128)S(1)}, f32[640,128]{1,0:T(8,128)S(1)}, u32[]{:S(2)}, u32[]{:S(2)}) %collective-permute-start.2) | collective-permute-done | bytes 327712 | tf_op jit(solution)/shard_map/ppermute | solution.py:563
  61.0 4.9 %all-to-all-done.1 = f32[128,1,384]{2,1,0:T(1,128)S(1)} async-done(((f32[128,1,384]{2,1,0:T(1,128)}), f32[128,1,384]{2,1,0:T(1,128)S(1)}, u32[]{:S(2)}, u32[]{:S(2)}) %all-to-all-start.1) | async-done | bytes 196640 | tf_op jit(solution)/shard_map/all_to_all | solution.py:568
  65.8 0.1 shard_map.123
  66.0 25.7 %all_to_all.15 = f32[128,1,896]{2,1,0:T(1,128)S(1)} all-to-all(f32[128,1,896]{2,1,0:T(1,128)S(1)} %bitcast.15), channel_id=1, replica_groups=mesh['gs'=128,'px'=2] {'gs'}, dimensions={0} | all-to-all | bytes 917504 | tf_op jit(solution)/shard_map/all_to_all | solution.py:568
  91.7 2.7 %collective-permute-start.3 = (f32[896,128]{1,0:T(8,128)S(1)}, f32[896,128]{1,0:T(8,128)S(1)}, u32[]{:S(2)}, u32[]{:S(2)}) collective-permute-start(f32[896,128]{1,0:T(8,128)S(1)} %bitcast.13), channel_id=1, source_target_pairs={{0,1},{1,0},{2,3},{3,2},{4,5},{5,4},{6,7},{7,6},{8,9},{9,8},{10,11... | collective-permute-start | bytes 1376264 | tf_op jit(solution)/shard_map/ppermute | solution.py:563
  94.4 1.4 %collective-permute-done.3.peer_ref = f32[896,128]{1,0:T(8,128)S(1)} collective-permute-done((f32[896,128]{1,0:T(8,128)S(1)}, f32[896,128]{1,0:T(8,128)S(1)}, u32[]{:S(2)}, u32[]{:S(2)}) %collective-permute-start.3) | collective-permute-done | bytes 458784 | tf_op jit(solution)/shard_map/ppermute | solution.py:563
  95.8 2.6 %shard_map.124 = (f32[2048,128]{1,0:T(8,128)}, f32[6,2048]{1,0:T(8,128)}, f32[128,512]{1,0:T(8,128)}, f32[1,512]{1,0:T(1,128)}, f32[1,128]{1,0:T(1,128)}) custom-call(s32[1]{0:T(128)} %bitcast.par_ref, s32[8,128]{1,0:T(8,128)S(1)} %copy-done.7, f32[896,128]{1,0:T(8,128)S(1)} %bitcast.14, f32[896,128]{1,0:T(8,128)S(1)} %collective-permute-done.3.peer_ref), custom_call_target="tpu_custom_call" | custom-call | flops 4000000000 | bytes 13333333 | tf_op jit(solution)/shard_map/pallas_call | solution.py:554
  (12 shorter events, 0.0 us)
Async XLA Ops:
  0.6 19.3 %copy-start.1 = (f32[128,512]{1,0:T(8,128)S(1)}, f32[128,512]{1,0:T(8,128)}, u32[]{:S(2)}) copy-start(f32[128,512]{1,0:T(8,128)} %weight_ref) | copy-start | bytes 786436
  0.6 19.3 %copy-start.2 = (s32[8,512]{1,0:T(8,128)S(1)}, s32[8,512]{1,0:T(8,128)}, u32[]{:S(2)}) copy-start(s32[8,512]{1,0:T(8,128)} %lists_ref) | copy-start | bytes 49156
  3.6 31.1 %all-to-all-start = ((f32[128,1,640]{2,1,0:T(1,128)}), f32[128,1,640]{2,1,0:T(1,128)S(1)}, u32[]{:S(2)}, u32[]{:S(2)}) async-start(f32[128,1,640]{2,1,0:T(1,128)} %bitcast.22), calls=%async_computation | async-start | bytes 655360 | tf_op jit(solution)/shard_map/all_to_all | solution.py:568
  20.0 18.7 %copy-start = (f32[8,128,512]{2,1,0:T(8,128)S(1)}, f32[8,128,512]{2,1,0:T(8,128)}, u32[]{:S(2)}) copy-start(f32[8,128,512]{2,1,0:T(8,128)} %param.13) | copy-start | bytes 6291460
  20.0 18.7 %copy-start.3 = (f32[512]{0:T(512)S(1)}, f32[512]{0:T(512)}, u32[]{:S(2)}) copy-start(f32[512]{0:T(512)} %param.15) | copy-start | bytes 6148
  20.0 18.7 %copy-start.4 = (s32[8]{0:T(128)S(1)}, s32[8]{0:T(128)}, u32[]{:S(2)}) copy-start(s32[8]{0:T(128)} %ids_ref.3) | copy-start | bytes 100
  34.7 4.0 %collective-permute-start = (f32[640,128]{1,0:T(8,128)S(1)}, f32[640,128]{1,0:T(8,128)S(1)}, u32[]{:S(2)}, u32[]{:S(2)}) collective-permute-start(f32[640,128]{1,0:T(8,128)S(1)} %bitcast.16), channel_id=1, source_target_pairs={{0,1},{1,0},{2,3},{3,2},{4,5},{5,4},{6,7},{7,6},{8,9},{9,8},{10,11... | collective-permute-start | bytes 983048 | tf_op jit(solution)/shard_map/ppermute | solution.py:563
  44.9 2.3 %copy-start.5 = (f32[1024,128]{1,0:T(8,128)}, f32[1024,128]{1,0:T(8,128)S(1)}, u32[]{:S(2)}) copy-start(f32[1024,128]{1,0:T(8,128)S(1)} %get-tuple-element.51.grad_ref) | copy-start | bytes 1572868
  44.9 1.5 %collective-permute-start.1 = (f32[384,128]{1,0:T(8,128)S(1)}, f32[384,128]{1,0:T(8,128)S(1)}, u32[]{:S(2)}, u32[]{:S(2)}) collective-permute-start(f32[384,128]{1,0:T(8,128)S(1)} %get-tuple-element.46), channel_id=1, source_target_pairs={{0,1},{1,0},{2,3},{3,2},{4,5},{5,4},{6,7},{7,6},{8,9},{9,8},{10,11... | collective-permute-start | bytes 589832 | tf_op jit(solution)/shard_map/ppermute | solution.py:563
  47.1 18.7 %all-to-all-start.1 = ((f32[128,1,384]{2,1,0:T(1,128)}), f32[128,1,384]{2,1,0:T(1,128)S(1)}, u32[]{:S(2)}, u32[]{:S(2)}) async-start(f32[128,1,384]{2,1,0:T(1,128)} %bitcast.6), calls=%async_computation.1 | async-start | bytes 393216 | tf_op jit(solution)/shard_map/all_to_all | solution.py:568
  53.5 1.0 %copy-start.6 = (f32[1024,128]{1,0:T(8,128)S(1)}, f32[1024,128]{1,0:T(8,128)}, u32[]{:S(2)}) copy-start(f32[1024,128]{1,0:T(8,128)} %copy-done.5) | copy-start | bytes 1572868
  59.2 1.7 %collective-permute-start.2 = (f32[640,128]{1,0:T(8,128)S(1)}, f32[640,128]{1,0:T(8,128)S(1)}, u32[]{:S(2)}, u32[]{:S(2)}) collective-permute-start(f32[640,128]{1,0:T(8,128)S(1)} %get-tuple-element.53), channel_id=1, source_target_pairs={{0,1},{1,0},{2,3},{3,2},{4,5},{5,4},{6,7},{7,6},{8,9},{9,8},{10,11... | collective-permute-start | bytes 983048 | tf_op jit(solution)/shard_map/ppermute | solution.py:563
  65.8 30.0 %copy-start.7 = (s32[8,128]{1,0:T(8,128)S(1)}, s32[8,128]{1,0:T(8,128)}, u32[]{:S(2)}) copy-start(s32[8,128]{1,0:T(8,128)} %get-tuple-element.32.idx_ref) | copy-start | bytes 12292
  91.7 4.2 %collective-permute-start.3 = (f32[896,128]{1,0:T(8,128)S(1)}, f32[896,128]{1,0:T(8,128)S(1)}, u32[]{:S(2)}, u32[]{:S(2)}) collective-permute-start(f32[896,128]{1,0:T(8,128)S(1)} %bitcast.13), channel_id=1, source_target_pairs={{0,1},{1,0},{2,3},{3,2},{4,5},{5,4},{6,7},{7,6},{8,9},{9,8},{10,11... | collective-permute-start | bytes 1376264 | tf_op jit(solution)/shard_map/ppermute | solution.py:563

commit v5 on v4

--- a/solution.py
+++ b/solution.py
@@ -133,7 +133,7 @@
 
 
 class Pool:
-    def __init__(self, length, par_ref, ids_ref, keyrow_ref, prm_ref, own_ref, peer_ref):
+    def __init__(self, length, par_ref, ids_ref, keyrow_ref, prm_ref, sides):
         self.length, self.prm_ref = length, prm_ref
         stripe = par_ref[0]
         self.key = keyrow_ref[...]
@@ -152,7 +152,7 @@
         self.live = ones_where(live)
         self.kx = lax.broadcasted_iota(jnp.int32, (16, L), 0).astype(F32)
         self.ky = lax.broadcasted_iota(jnp.int32, (8, L), 0).astype(F32)
-        for side, ref in ((0, own_ref), (1, peer_ref)):
+        for side, ref in sides:
             prm_ref[side * 32 : side * 32 + 32, :] = ref[pl.ds(4, L, stride=FWD), :].T[0:32]
 
     def geometry(self, b):
@@ -198,6 +198,24 @@
             feat_ref[at : at + L, L : 2 * L] = low
 
 
+def fill_logs(pool, b, alpha_ref, lk_ref):
+    cols = slice(b * L, b * L + L)
+    for spot, ex, alpha in pool.alphas(b):
+        high, low = split2(jnp.log1p(-alpha))
+        alpha_ref[spot, cols] = alpha
+        lk_ref[spot, cols] = high
+        lk_ref[L + spot.start : L + spot.stop, cols] = low
+
+
+def ready_kernel(
+    length, par_ref, ids_ref, own_ref, keyrow_ref, mask_ref, alpha_ref, lk_ref, prm_ref
+):
+    pool = Pool(length, par_ref, ids_ref, keyrow_ref, prm_ref, ((0, own_ref),))
+    pool.fill_mask(mask_ref)
+    for b in range(4):
+        fill_logs(pool, b, alpha_ref, lk_ref)
+
+
 def front_kernel(
     length,
     par_ref,
@@ -205,6 +223,9 @@
     own_ref,
     peer_ref,
     keyrow_ref,
+    mask_ref,
+    half_alpha_ref,
+    half_lk_ref,
     teacher_ref,
     whigh_ref,
     wlow_ref,
@@ -213,7 +234,6 @@
     give_ref,
     trans_ref,
     grad_ref,
-    mask_ref,
     prm_ref,
     feat_ref,
     alpha_ref,
@@ -224,16 +244,15 @@
     resid_hi,
     resid_lo,
 ):
-    pool = Pool(length, par_ref, ids_ref, keyrow_ref, prm_ref, own_ref, peer_ref)
+    pool = Pool(
+        length, par_ref, ids_ref, keyrow_ref, prm_ref, ((0, own_ref), (1, peer_ref))
+    )
     fill_features(own_ref, peer_ref, feat_ref)
-    pool.fill_mask(mask_ref)
-    for b in range(8):
-        cols = slice(b * L, b * L + L)
-        for spot, ex, alpha in pool.alphas(b):
-            high, low = split2(jnp.log1p(-alpha))
-            alpha_ref[spot, cols] = alpha
-            lk_ref[spot, cols] = high
-            lk_ref[L + spot.start : L + spot.stop, cols] = low
+    half = 4 * L
+    alpha_ref[:, 0:half] = half_alpha_ref[...]
+    lk_ref[:, 0:half] = half_lk_ref[...]
+    for b in range(4, 8):
+        fill_logs(pool, b, alpha_ref, lk_ref)
 
     for b in range(0, 8, 2):
         both = nn(lk_ref[...], mask_ref[:, b * L : b * L + 2 * L])
@@ -306,7 +325,9 @@
     drt_ref,
     dw_ref,
 ):
-    pool = Pool(length, par_ref, ids_ref, keyrow_ref, prm_ref, own_ref, peer_ref)
+    pool = Pool(
+        length, par_ref, ids_ref, keyrow_ref, prm_ref, ((0, own_ref), (1, peer_ref))
+    )
     fill_features(own_ref, peer_ref, feat_ref)
     feat2_ref[:, 0:L] = feat_ref[:, 0:L]
     feat2_ref[:, L : 2 * L] = feat_ref[:, 0:L]
@@ -405,43 +426,68 @@
         out_ref[pl.ds(5 + c, L, stride=RET), :] = jnp.broadcast_to(total, (L, L))
 
 
-def final_kernel(
-    pixels, par_ref, idx_ref, own_ref, peer_ref, feat_ref, prm_ref, weight_ref, bias_ref, loss_ref
-):
+def place_kernel(par_ref, idx_ref, own_ref, feat_ref, prm_ref, hot_ref):
     gauss = feat_ref.shape[0]
-    groups = gauss // L
     first = par_ref[0] == 0
     idx = idx_ref[...]
     top, bottom = idx[0:4], idx[4:8]
-    idx = jnp.concatenate(
-        [jnp.where(first, top, bottom), jnp.where(first, bottom, top)], axis=0
-    )
-    grads = []
-    hots = []
     sub = lax.broadcasted_iota(jnp.int32, (gauss, L), 0)
+    other = jnp.where(first, bottom, top)
+    for c in range(4):
+        hot_ref[:, c * L : c * L + L] = ones_where(other[c : c + 1] == sub).astype(BF16)
+    mine = jnp.where(first, top, bottom)
+    hots = [ones_where(mine[c : c + 1] == sub).astype(BF16) for c in range(4)]
+    feat_ref[...] = place_features(own_ref, jnp.concatenate(hots, axis=1))
+    prm_ref[...] = place_params(own_ref, mine, gauss // L)
+
+
+def place_features(ref, onehot):
+    grads = [
+        jnp.concatenate(split2(ref[pl.ds(c, L, stride=RET), :]), axis=1) for c in range(4)
+    ]
+    both = nn(onehot, jnp.concatenate(grads, axis=0))
+    return both[:, :L] + both[:, L:]
+
+
+def place_params(ref, idx, groups):
     low_iota = lax.broadcasted_iota(jnp.int32, (L, L), 0)
+    prm = ref[pl.ds(4, L, stride=RET), :].T
     params = jnp.zeros((2 * groups * 8, L), F32)
-    for side, ref in ((0, own_ref), (1, peer_ref)):
-        prm = ref[pl.ds(4, L, stride=RET), :].T
-        for c in range(4):
-            b = side * 4 + c
-            row = idx[b : b + 1]
-            high, low = split2(ref[pl.ds(c, L, stride=RET), :])
-            grads.append(jnp.concatenate([high, low], axis=1))
-            hots.append(ones_where(row == sub).astype(BF16))
-            block = prm[c * 8 : c * 8 + 8]
-            spread = jnp.concatenate(
-                [jnp.where((row >> 7) == g, block, 0.0) for g in range(groups)], axis=0
-            )
-            both = jnp.concatenate(split2(spread), axis=0)
-            hot = ones_where((row & (L - 1)) == low_iota).astype(BF16)
-            params = params + nt(both, hot)
-    params = params[: groups * 8] + params[groups * 8 :]
+    for c in range(4):
+        row = idx[c : c + 1]
+        block = prm[c * 8 : c * 8 + 8]
+        spread = jnp.concatenate(
+            [jnp.where((row >> 7) == g, block, 0.0) for g in range(groups)], axis=0
+        )
+        both = jnp.concatenate(split2(spread), axis=0)
+        hot = ones_where((row & (L - 1)) == low_iota).astype(BF16)
+        params = params + nt(both, hot)
+    return params[: groups * 8] + params[groups * 8 :]
+
+
+def final_kernel(
+    pixels,
+    par_ref,
+    idx_ref,
+    own_ref,
+    peer_ref,
+    part_feat_ref,
+    part_prm_ref,
+    hot_ref,
+    feat_ref,
+    prm_ref,
+    weight_ref,
+    bias_ref,
+    loss_ref,
+):
+    first = par_ref[0] == 0
+    feat_ref[...] = part_feat_ref[...] + place_features(peer_ref, hot_ref[...])
+    groups = feat_ref.shape[0] // L
+    idx = idx_ref[...]
+    other = jnp.where(first, idx[4:8], idx[0:4])
+    params = part_prm_ref[...] + place_params(peer_ref, other, groups)
     for g in range(groups):
         prm_ref[:, g * L : g * L + L] = params[g * 8 : g * 8 + 6]
-    onehot = jnp.concatenate(hots, axis=1)
-    both = nn(onehot, jnp.concatenate(grads, axis=0))
-    feat_ref[...] = both[:, :L] + both[:, L:]
 
     width = weight_ref.shape[1]
     half = width // 2
@@ -497,11 +543,21 @@
     return call(key_kernel, shapes, [SMEM, VMEM, VMEM], flops=2 * 10**9)(par, tile_lists, weight)
 
 
-def front(par, ids, own, peer, keyrow, teacher, whigh, wlow, bias, length):
+def ready(par, ids, own, keyrow, length):
+    pool = 8 * L
+    return call(
+        functools.partial(ready_kernel, float(length)),
+        [bf16(pool, pool), f32(L, pool // 2), bf16(2 * L, pool // 2)],
+        [SMEM, SMEM, VMEM, VMEM],
+        [pltpu.VMEM((64, L), F32)],
+        flops=10**9,
+    )(par, ids, own, keyrow)
+
+
+def front(par, ids, own, peer, keyrow, halves, teacher, whigh, wlow, bias, length):
     pixels, width = teacher.shape
     pool = 8 * L
     scratch = [
-        pltpu.VMEM((pool, pool), BF16),
         pltpu.VMEM((64, L), F32),
         pltpu.VMEM((pool, 2 * L), BF16),
         pltpu.VMEM((L, pool), F32),
@@ -515,10 +571,10 @@
     return call(
         functools.partial(front_kernel, float(length)),
         [f32(GAT * L, L), f32(GAT * L, L), f32(L, pool), f32(pixels, L)],
-        [SMEM, SMEM] + [VMEM] * 7,
+        [SMEM, SMEM] + [VMEM] * 10,
         scratch,
         flops=10**10,
-    )(par, ids, own, peer, keyrow, teacher, whigh, wlow, bias)
+    )(par, ids, own, peer, keyrow, *halves, teacher, whigh, wlow, bias)
 
 
 def back(par, ids, own, peer, keyrow, trans, grad, length):
@@ -550,13 +606,23 @@
     return call(compose_kernel, f32(RET * L, L), [VMEM] * 3, flops=10**9)(share, keep, give)
 
 
-def final(par, idx, own, peer, gauss, width, pixels):
+def place(par, idx, own, gauss):
+    return call(
+        place_kernel,
+        [f32(gauss, L), f32(gauss // L * 8, L), bf16(gauss, 4 * L)],
+        [SMEM, VMEM, VMEM],
+        flops=10**9,
+    )(par, idx, own)
+
+
+def final(par, idx, own, peer, parts, width, pixels):
+    gauss = parts[0].shape[0]
     return call(
         functools.partial(final_kernel, float(pixels)),
         [f32(gauss, L), f32(6, gauss), f32(L, width), f32(1, width), f32(1, L)],
-        [SMEM, VMEM, VMEM, VMEM],
-        flops=4 * 10**9,
-    )(par, idx, own, peer)
+        [SMEM] + [VMEM] * 6,
+        flops=2 * 10**9,
+    )(par, idx, own, peer, *parts)
 
 
 def swap(value):
@@ -583,18 +649,21 @@
     got, (keyrow, whigh, wlow) = lax.optimization_barrier((got, prepared))
     peer = swap(got)
     length = tile_lists.shape[1]
+    halves = ready(par, tile_ids, got, keyrow, length)
     flat_teacher = teacher.reshape(-1, width)
     bias = decoder_bias.reshape(1, -1)
     keep, give, trans, grad = front(
-        par, tile_ids, got, peer, keyrow, flat_teacher, whigh, wlow, bias, length
+        par, tile_ids, got, peer, keyrow, halves, flat_teacher, whigh, wlow, bias, length
     )
     part, trans, grad = lax.optimization_barrier((keep + swap(give), trans, grad))
     share = exchange(part, GAT)
     keep, give = back(par, tile_ids, got, peer, keyrow, trans, grad, length)
     ret = exchange(compose(share, keep, swap(give)), RET)
+    other = swap(ret)
+    parts = place(par, idx, ret, features.shape[0])
     pixels = holders * tile_ids.shape[0] * 256
     grad_features, grad_params, grad_weight, grad_bias, loss = final(
-        par, idx, ret, swap(ret), features.shape[0], width, pixels
+        par, idx, ret, other, parts, width, pixels
     )
     return grad_features, grad_params, grad_weight, grad_bias.reshape(-1), loss[0, 0]
 

time: 98.8 us -> 97.1 us (0.983)
  waiting for transfers between devices: 24.1 us -> 22.6 us
    pallas_call x0 -> x2, Pallas kernels: none -> 2.59 us  [the longest x1 1.54 us: ready(): call(functools.partial(ready_kernel, float(length)), [bf16(pool, pool), f...]
    ppermute x4, waiting for transfers between devices: 5.03 us -> 3.28 us  [swap(): return lax.ppermute(value, 'px', SWAP)]
    pallas_call x1, Pallas kernels: 6.13 us -> 4.92 us  [front(): call(functools.partial(front_kernel, float(length)), [f32(GAT * L, L), f3...]
  transfers between devices with their start and end apart: 6 -> 6, of which waited for: 6 -> 5; matrix products, arithmetic and copies ran while one was open for 0% -> 0% of each run, Pallas kernels for 5% -> 8%
where the time goes in v5:
time: 97.1 us; the launch traced here: 96.7 us
  starting transfers between devices  28.6 us (29%)
  blocking collectives  25.2 us (26%)
  waiting for transfers between devices  22.6 us (23%)
  Pallas kernels  17.8 us (18%)
  local copies, waits for them, and re-layouts  1.07 us (1%)
    all_to_all x1, blocking collectives, exchange(): lax.all_to_all(sent, 'gs', split_axis=0, concat_axis=0, tiled=True)  25.2 us
    all_to_all x2, starting transfers between devices, exchange(): lax.all_to_all(sent, 'gs', split_axis=0, concat_axis=0, tiled=True)  22.7 us
    all_to_all x2, waiting for transfers between devices, exchange(): lax.all_to_all(sent, 'gs', split_axis=0, concat_axis=0, tiled=True)  19.3 us
    ppermute x4, starting transfers between devices, swap(): return lax.ppermute(value, 'px', SWAP)  5.88 us
    pallas_call x1, Pallas kernels, front(): call(functools.partial(front_kernel, float(length)), [f32(GAT * L, L), f3...  4.92 us
    pallas_call x1, Pallas kernels, back(): call(functools.partial(back_kernel, float(length)), [f32(FWD * L, L), f32...  4.74 us
    ppermute x4, waiting for transfers between devices, swap(): return lax.ppermute(value, 'px', SWAP)  3.28 us
    pallas_call x1, Pallas kernels, pack(): call(pack_kernel, shapes, [SMEM, HBM, HBM, HBM], scratch, flops=2 * 10 **...  2.95 us
  transfers between devices with their start and end apart: 6, of which 5 were waited for; matrix products, arithmetic and copies ran while one was open for 0% of the time, Pallas kernels for 8%

profile of v5, /device:TPU:1, one launch (start us, length us, event | category | flops | bytes accessed | tf_op | source)
XLA Modules:
  0.0 96.7 jit_solution(11801000402559565662)
XLA Ops:
  0.7 2.9 %shard_map.119 = (f32[640,128]{1,0:T(8,128)}, s32[8,128]{1,0:T(8,128)}) custom-call(s32[1]{0:T(128)} %bitcast.par_ref, s32[8,128]{1,0:T(8,128)} %bitcast.25, f32[2048,128]{1,0:T(8,128)} %feat_hbm.1, f32[6,2048]{1,0:T(8,128)} %prm_hbm.1), custom_call_target="tpu_custom_call" | custom-call | flops 2000000000 | bytes 6666666 | tf_op jit(solution)/shard_map/pallas_call | solution.py:538
  3.6 16.3 %all-to-all-start = ((f32[128,1,640]{2,1,0:T(1,128)}), f32[128,1,640]{2,1,0:T(1,128)S(1)}, u32[]{:S(2)}, u32[]{:S(2)}) async-start(f32[128,1,640]{2,1,0:T(1,128)} %bitcast.24), calls=%async_computation | async-start | bytes 655360 | tf_op jit(solution)/shard_map/all_to_all | solution.py:634
  20.0 0.5 shard_map.120
  20.5 0.0 copy-start
  20.5 0.0 copy-start.3
  20.5 14.1 %all-to-all-done = f32[128,1,640]{2,1,0:T(1,128)S(1)} async-done(((f32[128,1,640]{2,1,0:T(1,128)}), f32[128,1,640]{2,1,0:T(1,128)S(1)}, u32[]{:S(2)}, u32[]{:S(2)}) %all-to-all-start) | async-done | bytes 327712 | tf_op jit(solution)/shard_map/all_to_all | solution.py:634
  34.7 2.8 %collective-permute-start = (f32[640,128]{1,0:T(8,128)S(1)}, f32[640,128]{1,0:T(8,128)S(1)}, u32[]{:S(2)}, u32[]{:S(2)}) collective-permute-start(f32[640,128]{1,0:T(8,128)S(1)} %bitcast.17), channel_id=1, source_target_pairs={{0,1},{1,0},{2,3},{3,2},{4,5},{5,4},{6,7},{7,6},{8,9},{9,8},{10,11... | collective-permute-start | bytes 983048 | tf_op jit(solution)/shard_map/ppermute | solution.py:629
  37.5 1.5 %shard_map.121 = (bf16[1024,1024]{1,0:T(8,128)(2,1)S(1)}, f32[128,512]{1,0:T(8,128)S(1)}, bf16[256,512]{1,0:T(8,128)(2,1)S(1)}) custom-call(s32[1]{0:T(128)} %bitcast.par_ref, s32[8]{0:T(128)S(1)} %copy-done.4, f32[640,128]{1,0:T(8,128)S(1)} %bitcast.18, f32[8,128]{1,0:T(8,128)S(1)} %get-tuple-element.47.keyrow_ref), custom_call_target="tpu_custom_call" | custom-call | flops 1000000000 | bytes 3333333 | tf_op jit(solution)/shard_map/pallas_call | solution.py:548
  39.0 4.9 %shard_map.122 = (f32[384,128]{1,0:T(8,128)S(1)}, f32[384,128]{1,0:T(8,128)S(1)}, f32[128,1024]{1,0:T(8,128)S(1)}, f32[1024,128]{1,0:T(8,128)S(1)}) custom-call(s32[1]{0:T(128)} %bitcast.par_ref, s32[8]{0:T(128)S(1)} %copy-done.4, f32[640,128]{1,0:T(8,128)S(1)} %bitcast.19, f32[640,128]{1,0:T(8,128)S(1)} %collective-permute-done.peer_ref, ...), custom_call_target="tpu_custom_call" | custom-call | flops 10000000000 | bytes 33333332 | tf_op jit(solution)/shard_map/pallas_call | solution.py:571
  44.0 0.1 collective-permute-start.1
  44.1 1.4 %collective-permute-done.1 = f32[384,128]{1,0:T(8,128)S(1)} collective-permute-done((f32[384,128]{1,0:T(8,128)S(1)}, f32[384,128]{1,0:T(8,128)S(1)}, u32[]{:S(2)}, u32[]{:S(2)}) %collective-permute-start.1) | collective-permute-done | bytes 196640 | tf_op jit(solution)/shard_map/ppermute | solution.py:629
  45.5 0.7 add.3
  46.2 6.4 %all-to-all-start.1 = ((f32[128,1,384]{2,1,0:T(1,128)}), f32[128,1,384]{2,1,0:T(1,128)S(1)}, u32[]{:S(2)}, u32[]{:S(2)}) async-start(f32[128,1,384]{2,1,0:T(1,128)} %bitcast.6), calls=%async_computation.1 | async-start | bytes 393216 | tf_op jit(solution)/shard_map/all_to_all | solution.py:634
  52.6 1.0 %copy-done.6 = f32[1024,128]{1,0:T(8,128)S(1)} copy-done((f32[1024,128]{1,0:T(8,128)S(1)}, f32[1024,128]{1,0:T(8,128)}, u32[]{:S(2)}) %copy-start.6) | copy-done | bytes 524312
  53.6 4.7 %shard_map.123 = (f32[640,128]{1,0:T(8,128)S(1)}, f32[640,128]{1,0:T(8,128)S(1)}) custom-call(s32[1]{0:T(128)} %bitcast.par_ref, s32[8]{0:T(128)S(1)} %copy-done.4, f32[640,128]{1,0:T(8,128)S(1)} %bitcast.20, f32[640,128]{1,0:T(8,128)S(1)} %collective-permute-done.peer_ref, f32[8,128]{1,0:T(8,128)S(1)} %get-tuple-element.47.keyrow_ref, ...), custom_call_target="tpu_custom_call" | custom-call | flops 8000000000 | bytes 26666666 | tf_op jit(solution)/shard_map/pallas_call | solution.py:596
  58.4 0.2 collective-permute-start.2
  58.6 1.5 %collective-permute-done.2.give_ref = f32[640,128]{1,0:T(8,128)S(1)} collective-permute-done((f32[640,128]{1,0:T(8,128)S(1)}, f32[640,128]{1,0:T(8,128)S(1)}, u32[]{:S(2)}, u32[]{:S(2)}) %collective-permute-start.2) | collective-permute-done | bytes 327712 | tf_op jit(solution)/shard_map/ppermute | solution.py:629
  60.1 5.2 %all-to-all-done.1 = f32[128,1,384]{2,1,0:T(1,128)S(1)} async-done(((f32[128,1,384]{2,1,0:T(1,128)}), f32[128,1,384]{2,1,0:T(1,128)S(1)}, u32[]{:S(2)}, u32[]{:S(2)}) %all-to-all-start.1) | async-done | bytes 196640 | tf_op jit(solution)/shard_map/all_to_all | solution.py:634
  65.3 0.1 shard_map.124
  65.4 25.2 %all_to_all.15 = f32[128,1,896]{2,1,0:T(1,128)S(1)} all-to-all(f32[128,1,896]{2,1,0:T(1,128)S(1)} %bitcast.16), channel_id=1, replica_groups=mesh['gs'=128,'px'=2] {'gs'}, dimensions={0} | all-to-all | bytes 917504 | tf_op jit(solution)/shard_map/all_to_all | solution.py:634
  90.6 2.7 %collective-permute-start.3 = (f32[896,128]{1,0:T(8,128)S(1)}, f32[896,128]{1,0:T(8,128)S(1)}, u32[]{:S(2)}, u32[]{:S(2)}) collective-permute-start(f32[896,128]{1,0:T(8,128)S(1)} %bitcast.13), channel_id=1, source_target_pairs={{0,1},{1,0},{2,3},{3,2},{4,5},{5,4},{6,7},{7,6},{8,9},{9,8},{10,11... | collective-permute-start | bytes 1376264 | tf_op jit(solution)/shard_map/ppermute | solution.py:629
  93.3 1.0 %shard_map.125 = (f32[2048,128]{1,0:T(8,128)S(1)}, f32[128,128]{1,0:T(8,128)S(1)}, bf16[2048,512]{1,0:T(8,128)(2,1)S(1)}) custom-call(s32[1]{0:T(128)} %bitcast.par_ref, s32[8,128]{1,0:T(8,128)S(1)} %copy-done.7, f32[896,128]{1,0:T(8,128)S(1)} %bitcast.14), custom_call_target="tpu_custom_call" | custom-call | flops 1000000000 | bytes 3333333 | tf_op jit(solution)/shard_map/pallas_call | solution.py:610
  94.4 0.4 collective-permute-done.3.peer_ref
  94.8 2.0 %shard_map.126 = (f32[2048,128]{1,0:T(8,128)}, f32[6,2048]{1,0:T(8,128)}, f32[128,512]{1,0:T(8,128)}, f32[1,512]{1,0:T(1,128)}, f32[1,128]{1,0:T(1,128)}) custom-call(s32[1]{0:T(128)} %bitcast.par_ref, s32[8,128]{1,0:T(8,128)S(1)} %copy-done.7, f32[896,128]{1,0:T(8,128)S(1)} %bitcast.15, f32[896,128]{1,0:T(8,128)S(1)} %collective-permute-done.3.peer_ref, ...), custom_call_target="tpu_custom_call" | custom-call | flops 2000000000 | bytes 6666666 | tf_op jit(solution)/shard_map/pallas_call | solution.py:620
  (14 shorter events, 0.0 us)
Async XLA Ops:
  0.6 19.3 %copy-start.1 = (f32[128,512]{1,0:T(8,128)S(1)}, f32[128,512]{1,0:T(8,128)}, u32[]{:S(2)}) copy-start(f32[128,512]{1,0:T(8,128)} %weight_ref) | copy-start | bytes 786436
  0.6 19.3 %copy-start.2 = (s32[8,512]{1,0:T(8,128)S(1)}, s32[8,512]{1,0:T(8,128)}, u32[]{:S(2)}) copy-start(s32[8,512]{1,0:T(8,128)} %lists_ref) | copy-start | bytes 49156
  3.6 31.1 %all-to-all-start = ((f32[128,1,640]{2,1,0:T(1,128)}), f32[128,1,640]{2,1,0:T(1,128)S(1)}, u32[]{:S(2)}, u32[]{:S(2)}) async-start(f32[128,1,640]{2,1,0:T(1,128)} %bitcast.24), calls=%async_computation | async-start | bytes 655360 | tf_op jit(solution)/shard_map/all_to_all | solution.py:634
  20.0 17.5 %copy-start.4 = (s32[8]{0:T(128)S(1)}, s32[8]{0:T(128)}, u32[]{:S(2)}) copy-start(s32[8]{0:T(128)} %ids_ref.5) | copy-start | bytes 100
  20.5 18.5 %copy-start = (f32[8,128,512]{2,1,0:T(8,128)S(1)}, f32[8,128,512]{2,1,0:T(8,128)}, u32[]{:S(2)}) copy-start(f32[8,128,512]{2,1,0:T(8,128)} %param.13) | copy-start | bytes 6291460
  20.5 18.5 %copy-start.3 = (f32[512]{0:T(512)S(1)}, f32[512]{0:T(512)}, u32[]{:S(2)}) copy-start(f32[512]{0:T(512)} %param.15) | copy-start | bytes 6148
  34.7 4.3 %collective-permute-start = (f32[640,128]{1,0:T(8,128)S(1)}, f32[640,128]{1,0:T(8,128)S(1)}, u32[]{:S(2)}, u32[]{:S(2)}) collective-permute-start(f32[640,128]{1,0:T(8,128)S(1)} %bitcast.17), channel_id=1, source_target_pairs={{0,1},{1,0},{2,3},{3,2},{4,5},{5,4},{6,7},{7,6},{8,9},{9,8},{10,11... | collective-permute-start | bytes 983048 | tf_op jit(solution)/shard_map/ppermute | solution.py:629
  44.0 2.2 %copy-start.5 = (f32[1024,128]{1,0:T(8,128)}, f32[1024,128]{1,0:T(8,128)S(1)}, u32[]{:S(2)}) copy-start(f32[1024,128]{1,0:T(8,128)S(1)} %get-tuple-element.60.grad_ref) | copy-start | bytes 1572868
  44.0 1.5 %collective-permute-start.1 = (f32[384,128]{1,0:T(8,128)S(1)}, f32[384,128]{1,0:T(8,128)S(1)}, u32[]{:S(2)}, u32[]{:S(2)}) collective-permute-start(f32[384,128]{1,0:T(8,128)S(1)} %get-tuple-element.55), channel_id=1, source_target_pairs={{0,1},{1,0},{2,3},{3,2},{4,5},{5,4},{6,7},{7,6},{8,9},{9,8},{10,11... | collective-permute-start | bytes 589832 | tf_op jit(solution)/shard_map/ppermute | solution.py:629
  46.2 19.0 %all-to-all-start.1 = ((f32[128,1,384]{2,1,0:T(1,128)}), f32[128,1,384]{2,1,0:T(1,128)S(1)}, u32[]{:S(2)}, u32[]{:S(2)}) async-start(f32[128,1,384]{2,1,0:T(1,128)} %bitcast.6), calls=%async_computation.1 | async-start | bytes 393216 | tf_op jit(solution)/shard_map/all_to_all | solution.py:634
  52.6 1.0 %copy-start.6 = (f32[1024,128]{1,0:T(8,128)S(1)}, f32[1024,128]{1,0:T(8,128)}, u32[]{:S(2)}) copy-start(f32[1024,128]{1,0:T(8,128)} %copy-done.5) | copy-start | bytes 1572868
  58.4 1.7 %collective-permute-start.2 = (f32[640,128]{1,0:T(8,128)S(1)}, f32[640,128]{1,0:T(8,128)S(1)}, u32[]{:S(2)}, u32[]{:S(2)}) collective-permute-start(f32[640,128]{1,0:T(8,128)S(1)} %get-tuple-element.62), channel_id=1, source_target_pairs={{0,1},{1,0},{2,3},{3,2},{4,5},{5,4},{6,7},{7,6},{8,9},{9,8},{10,11... | collective-permute-start | bytes 983048 | tf_op jit(solution)/shard_map/ppermute | solution.py:629
  65.3 28.1 %copy-start.7 = (s32[8,128]{1,0:T(8,128)S(1)}, s32[8,128]{1,0:T(8,128)}, u32[]{:S(2)}) copy-start(s32[8,128]{1,0:T(8,128)} %get-tuple-element.38.idx_ref) | copy-start | bytes 12292
  90.6 4.2 %collective-permute-start.3 = (f32[896,128]{1,0:T(8,128)S(1)}, f32[896,128]{1,0:T(8,128)S(1)}, u32[]{:S(2)}, u32[]{:S(2)}) collective-permute-start(f32[896,128]{1,0:T(8,128)S(1)} %bitcast.13), channel_id=1, source_target_pairs={{0,1},{1,0},{2,3},{3,2},{4,5},{5,4},{6,7},{7,6},{8,9},{9,8},{10,11... | collective-permute-start | bytes 1376264 | tf_op jit(solution)/shard_map/ppermute | solution.py:629

commit v6 on v5

--- a/solution.py
+++ b/solution.py
@@ -233,7 +233,8 @@
     keep_ref,
     give_ref,
     trans_ref,
-    grad_ref,
+    resid_hi,
+    resid_lo,
     prm_ref,
     feat_ref,
     alpha_ref,
@@ -241,8 +242,6 @@
     wm_hi,
     wm_lo,
     rt_ref,
-    resid_hi,
-    resid_lo,
 ):
     pool = Pool(
         length, par_ref, ids_ref, keyrow_ref, prm_ref, ((0, own_ref), (1, peer_ref))
@@ -265,7 +264,6 @@
 
     w_hi, w_lo = whigh_ref[...], wlow_ref[...]
     w_pair = jnp.concatenate([w_hi, w_hi], axis=0)
-    w_both = jnp.concatenate([w_hi, w_lo], axis=0)
     width = whigh_ref.shape[1]
     squares = jnp.zeros((1, width), F32)
     bias_sum = jnp.zeros((1, width), F32)
@@ -285,8 +283,6 @@
         high, low = split2(resid)
         resid_hi[rows, :] = high
         resid_lo[rows, :] = low
-        both = nt(high, w_both)
-        grad_ref[rows, :] = both[:, :L] + both[:, L:] + nt(low, w_hi)
 
     both = nn(rt_ref[...], resid_hi[...])
     grad_w = both[:L] + both[L:] + nn(rt_ref[0:L, :], resid_lo[...])
@@ -300,6 +296,16 @@
         piece = jnp.where(left, bias_sum[:, :half], bias_sum[:, half:])
         rows = jnp.concatenate([piece[:, :L], piece[:, L:], sq_row], axis=0)
         ref[pl.ds(2, L, stride=GAT), :] = column_of(rows)
+
+
+def pixel_kernel(resid_hi, resid_lo, whigh_ref, wlow_ref, grad_ref):
+    w_hi = whigh_ref[...]
+    w_both = jnp.concatenate([w_hi, wlow_ref[...]], axis=0)
+    step = 2 * L
+    for r in range(4):
+        rows = slice(r * step, r * step + step)
+        both = nt(resid_hi[rows, :], w_both)
+        grad_ref[rows, :] = both[:, :L] + both[:, L:] + nt(resid_lo[rows, :], w_hi)
 
 
 def back_kernel(
@@ -565,16 +571,19 @@
         pltpu.VMEM((pixels, pool), BF16),
         pltpu.VMEM((pixels, pool), BF16),
         pltpu.VMEM((2 * L, pixels), BF16),
-        pltpu.VMEM((pixels, width), BF16),
-        pltpu.VMEM((pixels, width), BF16),
     ]
     return call(
         functools.partial(front_kernel, float(length)),
-        [f32(GAT * L, L), f32(GAT * L, L), f32(L, pool), f32(pixels, L)],
+        [f32(GAT * L, L), f32(GAT * L, L), f32(L, pool), bf16(pixels, width), bf16(pixels, width)],
         [SMEM, SMEM] + [VMEM] * 10,
         scratch,
         flops=10**10,
     )(par, ids, own, peer, keyrow, *halves, teacher, whigh, wlow, bias)
+
+
+def pixel(resid_hi, resid_lo, whigh, wlow):
+    shape = f32(resid_hi.shape[0], whigh.shape[0])
+    return call(pixel_kernel, shape, [VMEM] * 4, flops=10**9)(resid_hi, resid_lo, whigh, wlow)
 
 
 def back(par, ids, own, peer, keyrow, trans, grad, length):
@@ -652,10 +661,12 @@
     halves = ready(par, tile_ids, got, keyrow, length)
     flat_teacher = teacher.reshape(-1, width)
     bias = decoder_bias.reshape(1, -1)
-    keep, give, trans, grad = front(
+    keep, give, trans, resid_hi, resid_lo = front(
         par, tile_ids, got, peer, keyrow, halves, flat_teacher, whigh, wlow, bias, length
     )
-    part, trans, grad = lax.optimization_barrier((keep + swap(give), trans, grad))
+    given = swap(give)
+    grad = pixel(resid_hi, resid_lo, whigh, wlow)
+    part, trans, grad = lax.optimization_barrier((keep + given, trans, grad))
     share = exchange(part, GAT)
     keep, give = back(par, tile_ids, got, peer, keyrow, trans, grad, length)
     ret = exchange(compose(share, keep, swap(give)), RET)

time: 97.1 us -> 95.3 us (0.981)
  blocking collectives: 25.2 us -> 24.1 us
  local copies, waits for them, and re-layouts: 1.07 us -> 0.03 us
    all_to_all x1, blocking collectives: 25.2 us -> 24.1 us  [exchange(): lax.all_to_all(sent, 'gs', split_axis=0, concat_axis=0, tiled=True)]
    unnamed x16 -> x12, local copies, waits for them, and re-layouts: 1.07 us -> 0.03 us
    all_to_all x2, waiting for transfers between devices: 19.3 us -> 20.3 us  [exchange(): lax.all_to_all(sent, 'gs', split_axis=0, concat_axis=0, tiled=True)]
  transfers between devices with their start and end apart: 6 -> 6, of which waited for: 5 -> 5; matrix products, arithmetic and copies ran while one was open for 0% -> 0% of each run, Pallas kernels for 8% -> 9%
where the time goes in v6:
time: 95.3 us; the launch traced here: 95 us
  starting transfers between devices  28.6 us (30%)
  blocking collectives  24.1 us (25%)
  waiting for transfers between devices  22.9 us (24%)
  Pallas kernels  17.8 us (19%)
    all_to_all x1, blocking collectives, exchange(): lax.all_to_all(sent, 'gs', split_axis=0, concat_axis=0, tiled=True)  24.1 us
    all_to_all x2, starting transfers between devices, exchange(): lax.all_to_all(sent, 'gs', split_axis=0, concat_axis=0, tiled=True)  22.7 us
    all_to_all x2, waiting for transfers between devices, exchange(): lax.all_to_all(sent, 'gs', split_axis=0, concat_axis=0, tiled=True)  20.3 us
    ppermute x4, starting transfers between devices, swap(): return lax.ppermute(value, 'px', SWAP)  5.91 us
    pallas_call x1, Pallas kernels, back(): call(functools.partial(back_kernel, float(length)), [f32(FWD * L, L), f32...  4.75 us
    pallas_call x1, Pallas kernels, front(): call(functools.partial(front_kernel, float(length)), [f32(GAT * L, L), f3...  4.25 us
    pallas_call x1, Pallas kernels, pack(): call(pack_kernel, shapes, [SMEM, HBM, HBM, HBM], scratch, flops=2 * 10 **...  2.95 us
    ppermute x4, waiting for transfers between devices, swap(): return lax.ppermute(value, 'px', SWAP)  2.57 us
  transfers between devices with their start and end apart: 6, of which 5 were waited for; matrix products, arithmetic and copies ran while one was open for 0% of the time, Pallas kernels for 9%

profile of v6, /device:TPU:1, one launch (start us, length us, event | category | flops | bytes accessed | tf_op | source)
XLA Modules:
  0.0 95.0 jit_solution(15906167574993695395)
XLA Ops:
  0.7 2.9 %shard_map.119 = (f32[640,128]{1,0:T(8,128)}, s32[8,128]{1,0:T(8,128)}) custom-call(s32[1]{0:T(128)} %bitcast.par_ref, s32[8,128]{1,0:T(8,128)} %bitcast.25, f32[2048,128]{1,0:T(8,128)} %feat_hbm.1, f32[6,2048]{1,0:T(8,128)} %prm_hbm.1), custom_call_target="tpu_custom_call" | custom-call | flops 2000000000 | bytes 6666666 | tf_op jit(solution)/shard_map/pallas_call | solution.py:544
  3.6 16.3 %all-to-all-start = ((f32[128,1,640]{2,1,0:T(1,128)}), f32[128,1,640]{2,1,0:T(1,128)S(1)}, u32[]{:S(2)}, u32[]{:S(2)}) async-start(f32[128,1,640]{2,1,0:T(1,128)} %bitcast.24), calls=%async_computation | async-start | bytes 655360 | tf_op jit(solution)/shard_map/all_to_all | solution.py:643
  20.0 0.5 shard_map.120
  20.5 0.0 copy-start
  20.5 0.0 copy-start.3
  20.5 14.1 %all-to-all-done = f32[128,1,640]{2,1,0:T(1,128)S(1)} async-done(((f32[128,1,640]{2,1,0:T(1,128)}), f32[128,1,640]{2,1,0:T(1,128)S(1)}, u32[]{:S(2)}, u32[]{:S(2)}) %all-to-all-start) | async-done | bytes 327712 | tf_op jit(solution)/shard_map/all_to_all | solution.py:643
  34.7 2.8 %collective-permute-start = (f32[640,128]{1,0:T(8,128)S(1)}, f32[640,128]{1,0:T(8,128)S(1)}, u32[]{:S(2)}, u32[]{:S(2)}) collective-permute-start(f32[640,128]{1,0:T(8,128)S(1)} %bitcast.17), channel_id=1, source_target_pairs={{0,1},{1,0},{2,3},{3,2},{4,5},{5,4},{6,7},{7,6},{8,9},{9,8},{10,11... | collective-permute-start | bytes 983048 | tf_op jit(solution)/shard_map/ppermute | solution.py:638
  37.5 1.5 %shard_map.121 = (bf16[1024,1024]{1,0:T(8,128)(2,1)S(1)}, f32[128,512]{1,0:T(8,128)S(1)}, bf16[256,512]{1,0:T(8,128)(2,1)S(1)}) custom-call(s32[1]{0:T(128)} %bitcast.par_ref, s32[8]{0:T(128)S(1)} %copy-done.4, f32[640,128]{1,0:T(8,128)S(1)} %bitcast.18, f32[8,128]{1,0:T(8,128)S(1)} %get-tuple-element.48.keyrow_ref), custom_call_target="tpu_custom_call" | custom-call | flops 1000000000 | bytes 3333333 | tf_op jit(solution)/shard_map/pallas_call | solution.py:554
  39.0 4.2 %shard_map.122 = (f32[384,128]{1,0:T(8,128)S(1)}, f32[384,128]{1,0:T(8,128)S(1)}, f32[128,1024]{1,0:T(8,128)S(1)}, bf16[1024,512]{1,0:T(8,128)(2,1)S(1)}, bf16[1024,512]{1,0:T(8,128)(2,1)S(1)}) custom-call(s32[1]{0:T(128)} %bitcast.par_ref, s32[8]{0:T(128)S(1)} %copy-done.4, f32[640,128]{1,0:T(8,128)S(1)} %bitcast.19, ...), custom_call_target="tpu_custom_call" | custom-call | flops 10000000000 | bytes 33333332 | tf_op jit(solution)/shard_map/pallas_call | solution.py:575
  43.3 0.1 collective-permute-start.1
  43.4 0.7 shard_map.123.grad_ref
  44.1 0.7 collective-permute-done.1
  44.8 0.7 add.3
  45.5 6.4 %all-to-all-start.1 = ((f32[128,1,384]{2,1,0:T(1,128)}), f32[128,1,384]{2,1,0:T(1,128)S(1)}, u32[]{:S(2)}, u32[]{:S(2)}) async-start(f32[128,1,384]{2,1,0:T(1,128)} %bitcast.6), calls=%async_computation.1 | async-start | bytes 393216 | tf_op jit(solution)/shard_map/all_to_all | solution.py:643
  51.9 4.8 %shard_map.124 = (f32[640,128]{1,0:T(8,128)S(1)}, f32[640,128]{1,0:T(8,128)S(1)}) custom-call(s32[1]{0:T(128)} %bitcast.par_ref, s32[8]{0:T(128)S(1)} %copy-done.4, f32[640,128]{1,0:T(8,128)S(1)} %bitcast.20, f32[640,128]{1,0:T(8,128)S(1)} %collective-permute-done.peer_ref, f32[8,128]{1,0:T(8,128)S(1)} %get-tuple-element.48.keyrow_ref, ...), custom_call_target="tpu_custom_call" | custom-call | flops 8000000000 | bytes 26666666 | tf_op jit(solution)/shard_map/pallas_call | solution.py:605
  56.6 0.2 collective-permute-start.2
  56.9 1.5 %collective-permute-done.2.give_ref = f32[640,128]{1,0:T(8,128)S(1)} collective-permute-done((f32[640,128]{1,0:T(8,128)S(1)}, f32[640,128]{1,0:T(8,128)S(1)}, u32[]{:S(2)}, u32[]{:S(2)}) %collective-permute-start.2) | collective-permute-done | bytes 327712 | tf_op jit(solution)/shard_map/ppermute | solution.py:638
  58.4 6.2 %all-to-all-done.1 = f32[128,1,384]{2,1,0:T(1,128)S(1)} async-done(((f32[128,1,384]{2,1,0:T(1,128)}), f32[128,1,384]{2,1,0:T(1,128)S(1)}, u32[]{:S(2)}, u32[]{:S(2)}) %all-to-all-start.1) | async-done | bytes 196640 | tf_op jit(solution)/shard_map/all_to_all | solution.py:643
  64.6 0.1 shard_map.125
  64.7 24.1 %all_to_all.15 = f32[128,1,896]{2,1,0:T(1,128)S(1)} all-to-all(f32[128,1,896]{2,1,0:T(1,128)S(1)} %bitcast.16), channel_id=1, replica_groups=mesh['gs'=128,'px'=2] {'gs'}, dimensions={0} | all-to-all | bytes 917504 | tf_op jit(solution)/shard_map/all_to_all | solution.py:643
  88.8 2.8 %collective-permute-start.3 = (f32[896,128]{1,0:T(8,128)S(1)}, f32[896,128]{1,0:T(8,128)S(1)}, u32[]{:S(2)}, u32[]{:S(2)}) collective-permute-start(f32[896,128]{1,0:T(8,128)S(1)} %bitcast.13), channel_id=1, source_target_pairs={{0,1},{1,0},{2,3},{3,2},{4,5},{5,4},{6,7},{7,6},{8,9},{9,8},{10,11... | collective-permute-start | bytes 1376264 | tf_op jit(solution)/shard_map/ppermute | solution.py:638
  91.6 1.0 %shard_map.126 = (f32[2048,128]{1,0:T(8,128)S(1)}, f32[128,128]{1,0:T(8,128)S(1)}, bf16[2048,512]{1,0:T(8,128)(2,1)S(1)}) custom-call(s32[1]{0:T(128)} %bitcast.par_ref, s32[8,128]{1,0:T(8,128)S(1)} %copy-done.5, f32[896,128]{1,0:T(8,128)S(1)} %bitcast.14), custom_call_target="tpu_custom_call" | custom-call | flops 1000000000 | bytes 3333333 | tf_op jit(solution)/shard_map/pallas_call | solution.py:619
  92.6 0.4 collective-permute-done.3.peer_ref
  93.0 2.0 %shard_map.127 = (f32[2048,128]{1,0:T(8,128)}, f32[6,2048]{1,0:T(8,128)}, f32[128,512]{1,0:T(8,128)}, f32[1,512]{1,0:T(1,128)}, f32[1,128]{1,0:T(1,128)}) custom-call(s32[1]{0:T(128)} %bitcast.par_ref, s32[8,128]{1,0:T(8,128)S(1)} %copy-done.5, f32[896,128]{1,0:T(8,128)S(1)} %bitcast.15, f32[896,128]{1,0:T(8,128)S(1)} %collective-permute-done.3.peer_ref, ...), custom_call_target="tpu_custom_call" | custom-call | flops 2000000000 | bytes 6666666 | tf_op jit(solution)/shard_map/pallas_call | solution.py:629
  (11 shorter events, 0.0 us)
Async XLA Ops:
  0.6 19.3 %copy-start.1 = (f32[128,512]{1,0:T(8,128)S(1)}, f32[128,512]{1,0:T(8,128)}, u32[]{:S(2)}) copy-start(f32[128,512]{1,0:T(8,128)} %weight_ref) | copy-start | bytes 786436
  0.6 19.3 %copy-start.2 = (s32[8,512]{1,0:T(8,128)S(1)}, s32[8,512]{1,0:T(8,128)}, u32[]{:S(2)}) copy-start(s32[8,512]{1,0:T(8,128)} %lists_ref) | copy-start | bytes 49156
  3.6 31.1 %all-to-all-start = ((f32[128,1,640]{2,1,0:T(1,128)}), f32[128,1,640]{2,1,0:T(1,128)S(1)}, u32[]{:S(2)}, u32[]{:S(2)}) async-start(f32[128,1,640]{2,1,0:T(1,128)} %bitcast.24), calls=%async_computation | async-start | bytes 655360 | tf_op jit(solution)/shard_map/all_to_all | solution.py:643
  20.0 17.5 %copy-start.4 = (s32[8]{0:T(128)S(1)}, s32[8]{0:T(128)}, u32[]{:S(2)}) copy-start(s32[8]{0:T(128)} %ids_ref.5) | copy-start | bytes 100
  20.5 18.5 %copy-start = (f32[8,128,512]{2,1,0:T(8,128)S(1)}, f32[8,128,512]{2,1,0:T(8,128)}, u32[]{:S(2)}) copy-start(f32[8,128,512]{2,1,0:T(8,128)} %param.13) | copy-start | bytes 6291460
  20.5 18.5 %copy-start.3 = (f32[512]{0:T(512)S(1)}, f32[512]{0:T(512)}, u32[]{:S(2)}) copy-start(f32[512]{0:T(512)} %param.15) | copy-start | bytes 6148
  34.7 4.3 %collective-permute-start = (f32[640,128]{1,0:T(8,128)S(1)}, f32[640,128]{1,0:T(8,128)S(1)}, u32[]{:S(2)}, u32[]{:S(2)}) collective-permute-start(f32[640,128]{1,0:T(8,128)S(1)} %bitcast.17), channel_id=1, source_target_pairs={{0,1},{1,0},{2,3},{3,2},{4,5},{5,4},{6,7},{7,6},{8,9},{9,8},{10,11... | collective-permute-start | bytes 983048 | tf_op jit(solution)/shard_map/ppermute | solution.py:638
  43.3 1.5 %collective-permute-start.1 = (f32[384,128]{1,0:T(8,128)S(1)}, f32[384,128]{1,0:T(8,128)S(1)}, u32[]{:S(2)}, u32[]{:S(2)}) collective-permute-start(f32[384,128]{1,0:T(8,128)S(1)} %get-tuple-element.56), channel_id=1, source_target_pairs={{0,1},{1,0},{2,3},{3,2},{4,5},{5,4},{6,7},{7,6},{8,9},{9,8},{10,11... | collective-permute-start | bytes 589832 | tf_op jit(solution)/shard_map/ppermute | solution.py:638
  45.5 19.0 %all-to-all-start.1 = ((f32[128,1,384]{2,1,0:T(1,128)}), f32[128,1,384]{2,1,0:T(1,128)S(1)}, u32[]{:S(2)}, u32[]{:S(2)}) async-start(f32[128,1,384]{2,1,0:T(1,128)} %bitcast.6), calls=%async_computation.1 | async-start | bytes 393216 | tf_op jit(solution)/shard_map/all_to_all | solution.py:643
  56.6 1.7 %collective-permute-start.2 = (f32[640,128]{1,0:T(8,128)S(1)}, f32[640,128]{1,0:T(8,128)S(1)}, u32[]{:S(2)}, u32[]{:S(2)}) collective-permute-start(f32[640,128]{1,0:T(8,128)S(1)} %get-tuple-element.64), channel_id=1, source_target_pairs={{0,1},{1,0},{2,3},{3,2},{4,5},{5,4},{6,7},{7,6},{8,9},{9,8},{10,11... | collective-permute-start | bytes 983048 | tf_op jit(solution)/shard_map/ppermute | solution.py:638
  64.6 27.0 %copy-start.5 = (s32[8,128]{1,0:T(8,128)S(1)}, s32[8,128]{1,0:T(8,128)}, u32[]{:S(2)}) copy-start(s32[8,128]{1,0:T(8,128)} %get-tuple-element.39.idx_ref) | copy-start | bytes 12292
  88.8 4.2 %collective-permute-start.3 = (f32[896,128]{1,0:T(8,128)S(1)}, f32[896,128]{1,0:T(8,128)S(1)}, u32[]{:S(2)}, u32[]{:S(2)}) collective-permute-start(f32[896,128]{1,0:T(8,128)S(1)} %bitcast.13), channel_id=1, source_target_pairs={{0,1},{1,0},{2,3},{3,2},{4,5},{5,4},{6,7},{7,6},{8,9},{9,8},{10,11... | collective-permute-start | bytes 1376264 | tf_op jit(solution)/shard_map/ppermute | solution.py:638

commit v7 on v6

--- a/solution.py
+++ b/solution.py
@@ -173,20 +173,29 @@
 
     def fill_mask(self, mask_ref):
         cols = column_of(self.key)
+        one, zero = jnp.ones((8, 16, L), BF16), jnp.zeros((8, 16, L), BF16)
+
+        def short(rows, shape):
+            return jnp.broadcast_to(rows, shape).astype(jnp.int32).astype(jnp.int16)
+
+        base = jnp.minimum(self.base, 30000.0)
+        ends = [short(self.key[b : b + 1, :], (16, L))[None] for b in range(8)]
+        starts = [short(base[b : b + 1, :], (16, L))[None] for b in range(8)]
         for a in range(8):
-            front = jnp.broadcast_to(cols[:, a : a + 1], (L, L))
+            front = short(cols[:, a : a + 1], (L, L)).reshape(8, 16, L)
             for b in range(8):
-                hit = (front < self.key[b : b + 1, :]) & (front >= self.base[b : b + 1, :])
-                mask_ref[a * L : a * L + L, b * L : b * L + L] = ones_where(hit).astype(BF16)
+                hit = (front < ends[b]) & (front >= starts[b])
+                got = jnp.where(hit, one, zero).reshape(L, L)
+                mask_ref[a * L : a * L + L, b * L : b * L + L] = got
 
     def spread(self, b, weights, high_ref, low_ref):
         cols = slice(b * L, b * L + L)
-        high, low = split2(weights)
+        high, low = (x.reshape(8, 16, L) for x in split2(weights))
         for t in range(8):
             here = ones_where(self.tile[b : b + 1, :] == float(t))
-            here = jnp.broadcast_to(here, (L, L)).astype(BF16)
-            high_ref[t * L : t * L + L, cols] = high * here
-            low_ref[t * L : t * L + L, cols] = low * here
+            here = jnp.broadcast_to(here, (16, L)).astype(BF16)[None]
+            high_ref[t * L : t * L + L, cols] = (high * here).reshape(L, L)
+            low_ref[t * L : t * L + L, cols] = (low * here).reshape(L, L)
 
 
 def fill_features(own_ref, peer_ref, feat_ref):
@@ -267,8 +276,8 @@
     width = whigh_ref.shape[1]
     squares = jnp.zeros((1, width), F32)
     bias_sum = jnp.zeros((1, width), F32)
-    step = 2 * L
-    for r in range(4):
+    step = 8 * L
+    for r in range(1):
         rows = slice(r * step, r * step + step)
         both = nn(wm_hi[rows, :], feat_ref[...])
         rendered = both[:, :L] + both[:, L:] + nn(wm_lo[rows, :], feat_ref[:, 0:L])
@@ -347,8 +356,9 @@
 
     dw_ref[...] = jnp.zeros(dw_ref.shape, F32)
     step = 2 * L
-    for r in range(4):
-        rows = slice(r * step, r * step + step)
+    span = 4
+    for r in range(8 // span):
+        rows = slice(r * span * L, (r + 1) * span * L)
         grad = grad_ref[rows, :]
         high, low = split2(grad)
         pair = jnp.concatenate([high, low], axis=1)
@@ -361,9 +371,11 @@
             for q in range(2):
                 cols = slice((b + q) * L, (b + q) * L + L)
                 tile = pool.tile[b + q : b + q + 1, :]
-                got = part[:, q * L : q * L + L]
-                kept = jnp.where(tile == float(2 * r), got[:L], dw_ref[:, cols])
-                dw_ref[:, cols] = jnp.where(tile == float(2 * r + 1), got[L:], kept)
+                kept = dw_ref[:, cols]
+                for t in range(span):
+                    got = part[t * L : t * L + L, q * L : q * L + L]
+                    kept = jnp.where(tile == float(r * span + t), got, kept)
+                dw_ref[:, cols] = kept
 
     for b in range(8):
         cols = slice(b * L, b * L + L)

time: 95.3 us -> 94.7 us (level)
  transfers between devices with their start and end apart: 6 -> 6, of which waited for: 5 -> 5; matrix products, arithmetic and copies ran while one was open for 0% -> 0% of each run, Pallas kernels for 9% -> 8%
where the time goes in v7:
time: 94.7 us; the launch traced here: 94.4 us
  starting transfers between devices  29.2 us (31%)
  blocking collectives  23.8 us (25%)
  waiting for transfers between devices  22.8 us (24%)
  Pallas kernels  17.1 us (18%)
    all_to_all x1, blocking collectives, exchange(): lax.all_to_all(sent, 'gs', split_axis=0, concat_axis=0, tiled=True)  23.8 us
    all_to_all x2, starting transfers between devices, exchange(): lax.all_to_all(sent, 'gs', split_axis=0, concat_axis=0, tiled=True)  22.7 us
    all_to_all x2, waiting for transfers between devices, exchange(): lax.all_to_all(sent, 'gs', split_axis=0, concat_axis=0, tiled=True)  20.6 us
    ppermute x4, starting transfers between devices, swap(): return lax.ppermute(value, 'px', SWAP)  6.48 us
    pallas_call x1, Pallas kernels, back(): call(functools.partial(back_kernel, float(length)), [f32(FWD * L, L), f32...  4.41 us
    pallas_call x1, Pallas kernels, front(): call(functools.partial(front_kernel, float(length)), [f32(GAT * L, L), f3...  4.05 us
    pallas_call x1, Pallas kernels, pack(): call(pack_kernel, shapes, [SMEM, HBM, HBM, HBM], scratch, flops=2 * 10 **...  2.95 us
    ppermute x4, waiting for transfers between devices, swap(): return lax.ppermute(value, 'px', SWAP)  2.22 us
  transfers between devices with their start and end apart: 6, of which 5 were waited for; matrix products, arithmetic and copies ran while one was open for 0% of the time, Pallas kernels for 8%

profile of v7, /device:TPU:1, one launch (start us, length us, event | category | flops | bytes accessed | tf_op | source)
XLA Modules:
  0.0 94.4 jit_solution(5790923772629521453)
XLA Ops:
  0.7 2.9 %shard_map.119 = (f32[640,128]{1,0:T(8,128)}, s32[8,128]{1,0:T(8,128)}) custom-call(s32[1]{0:T(128)} %bitcast.par_ref, s32[8,128]{1,0:T(8,128)} %bitcast.25, f32[2048,128]{1,0:T(8,128)} %feat_hbm.1, f32[6,2048]{1,0:T(8,128)} %prm_hbm.1), custom_call_target="tpu_custom_call" | custom-call | flops 2000000000 | bytes 6666666 | tf_op jit(solution)/shard_map/pallas_call | solution.py:556
  3.6 16.3 %all-to-all-start = ((f32[128,1,640]{2,1,0:T(1,128)}), f32[128,1,640]{2,1,0:T(1,128)S(1)}, u32[]{:S(2)}, u32[]{:S(2)}) async-start(f32[128,1,640]{2,1,0:T(1,128)} %bitcast.24), calls=%async_computation | async-start | bytes 655360 | tf_op jit(solution)/shard_map/all_to_all | solution.py:655
  20.0 0.5 shard_map.120
  20.5 0.0 copy-start
  20.5 0.0 copy-start.3
  20.5 14.1 %all-to-all-done = f32[128,1,640]{2,1,0:T(1,128)S(1)} async-done(((f32[128,1,640]{2,1,0:T(1,128)}), f32[128,1,640]{2,1,0:T(1,128)S(1)}, u32[]{:S(2)}, u32[]{:S(2)}) %all-to-all-start) | async-done | bytes 327712 | tf_op jit(solution)/shard_map/all_to_all | solution.py:655
  34.7 2.8 %collective-permute-start = (f32[640,128]{1,0:T(8,128)S(1)}, f32[640,128]{1,0:T(8,128)S(1)}, u32[]{:S(2)}, u32[]{:S(2)}) collective-permute-start(f32[640,128]{1,0:T(8,128)S(1)} %bitcast.17), channel_id=1, source_target_pairs={{0,1},{1,0},{2,3},{3,2},{4,5},{5,4},{6,7},{7,6},{8,9},{9,8},{10,11... | collective-permute-start | bytes 983048 | tf_op jit(solution)/shard_map/ppermute | solution.py:650
  37.5 1.3 %shard_map.121 = (bf16[1024,1024]{1,0:T(8,128)(2,1)S(1)}, f32[128,512]{1,0:T(8,128)S(1)}, bf16[256,512]{1,0:T(8,128)(2,1)S(1)}) custom-call(s32[1]{0:T(128)} %bitcast.par_ref, s32[8]{0:T(128)S(1)} %copy-done.4, f32[640,128]{1,0:T(8,128)S(1)} %bitcast.18, f32[8,128]{1,0:T(8,128)S(1)} %get-tuple-element.48.keyrow_ref), custom_call_target="tpu_custom_call" | custom-call | flops 1000000000 | bytes 3333333 | tf_op jit(solution)/shard_map/pallas_call | solution.py:566
  38.8 4.1 %shard_map.122 = (f32[384,128]{1,0:T(8,128)S(1)}, f32[384,128]{1,0:T(8,128)S(1)}, f32[128,1024]{1,0:T(8,128)S(1)}, bf16[1024,512]{1,0:T(8,128)(2,1)S(1)}, bf16[1024,512]{1,0:T(8,128)(2,1)S(1)}) custom-call(s32[1]{0:T(128)} %bitcast.par_ref, s32[8]{0:T(128)S(1)} %copy-done.4, f32[640,128]{1,0:T(8,128)S(1)} %bitcast.19, ...), custom_call_target="tpu_custom_call" | custom-call | flops 10000000000 | bytes 33333332 | tf_op jit(solution)/shard_map/pallas_call | solution.py:587
  42.9 0.3 collective-permute-start.1
  43.2 0.7 shard_map.123.grad_ref
  43.9 0.5 collective-permute-done.1
  44.4 0.7 add.3
  45.1 6.4 %all-to-all-start.1 = ((f32[128,1,384]{2,1,0:T(1,128)}), f32[128,1,384]{2,1,0:T(1,128)S(1)}, u32[]{:S(2)}, u32[]{:S(2)}) async-start(f32[128,1,384]{2,1,0:T(1,128)} %bitcast.6), calls=%async_computation.1 | async-start | bytes 393216 | tf_op jit(solution)/shard_map/all_to_all | solution.py:655
  51.5 4.4 %shard_map.124 = (f32[640,128]{1,0:T(8,128)S(1)}, f32[640,128]{1,0:T(8,128)S(1)}) custom-call(s32[1]{0:T(128)} %bitcast.par_ref, s32[8]{0:T(128)S(1)} %copy-done.4, f32[640,128]{1,0:T(8,128)S(1)} %bitcast.20, f32[640,128]{1,0:T(8,128)S(1)} %collective-permute-done.peer_ref, f32[8,128]{1,0:T(8,128)S(1)} %get-tuple-element.48.keyrow_ref, ...), custom_call_target="tpu_custom_call" | custom-call | flops 8000000000 | bytes 26666666 | tf_op jit(solution)/shard_map/pallas_call | solution.py:617
  55.9 0.3 collective-permute-start.2
  56.2 1.4 %collective-permute-done.2.give_ref = f32[640,128]{1,0:T(8,128)S(1)} collective-permute-done((f32[640,128]{1,0:T(8,128)S(1)}, f32[640,128]{1,0:T(8,128)S(1)}, u32[]{:S(2)}, u32[]{:S(2)}) %collective-permute-start.2) | collective-permute-done | bytes 327712 | tf_op jit(solution)/shard_map/ppermute | solution.py:650
  57.6 6.4 %all-to-all-done.1 = f32[128,1,384]{2,1,0:T(1,128)S(1)} async-done(((f32[128,1,384]{2,1,0:T(1,128)}), f32[128,1,384]{2,1,0:T(1,128)S(1)}, u32[]{:S(2)}, u32[]{:S(2)}) %all-to-all-start.1) | async-done | bytes 196640 | tf_op jit(solution)/shard_map/all_to_all | solution.py:655
  64.0 0.1 shard_map.125
  64.2 23.8 %all_to_all.15 = f32[128,1,896]{2,1,0:T(1,128)S(1)} all-to-all(f32[128,1,896]{2,1,0:T(1,128)S(1)} %bitcast.16), channel_id=1, replica_groups=mesh['gs'=128,'px'=2] {'gs'}, dimensions={0} | all-to-all | bytes 917504 | tf_op jit(solution)/shard_map/all_to_all | solution.py:655
  88.0 3.0 %collective-permute-start.3 = (f32[896,128]{1,0:T(8,128)S(1)}, f32[896,128]{1,0:T(8,128)S(1)}, u32[]{:S(2)}, u32[]{:S(2)}) collective-permute-start(f32[896,128]{1,0:T(8,128)S(1)} %bitcast.13), channel_id=1, source_target_pairs={{0,1},{1,0},{2,3},{3,2},{4,5},{5,4},{6,7},{7,6},{8,9},{9,8},{10,11... | collective-permute-start | bytes 1376264 | tf_op jit(solution)/shard_map/ppermute | solution.py:650
  91.0 1.0 %shard_map.126 = (f32[2048,128]{1,0:T(8,128)S(1)}, f32[128,128]{1,0:T(8,128)S(1)}, bf16[2048,512]{1,0:T(8,128)(2,1)S(1)}) custom-call(s32[1]{0:T(128)} %bitcast.par_ref, s32[8,128]{1,0:T(8,128)S(1)} %copy-done.5, f32[896,128]{1,0:T(8,128)S(1)} %bitcast.14), custom_call_target="tpu_custom_call" | custom-call | flops 1000000000 | bytes 3333333 | tf_op jit(solution)/shard_map/pallas_call | solution.py:631
  92.0 0.4 collective-permute-done.3.peer_ref
  92.4 2.0 %shard_map.127 = (f32[2048,128]{1,0:T(8,128)}, f32[6,2048]{1,0:T(8,128)}, f32[128,512]{1,0:T(8,128)}, f32[1,512]{1,0:T(1,128)}, f32[1,128]{1,0:T(1,128)}) custom-call(s32[1]{0:T(128)} %bitcast.par_ref, s32[8,128]{1,0:T(8,128)S(1)} %copy-done.5, f32[896,128]{1,0:T(8,128)S(1)} %bitcast.15, f32[896,128]{1,0:T(8,128)S(1)} %collective-permute-done.3.peer_ref, ...), custom_call_target="tpu_custom_call" | custom-call | flops 2000000000 | bytes 6666666 | tf_op jit(solution)/shard_map/pallas_call | solution.py:641
  (11 shorter events, 0.0 us)
Async XLA Ops:
  0.6 19.3 %copy-start.1 = (f32[128,512]{1,0:T(8,128)S(1)}, f32[128,512]{1,0:T(8,128)}, u32[]{:S(2)}) copy-start(f32[128,512]{1,0:T(8,128)} %weight_ref) | copy-start | bytes 786436
  0.6 19.3 %copy-start.2 = (s32[8,512]{1,0:T(8,128)S(1)}, s32[8,512]{1,0:T(8,128)}, u32[]{:S(2)}) copy-start(s32[8,512]{1,0:T(8,128)} %lists_ref) | copy-start | bytes 49156
  3.6 31.1 %all-to-all-start = ((f32[128,1,640]{2,1,0:T(1,128)}), f32[128,1,640]{2,1,0:T(1,128)S(1)}, u32[]{:S(2)}, u32[]{:S(2)}) async-start(f32[128,1,640]{2,1,0:T(1,128)} %bitcast.24), calls=%async_computation | async-start | bytes 655360 | tf_op jit(solution)/shard_map/all_to_all | solution.py:655
  20.0 17.5 %copy-start.4 = (s32[8]{0:T(128)S(1)}, s32[8]{0:T(128)}, u32[]{:S(2)}) copy-start(s32[8]{0:T(128)} %ids_ref.5) | copy-start | bytes 100
  20.5 18.3 %copy-start = (f32[8,128,512]{2,1,0:T(8,128)S(1)}, f32[8,128,512]{2,1,0:T(8,128)}, u32[]{:S(2)}) copy-start(f32[8,128,512]{2,1,0:T(8,128)} %param.13) | copy-start | bytes 6291460
  20.5 18.3 %copy-start.3 = (f32[512]{0:T(512)S(1)}, f32[512]{0:T(512)}, u32[]{:S(2)}) copy-start(f32[512]{0:T(512)} %param.15) | copy-start | bytes 6148
  34.7 4.1 %collective-permute-start = (f32[640,128]{1,0:T(8,128)S(1)}, f32[640,128]{1,0:T(8,128)S(1)}, u32[]{:S(2)}, u32[]{:S(2)}) collective-permute-start(f32[640,128]{1,0:T(8,128)S(1)} %bitcast.17), channel_id=1, source_target_pairs={{0,1},{1,0},{2,3},{3,2},{4,5},{5,4},{6,7},{7,6},{8,9},{9,8},{10,11... | collective-permute-start | bytes 983048 | tf_op jit(solution)/shard_map/ppermute | solution.py:650
  42.9 1.5 %collective-permute-start.1 = (f32[384,128]{1,0:T(8,128)S(1)}, f32[384,128]{1,0:T(8,128)S(1)}, u32[]{:S(2)}, u32[]{:S(2)}) collective-permute-start(f32[384,128]{1,0:T(8,128)S(1)} %get-tuple-element.56), channel_id=1, source_target_pairs={{0,1},{1,0},{2,3},{3,2},{4,5},{5,4},{6,7},{7,6},{8,9},{9,8},{10,11... | collective-permute-start | bytes 589832 | tf_op jit(solution)/shard_map/ppermute | solution.py:650
  45.1 18.9 %all-to-all-start.1 = ((f32[128,1,384]{2,1,0:T(1,128)}), f32[128,1,384]{2,1,0:T(1,128)S(1)}, u32[]{:S(2)}, u32[]{:S(2)}) async-start(f32[128,1,384]{2,1,0:T(1,128)} %bitcast.6), calls=%async_computation.1 | async-start | bytes 393216 | tf_op jit(solution)/shard_map/all_to_all | solution.py:655
  55.9 1.7 %collective-permute-start.2 = (f32[640,128]{1,0:T(8,128)S(1)}, f32[640,128]{1,0:T(8,128)S(1)}, u32[]{:S(2)}, u32[]{:S(2)}) collective-permute-start(f32[640,128]{1,0:T(8,128)S(1)} %get-tuple-element.64), channel_id=1, source_target_pairs={{0,1},{1,0},{2,3},{3,2},{4,5},{5,4},{6,7},{7,6},{8,9},{9,8},{10,11... | collective-permute-start | bytes 983048 | tf_op jit(solution)/shard_map/ppermute | solution.py:650
  64.0 26.9 %copy-start.5 = (s32[8,128]{1,0:T(8,128)S(1)}, s32[8,128]{1,0:T(8,128)}, u32[]{:S(2)}) copy-start(s32[8,128]{1,0:T(8,128)} %get-tuple-element.39.idx_ref) | copy-start | bytes 12292
  88.0 4.4 %collective-permute-start.3 = (f32[896,128]{1,0:T(8,128)S(1)}, f32[896,128]{1,0:T(8,128)S(1)}, u32[]{:S(2)}, u32[]{:S(2)}) collective-permute-start(f32[896,128]{1,0:T(8,128)S(1)} %bitcast.13), channel_id=1, source_target_pairs={{0,1},{1,0},{2,3},{3,2},{4,5},{5,4},{6,7},{7,6},{8,9},{9,8},{10,11... | collective-permute-start | bytes 1376264 | tf_op jit(solution)/shard_map/ppermute | solution.py:650

commit v8 on v7

--- a/solution.py
+++ b/solution.py
@@ -133,6 +133,7 @@
 
 
 class Pool:
+
     def __init__(self, length, par_ref, ids_ref, keyrow_ref, prm_ref, sides):
         self.length, self.prm_ref = length, prm_ref
         stripe = par_ref[0]
@@ -149,7 +150,6 @@
                 here, ((ident >> 7) * 16 + stripe * 8).astype(F32) + 0.5, self.oy
             )
         self.base = jnp.where(live, self.tile * length, 1.0e9)
-        self.live = ones_where(live)
         self.kx = lax.broadcasted_iota(jnp.int32, (16, L), 0).astype(F32)
         self.ky = lax.broadcasted_iota(jnp.int32, (8, L), 0).astype(F32)
         for side, ref in sides:
@@ -166,9 +166,10 @@
         ax = prm[2:3] * dx * dx
         cy = prm[4:5] * dy * dy
         bx = prm[3:4] * dx
+        live = self.key[b : b + 1, :] >= 0.0
         for j in range(8):
             power = -0.5 * (ax + cy[j : j + 1]) - bx * dy[j : j + 1]
-            ex = self.live[b : b + 1, :] * jnp.exp(power)
+            ex = jnp.where(live, jnp.exp(power), 0.0)
             yield slice(j * 16, j * 16 + 16), ex, prm[5:6] * ex
 
     def fill_mask(self, mask_ref):

time: 94.7 us -> 94.6 us (level)
  no operation moved by 1% of the time
where the time goes in v8:
time: 94.6 us; the launch traced here: 94.3 us
  starting transfers between devices  29.3 us (31%)
  blocking collectives  23.7 us (25%)
  waiting for transfers between devices  22.8 us (24%)
  Pallas kernels  17 us (18%)
    all_to_all x1, blocking collectives, exchange(): lax.all_to_all(sent, 'gs', split_axis=0, concat_axis=0, tiled=True)  23.7 us
    all_to_all x2, starting transfers between devices, exchange(): lax.all_to_all(sent, 'gs', split_axis=0, concat_axis=0, tiled=True)  22.7 us
    all_to_all x2, waiting for transfers between devices, exchange(): lax.all_to_all(sent, 'gs', split_axis=0, concat_axis=0, tiled=True)  20.6 us
    ppermute x4, starting transfers between devices, swap(): return lax.ppermute(value, 'px', SWAP)  6.59 us
    pallas_call x1, Pallas kernels, back(): call(functools.partial(back_kernel, float(length)), [f32(FWD * L, L), f32...  4.39 us
    pallas_call x1, Pallas kernels, front(): call(functools.partial(front_kernel, float(length)), [f32(GAT * L, L), f3...  4.05 us
    pallas_call x1, Pallas kernels, pack(): call(pack_kernel, shapes, [SMEM, HBM, HBM, HBM], scratch, flops=2 * 10 **...  2.95 us
    ppermute x4, waiting for transfers between devices, swap(): return lax.ppermute(value, 'px', SWAP)  2.23 us
  transfers between devices with their start and end apart: 6, of which 5 were waited for; matrix products, arithmetic and copies ran while one was open for 0% of the time, Pallas kernels for 8%

profile of v8, /device:TPU:1, one launch (start us, length us, event | category | flops | bytes accessed | tf_op | source)
XLA Modules:
  0.0 94.3 jit_solution(3756343747069062568)
XLA Ops:
  0.7 2.9 %shard_map.119 = (f32[640,128]{1,0:T(8,128)}, s32[8,128]{1,0:T(8,128)}) custom-call(s32[1]{0:T(128)} %bitcast.par_ref, s32[8,128]{1,0:T(8,128)} %bitcast.25, f32[2048,128]{1,0:T(8,128)} %feat_hbm.1, f32[6,2048]{1,0:T(8,128)} %prm_hbm.1), custom_call_target="tpu_custom_call" | custom-call | flops 2000000000 | bytes 6666666 | tf_op jit(solution)/shard_map/pallas_call | solution.py:557
  3.6 16.3 %all-to-all-start = ((f32[128,1,640]{2,1,0:T(1,128)}), f32[128,1,640]{2,1,0:T(1,128)S(1)}, u32[]{:S(2)}, u32[]{:S(2)}) async-start(f32[128,1,640]{2,1,0:T(1,128)} %bitcast.24), calls=%async_computation | async-start | bytes 655360 | tf_op jit(solution)/shard_map/all_to_all | solution.py:656
  20.0 0.0 copy-start.4
  20.0 0.5 shard_map.120
  20.5 0.0 copy-start
  20.5 14.1 %all-to-all-done = f32[128,1,640]{2,1,0:T(1,128)S(1)} async-done(((f32[128,1,640]{2,1,0:T(1,128)}), f32[128,1,640]{2,1,0:T(1,128)S(1)}, u32[]{:S(2)}, u32[]{:S(2)}) %all-to-all-start) | async-done | bytes 327712 | tf_op jit(solution)/shard_map/all_to_all | solution.py:656
  34.7 2.8 %collective-permute-start = (f32[640,128]{1,0:T(8,128)S(1)}, f32[640,128]{1,0:T(8,128)S(1)}, u32[]{:S(2)}, u32[]{:S(2)}) collective-permute-start(f32[640,128]{1,0:T(8,128)S(1)} %bitcast.17), channel_id=1, source_target_pairs={{0,1},{1,0},{2,3},{3,2},{4,5},{5,4},{6,7},{7,6},{8,9},{9,8},{10,11... | collective-permute-start | bytes 983048 | tf_op jit(solution)/shard_map/ppermute | solution.py:651
  37.5 1.3 %shard_map.121 = (bf16[1024,1024]{1,0:T(8,128)(2,1)S(1)}, f32[128,512]{1,0:T(8,128)S(1)}, bf16[256,512]{1,0:T(8,128)(2,1)S(1)}) custom-call(s32[1]{0:T(128)} %bitcast.par_ref, s32[8]{0:T(128)S(1)} %copy-done.4, f32[640,128]{1,0:T(8,128)S(1)} %bitcast.18, f32[8,128]{1,0:T(8,128)S(1)} %get-tuple-element.48.keyrow_ref), custom_call_target="tpu_custom_call" | custom-call | flops 1000000000 | bytes 3333333 | tf_op jit(solution)/shard_map/pallas_call | solution.py:567
  38.8 4.0 %shard_map.122 = (f32[384,128]{1,0:T(8,128)S(1)}, f32[384,128]{1,0:T(8,128)S(1)}, f32[128,1024]{1,0:T(8,128)S(1)}, bf16[1024,512]{1,0:T(8,128)(2,1)S(1)}, bf16[1024,512]{1,0:T(8,128)(2,1)S(1)}) custom-call(s32[1]{0:T(128)} %bitcast.par_ref, s32[8]{0:T(128)S(1)} %copy-done.4, f32[640,128]{1,0:T(8,128)S(1)} %bitcast.19, ...), custom_call_target="tpu_custom_call" | custom-call | flops 10000000000 | bytes 33333332 | tf_op jit(solution)/shard_map/pallas_call | solution.py:588
  42.9 0.4 collective-permute-start.1
  43.2 0.7 shard_map.123.grad_ref
  43.9 0.5 collective-permute-done.1
  44.4 0.7 add.3
  45.1 6.4 %all-to-all-start.1 = ((f32[128,1,384]{2,1,0:T(1,128)}), f32[128,1,384]{2,1,0:T(1,128)S(1)}, u32[]{:S(2)}, u32[]{:S(2)}) async-start(f32[128,1,384]{2,1,0:T(1,128)} %bitcast.6), calls=%async_computation.1 | async-start | bytes 393216 | tf_op jit(solution)/shard_map/all_to_all | solution.py:656
  51.5 4.4 %shard_map.124 = (f32[640,128]{1,0:T(8,128)S(1)}, f32[640,128]{1,0:T(8,128)S(1)}) custom-call(s32[1]{0:T(128)} %bitcast.par_ref, s32[8]{0:T(128)S(1)} %copy-done.4, f32[640,128]{1,0:T(8,128)S(1)} %bitcast.20, f32[640,128]{1,0:T(8,128)S(1)} %collective-permute-done.peer_ref, f32[8,128]{1,0:T(8,128)S(1)} %get-tuple-element.48.keyrow_ref, ...), custom_call_target="tpu_custom_call" | custom-call | flops 8000000000 | bytes 26666666 | tf_op jit(solution)/shard_map/pallas_call | solution.py:618
  55.9 0.3 collective-permute-start.2
  56.2 1.4 %collective-permute-done.2.give_ref = f32[640,128]{1,0:T(8,128)S(1)} collective-permute-done((f32[640,128]{1,0:T(8,128)S(1)}, f32[640,128]{1,0:T(8,128)S(1)}, u32[]{:S(2)}, u32[]{:S(2)}) %collective-permute-start.2) | collective-permute-done | bytes 327712 | tf_op jit(solution)/shard_map/ppermute | solution.py:651
  57.6 6.4 %all-to-all-done.1 = f32[128,1,384]{2,1,0:T(1,128)S(1)} async-done(((f32[128,1,384]{2,1,0:T(1,128)}), f32[128,1,384]{2,1,0:T(1,128)S(1)}, u32[]{:S(2)}, u32[]{:S(2)}) %all-to-all-start.1) | async-done | bytes 196640 | tf_op jit(solution)/shard_map/all_to_all | solution.py:656
  64.0 0.1 shard_map.125
  64.2 23.7 %all_to_all.15 = f32[128,1,896]{2,1,0:T(1,128)S(1)} all-to-all(f32[128,1,896]{2,1,0:T(1,128)S(1)} %bitcast.16), channel_id=1, replica_groups=mesh['gs'=128,'px'=2] {'gs'}, dimensions={0} | all-to-all | bytes 917504 | tf_op jit(solution)/shard_map/all_to_all | solution.py:656
  87.8 3.1 %collective-permute-start.3 = (f32[896,128]{1,0:T(8,128)S(1)}, f32[896,128]{1,0:T(8,128)S(1)}, u32[]{:S(2)}, u32[]{:S(2)}) collective-permute-start(f32[896,128]{1,0:T(8,128)S(1)} %bitcast.13), channel_id=1, source_target_pairs={{0,1},{1,0},{2,3},{3,2},{4,5},{5,4},{6,7},{7,6},{8,9},{9,8},{10,11... | collective-permute-start | bytes 1376264 | tf_op jit(solution)/shard_map/ppermute | solution.py:651
  90.9 1.0 %shard_map.126 = (f32[2048,128]{1,0:T(8,128)S(1)}, f32[128,128]{1,0:T(8,128)S(1)}, bf16[2048,512]{1,0:T(8,128)(2,1)S(1)}) custom-call(s32[1]{0:T(128)} %bitcast.par_ref, s32[8,128]{1,0:T(8,128)S(1)} %copy-done.5, f32[896,128]{1,0:T(8,128)S(1)} %bitcast.14), custom_call_target="tpu_custom_call" | custom-call | flops 1000000000 | bytes 3333333 | tf_op jit(solution)/shard_map/pallas_call | solution.py:632
  92.0 0.4 collective-permute-done.3.peer_ref
  92.4 2.0 %shard_map.127 = (f32[2048,128]{1,0:T(8,128)}, f32[6,2048]{1,0:T(8,128)}, f32[128,512]{1,0:T(8,128)}, f32[1,512]{1,0:T(1,128)}, f32[1,128]{1,0:T(1,128)}) custom-call(s32[1]{0:T(128)} %bitcast.par_ref, s32[8,128]{1,0:T(8,128)S(1)} %copy-done.5, f32[896,128]{1,0:T(8,128)S(1)} %bitcast.15, f32[896,128]{1,0:T(8,128)S(1)} %collective-permute-done.3.peer_ref, ...), custom_call_target="tpu_custom_call" | custom-call | flops 2000000000 | bytes 6666666 | tf_op jit(solution)/shard_map/pallas_call | solution.py:642
  (11 shorter events, 0.0 us)
Async XLA Ops:
  0.6 19.3 %copy-start.1 = (f32[128,512]{1,0:T(8,128)S(1)}, f32[128,512]{1,0:T(8,128)}, u32[]{:S(2)}) copy-start(f32[128,512]{1,0:T(8,128)} %weight_ref) | copy-start | bytes 786436
  0.6 19.3 %copy-start.2 = (s32[8,512]{1,0:T(8,128)S(1)}, s32[8,512]{1,0:T(8,128)}, u32[]{:S(2)}) copy-start(s32[8,512]{1,0:T(8,128)} %lists_ref) | copy-start | bytes 49156
  3.6 31.1 %all-to-all-start = ((f32[128,1,640]{2,1,0:T(1,128)}), f32[128,1,640]{2,1,0:T(1,128)S(1)}, u32[]{:S(2)}, u32[]{:S(2)}) async-start(f32[128,1,640]{2,1,0:T(1,128)} %bitcast.24), calls=%async_computation | async-start | bytes 655360 | tf_op jit(solution)/shard_map/all_to_all | solution.py:656
  20.0 17.5 %copy-start.4 = (s32[8]{0:T(128)S(1)}, s32[8]{0:T(128)}, u32[]{:S(2)}) copy-start(s32[8]{0:T(128)} %ids_ref.5) | copy-start | bytes 100
  20.5 18.3 %copy-start = (f32[8,128,512]{2,1,0:T(8,128)S(1)}, f32[8,128,512]{2,1,0:T(8,128)}, u32[]{:S(2)}) copy-start(f32[8,128,512]{2,1,0:T(8,128)} %param.13) | copy-start | bytes 6291460
  20.5 18.3 %copy-start.3 = (f32[512]{0:T(512)S(1)}, f32[512]{0:T(512)}, u32[]{:S(2)}) copy-start(f32[512]{0:T(512)} %param.15) | copy-start | bytes 6148
  34.7 4.1 %collective-permute-start = (f32[640,128]{1,0:T(8,128)S(1)}, f32[640,128]{1,0:T(8,128)S(1)}, u32[]{:S(2)}, u32[]{:S(2)}) collective-permute-start(f32[640,128]{1,0:T(8,128)S(1)} %bitcast.17), channel_id=1, source_target_pairs={{0,1},{1,0},{2,3},{3,2},{4,5},{5,4},{6,7},{7,6},{8,9},{9,8},{10,11... | collective-permute-start | bytes 983048 | tf_op jit(solution)/shard_map/ppermute | solution.py:651
  42.9 1.5 %collective-permute-start.1 = (f32[384,128]{1,0:T(8,128)S(1)}, f32[384,128]{1,0:T(8,128)S(1)}, u32[]{:S(2)}, u32[]{:S(2)}) collective-permute-start(f32[384,128]{1,0:T(8,128)S(1)} %get-tuple-element.56), channel_id=1, source_target_pairs={{0,1},{1,0},{2,3},{3,2},{4,5},{5,4},{6,7},{7,6},{8,9},{9,8},{10,11... | collective-permute-start | bytes 589832 | tf_op jit(solution)/shard_map/ppermute | solution.py:651
  45.1 18.9 %all-to-all-start.1 = ((f32[128,1,384]{2,1,0:T(1,128)}), f32[128,1,384]{2,1,0:T(1,128)S(1)}, u32[]{:S(2)}, u32[]{:S(2)}) async-start(f32[128,1,384]{2,1,0:T(1,128)} %bitcast.6), calls=%async_computation.1 | async-start | bytes 393216 | tf_op jit(solution)/shard_map/all_to_all | solution.py:656
  55.9 1.7 %collective-permute-start.2 = (f32[640,128]{1,0:T(8,128)S(1)}, f32[640,128]{1,0:T(8,128)S(1)}, u32[]{:S(2)}, u32[]{:S(2)}) collective-permute-start(f32[640,128]{1,0:T(8,128)S(1)} %get-tuple-element.64), channel_id=1, source_target_pairs={{0,1},{1,0},{2,3},{3,2},{4,5},{5,4},{6,7},{7,6},{8,9},{9,8},{10,11... | collective-permute-start | bytes 983048 | tf_op jit(solution)/shard_map/ppermute | solution.py:651
  64.0 26.9 %copy-start.5 = (s32[8,128]{1,0:T(8,128)S(1)}, s32[8,128]{1,0:T(8,128)}, u32[]{:S(2)}) copy-start(s32[8,128]{1,0:T(8,128)} %get-tuple-element.39.idx_ref) | copy-start | bytes 12292
  87.8 4.6 %collective-permute-start.3 = (f32[896,128]{1,0:T(8,128)S(1)}, f32[896,128]{1,0:T(8,128)S(1)}, u32[]{:S(2)}, u32[]{:S(2)}) collective-permute-start(f32[896,128]{1,0:T(8,128)S(1)} %bitcast.13), channel_id=1, source_target_pairs={{0,1},{1,0},{2,3},{3,2},{4,5},{5,4},{6,7},{7,6},{8,9},{9,8},{10,11... | collective-permute-start | bytes 1376264 | tf_op jit(solution)/shard_map/ppermute | solution.py:651
